TPU v7x, 32 devices: a whole 2x2x4 slice. The times are simulated.
32 devices in a mesh: groups: 2 (over y), branch: 4 (over x, core), head: 4 (over z).
Axes of the slice: x: 2, y: 2, z: 4, core: 2. Of those that a mesh axis runs over, the one named last changes fastest.
Arguments:
- hidden_in: bfloat16 [256, 8192], P(('groups', 'branch')), parts along dimension 0, may hold values from -40 to 40
- input_gain: bfloat16 [8192], replicated, may hold values from 0.099609375 to 1.8984375
- w_query: bfloat16 [8192, 8192], P('branch', 'head'), may hold values from -0.0625 to 0.0625
- b_query: bfloat16 [8192], P('head'), may hold values from -6 to 6
- w_key: bfloat16 [8192, 1024], P('branch', 'head'), may hold values from -0.0625 to 0.0625
- b_key: bfloat16 [1024], P('head'), may hold values from -6 to 6
- w_value: bfloat16 [8192, 1024], P('branch', 'head'), may hold values from -0.0625 to 0.0625
- b_value: bfloat16 [1024], P('head'), may hold values from -6 to 6
- key_pages: bfloat16 [512, 128, 1024], P(('groups', 'branch'), None, 'head'), parts along dimension 0, may hold values from -1300 to 1300
- value_pages: bfloat16 [512, 128, 1024], P(('groups', 'branch'), None, 'head'), parts along dimension 0, may hold values from -12 to 12
- path_pages: int32 [32], P(('groups', 'branch')), parts along dimension 0, may hold values from 1 to 32, as said below
- page_table: int32 [32, 32], P(('groups', 'branch')), parts along dimension 0, may hold values from 0 to 63, as said below
- parent_index: int32 [256], P(('groups', 'branch')), parts along dimension 0, may hold values from 0 to 15, as said below
- w_out: bfloat16 [8192, 8192], P('head', 'branch'), may hold values from -0.0625 to 0.0625
- post_gain: bfloat16 [8192], replicated, may hold values from 0.099609375 to 1.8984375
- w_gate: bfloat16 [8192, 15360], P('branch', 'head'), may hold values from -0.0625 to 0.0625
- w_up: bfloat16 [8192, 15360], P('branch', 'head'), may hold values from -0.0625 to 0.0625
- w_down: bfloat16 [15360, 8192], P('head', 'branch'), may hold values from -0.046875 to 0.046875
Outputs:
- layer_out: bfloat16 [256, 8192], P(('groups', 'head'), 'branch'), parts along dimension 0
There are 2 independent parts, one for each index of `groups`. A program takes and returns all parts, laid end to end along the dimension named above; an argument that names none is the same for every part. Nothing has to cross between parts.
Inputs may be any that keep to these rules, and one draw needn't show every extreme that they name: `parent_index`: children lie 32 to a device along branch, in row order; the parent of a child lies on device parent // 4. Among the children of one device at most 8 have parents on one device, and some device has exactly 8 such children from every device. `path_pages`: paths are whole pages; the 4 paths of one device take 64 pages or fewer together, and on every device one path has exactly 32 pages. `page_table`: entries j < path_pages[p] of row p are distinct from all other such entries of the parents of the same device; entries past a path's length are to be ignored.
All inputs are finite; a program needn't handle non-finite values.
Results may differ from a plain program's by a relative error of at most 0.025.
Values may be sent and summed in bfloat16 or wider, within the bound.
No kernel may reach another device: no remote copies, remote signals or barrier semaphores. Data moves between devices by JAX's collectives and lax.ppermute only.
A program may use at most 192 MiB of HBM per device.

v0:
```python
import math

import jax
import jax.numpy as jnp
from jax import lax
from jax.sharding import PartitionSpec as P

D = 8192
HD = 128
PAGE = 128
MAXP = 32
POOL = 64
P_DEV = 4
CAP = 8


EPS = 1e-06
THETA = 1000000.0


def hadamard(order_size):
    index = jnp.arange(order_size, dtype=jnp.int32)
    common = index[:, None] & index[None, :]
    parity = jnp.zeros((order_size, order_size), jnp.int32)
    for bit_level in range(order_size.bit_length() - 1):
        parity = parity ^ common >> bit_level & 1
    return (1 - 2 * parity).astype(jnp.float32) / math.sqrt(order_size)


def rotary(vectors, position):
    width = vectors.shape[-1]
    half_width = width // 2
    freqs = THETA ** (-(jnp.arange(half_width, dtype=jnp.float32) * 2.0 / width))
    angle = position[..., None] * freqs
    first_half = vectors[..., :half_width]
    second_half = vectors[..., half_width:]
    return jnp.concatenate(
        [
            first_half * jnp.cos(angle) - second_half * jnp.sin(angle),
            second_half * jnp.cos(angle) + first_half * jnp.sin(angle),
        ],
        -1,
    )


def slot_codes(parents, dest_count):
    destination = parents // P_DEV
    onehot = (destination[:, None] == jnp.arange(dest_count, dtype=jnp.int32)[None, :]).astype(
        jnp.int32
    )
    before = jnp.cumsum(onehot, 0) - onehot
    return destination * CAP + jnp.sum(before * onehot, 1)


def attend_block(
    turned_block, query_block, key_new, value_new, keys_now, values_now, token_live, rotation
):
    slots, heads_here = (turned_block.shape[0], turned_block.shape[1])
    score_scale = 1.0 / math.sqrt(HD)
    scores = jnp.einsum(
        "rd,td->rt",
        turned_block.reshape(slots * heads_here, HD),
        keys_now,
        preferred_element_type=jnp.float32,
    )
    scores = scores.reshape(slots, heads_here, -1) * score_scale
    own_score = jnp.sum(query_block * key_new[:, None, :], -1) * score_scale
    live = token_live[:, None, :]
    top = jnp.maximum(jnp.max(jnp.where(live, scores, -jnp.inf), -1), own_score)
    weights = jnp.where(live, jnp.exp(scores - top[..., None]), 0.0)
    own_weight = jnp.exp(own_score - top)
    total = jnp.sum(weights, -1) + own_weight
    mixed = jnp.dot(
        weights.astype(jnp.bfloat16).reshape(slots * heads_here, -1),
        values_now,
        preferred_element_type=jnp.float32,
    )
    unturned = jnp.dot(mixed, rotation, precision=lax.Precision.HIGHEST).reshape(
        slots, heads_here, HD
    )
    result = (unturned + own_weight[..., None] * value_new[:, None, :]) / total[..., None]
    return result.astype(jnp.bfloat16)


def local(
    hidden_in,
    input_gain,
    w_query,
    b_query,
    w_key,
    b_key,
    w_value,
    b_value,
    key_pages,
    value_pages,
    path_pages,
    page_table,
    parent_index,
    w_out,
    post_gain,
    w_gate,
    w_up,
    w_down,
):
    branch_count = lax.axis_size("branch")
    head_count = lax.axis_size("head")
    branch_pos = lax.axis_index("branch")
    head_pos = lax.axis_index("head")
    local_rows = hidden_in.shape[0]
    all_rows = local_rows * branch_count
    model_cols = w_query.shape[0]
    query_cols = w_query.shape[1]
    kv_cols = w_key.shape[1]
    kv_local = kv_cols // HD
    heads_local = query_cols // HD
    group_size = heads_local // kv_local
    slot_total = branch_count * CAP
    hidden_f32 = hidden_in.astype(jnp.float32)
    normed = (
        hidden_f32
        * lax.rsqrt(jnp.mean(hidden_f32 * hidden_f32, -1, keepdims=True) + EPS)
        * input_gain.astype(jnp.float32)
    ).astype(jnp.bfloat16)
    ex_normed, ex_hidden = (
        lax.all_to_all(normed, "branch", split_axis=1, concat_axis=0, tiled=True),
        lax.all_to_all(hidden_in, "branch", split_axis=1, concat_axis=0, tiled=True),
    )
    picked = ex_normed
    projected = lax.psum_scatter(
        jnp.concatenate(
            [
                jnp.dot(picked, w_query, preferred_element_type=jnp.float32),
                jnp.dot(picked, w_key, preferred_element_type=jnp.float32),
                jnp.dot(picked, w_value, preferred_element_type=jnp.float32),
            ],
            1,
        ),
        "branch",
        scatter_dimension=0,
        tiled=True,
    )
    biases = jnp.concatenate([b_query, b_key, b_value]).astype(jnp.float32)
    packed = (projected + biases).astype(jnp.bfloat16)
    parents_all = lax.all_gather(parent_index, "branch", axis=0, tiled=True)
    slot_ids = jnp.arange(slot_total, dtype=jnp.int32)
    own_codes = slot_codes(parent_index, branch_count)
    placing = (own_codes[None, :] == slot_ids[:, None]).astype(jnp.bfloat16)
    outgoing = jnp.dot(placing, packed, preferred_element_type=jnp.float32).astype(jnp.bfloat16)
    outgoing = outgoing.reshape(branch_count, CAP, -1)
    incoming = lax.all_to_all(outgoing, "branch", split_axis=0, concat_axis=0, tiled=True).reshape(
        slot_total, -1
    )
    grouped = parents_all.reshape(branch_count, local_rows)
    codes_all = jax.vmap(lambda row_parents: slot_codes(row_parents, branch_count))(grouped)
    wanted = branch_pos * CAP + jnp.arange(CAP, dtype=jnp.int32)
    matches = (codes_all[:, None, :] == wanted[None, :, None]).astype(jnp.float32)
    local_onehot = (
        (grouped % P_DEV)[:, :, None] == jnp.arange(P_DEV, dtype=jnp.int32)[None, None, :]
    ).astype(jnp.float32)
    slot_parent = jnp.einsum("skj,sjp->skp", matches, local_onehot).reshape(slot_total, P_DEV)
    page_live = (page_table[:, :, None] == jnp.arange(POOL, dtype=jnp.int32)[None, None, :]) & (
        jnp.arange(MAXP, dtype=jnp.int32)[None, :, None] < path_pages[:, None, None]
    )
    page_owned = jnp.any(page_live, 1).astype(jnp.float32)
    slot_pages = jnp.dot(slot_parent, page_owned, precision=lax.Precision.HIGHEST) > 0.5
    token_live = jnp.repeat(slot_pages, PAGE, axis=1)
    position = (
        jnp.dot(slot_parent, path_pages.astype(jnp.float32), precision=lax.Precision.HIGHEST) * PAGE
    )
    queries = rotary(
        incoming[:, :query_cols].astype(jnp.float32).reshape(slot_total, heads_local, HD),
        position[:, None],
    )
    new_keys = rotary(
        incoming[:, query_cols : query_cols + kv_cols]
        .astype(jnp.float32)
        .reshape(slot_total, kv_local, HD),
        position[:, None],
    )
    new_values = (
        incoming[:, query_cols + kv_cols :].astype(jnp.float32).reshape(slot_total, kv_local, HD)
    )
    rotation = hadamard(HD)
    turned = jnp.einsum("shd,de->she", queries, rotation, precision=lax.Precision.HIGHEST).astype(
        jnp.bfloat16
    )
    cache_keys = key_pages.reshape(POOL * PAGE, kv_local, HD)
    cache_values = value_pages.reshape(POOL * PAGE, kv_local, HD)
    block_heads = 1
    for candidate in range(group_size, 0, -1):
        if group_size % candidate == 0 and candidate * slot_total <= 512:
            block_heads = candidate
            break
    outputs = []
    for kv_index in range(kv_local):
        keys_now = cache_keys[:, kv_index, :]
        values_now = cache_values[:, kv_index, :]
        for head_start in range(kv_index * group_size, (kv_index + 1) * group_size, block_heads):
            head_stop = head_start + block_heads
            outputs.append(
                attend_block(
                    turned[:, head_start:head_stop],
                    queries[:, head_start:head_stop],
                    new_keys[:, kv_index],
                    new_values[:, kv_index],
                    keys_now,
                    values_now,
                    token_live,
                    rotation,
                )
            )
    attention = jnp.concatenate(outputs, 1).reshape(branch_count, CAP, query_cols)
    returned = lax.all_to_all(attention, "branch", split_axis=0, concat_axis=0, tiled=True).reshape(
        slot_total, query_cols
    )
    attn_rows = jnp.einsum(
        "sc,sq->cq", placing, returned, preferred_element_type=jnp.float32
    ).astype(jnp.bfloat16)
    mixer = jnp.dot(
        lax.all_gather(attn_rows, "branch", axis=0, tiled=True),
        w_out,
        preferred_element_type=jnp.float32,
    )
    gain_cols = lax.dynamic_slice_in_dim(post_gain, branch_pos * model_cols, model_cols, 0).astype(
        jnp.float32
    )
    share_rows = all_rows // head_count
    residual = lax.dynamic_slice_in_dim(ex_hidden, head_pos * share_rows, share_rows, 0).astype(
        jnp.float32
    )
    residual = residual + lax.psum_scatter(
        mixer.astype(jnp.bfloat16), "head", scatter_dimension=0, tiled=True
    ).astype(jnp.float32)
    squares = lax.psum(jnp.sum(residual * residual, 1), "branch")
    normed_share = (residual * lax.rsqrt(squares[:, None] / D + EPS) * gain_cols).astype(
        jnp.bfloat16
    )
    normed_ffn = lax.all_gather(normed_share, "head", axis=0, tiled=True)
    picked = normed_ffn
    gate_up = lax.psum_scatter(
        jnp.concatenate(
            [
                jnp.dot(picked, w_gate, preferred_element_type=jnp.float32),
                jnp.dot(picked, w_up, preferred_element_type=jnp.float32),
            ],
            1,
        ).astype(jnp.bfloat16),
        "branch",
        scatter_dimension=0,
        tiled=True,
    ).astype(jnp.float32)
    ff_local = w_gate.shape[1]
    activated = (jax.nn.silu(gate_up[:, :ff_local]) * gate_up[:, ff_local:]).astype(jnp.bfloat16)
    lowered = jnp.dot(
        lax.all_gather(activated, "branch", axis=0, tiled=True),
        w_down,
        preferred_element_type=jnp.float32,
    )
    final = residual + lax.psum_scatter(
        lowered.astype(jnp.bfloat16), "head", scatter_dimension=0, tiled=True
    ).astype(jnp.float32)
    return final.astype(jnp.bfloat16)


def solution(mesh):
    placed = (
        P(("groups", "branch"), None),
        P(),
        P("branch", "head"),
        P("head"),
        P("branch", "head"),
        P("head"),
        P("branch", "head"),
        P("head"),
        P(("groups", "branch"), None, "head"),
        P(("groups", "branch"), None, "head"),
        P(("groups", "branch")),
        P(("groups", "branch"), None),
        P(("groups", "branch")),
        P("head", "branch"),
        P(),
        P("branch", "head"),
        P("branch", "head"),
        P("head", "branch"),
    )
    return jax.shard_map(
        local,
        mesh=mesh,
        in_specs=placed,
        out_specs=P(("groups", "head"), "branch"),
        check_vma=False,
    )
```

profile of v0, /device:TPU:0, one launch (start us, length us, event | category | flops | bytes accessed | tf_op | source)
XLA Modules:
  0.0 266.4 jit_solution(5067334849544949606)
XLA Ops:
  6.5 0.8 convert_element_type.98
  7.3 1.2 fusion.24
  8.6 1.2 fusion.26
  9.8 0.8 copy.83
  10.7 4.2 %all-to-all-start.1 = ((bf16[32,4,2048]{2,0,1:T(8,128)(2,1)}), bf16[32,4,2048]{2,0,1:T(8,128)(2,1)S(1)}, u32[]{:S(2)}, u32[]{:S(2)}) async-start(bf16[32,4,2048]{2,0,1:T(8,128)(2,1)} %bitcast.101), calls=%async_computation.1 | async-start | bytes 1048576 | tf_op jit(solution)/shard_map/all_to_all | solution.py:125
  15.6 1.2 dynamic-slice
  17.5 0.9 dynamic-update-slice
  18.3 5.7 %all-reduce = s32[128]{0:T(128)S(1)} all-reduce(s32[128]{0:T(128)S(1)} %dynamic-update-slice), channel_id=1, replica_groups=mesh['groups'=2,'branch'=4,'head'=4] {'branch'}, use_global_device_ids=true, to_apply=%add | all-reduce | flops 128 | bytes 1024
  24.8 0.7 iota_compare_fusion.8
  25.5 0.8 fusion.23
  26.6 0.7 multiply_add_fusion.3
  27.3 0.7 maximum_convert_fusion
  28.0 0.8 fusion.44
  29.0 4.7 %fusion.89 = f32[128,2048]{1,0:T(8,128)S(1)} fusion(bf16[128,2048]{1,0:T(8,128)(2,1)S(1)} %bitcast.103, bf16[2048,2048]{1,0:T(8,128)(2,1)} %param.20), kind=kOutput, calls=%fused_computation.170 | convolution fusion | flops 1073741824 | bytes 9961472 | tf_op jit(solution)/shard_map/dot_general | solution.py:132
  34.4 1.2 pad_maximum_fusion.1
  36.2 7.0 %reshape.350 = bf16[8192,2,128]{2,1,0:T(2,128)(2,1)} reshape(bf16[64,128,256]{2,1,0:T(8,128)(2,1)} %param.26) | data formatting | bytes 8388608 | tf_op jit(solution)/shard_map/reshape | solution.py:187
  43.1 7.0 %reshape.351 = bf16[8192,2,128]{2,1,0:T(2,128)(2,1)} reshape(bf16[64,128,256]{2,1,0:T(8,128)(2,1)} %param.27) | data formatting | bytes 8388608 | tf_op jit(solution)/shard_map/reshape | solution.py:188
  50.1 10.1 %fusion.87 = (bf16[8192,1,128]{2,1,0:T(2,128)(2,1)}, bf16[8192,1,128]{2,1,0:T(2,128)(2,1)}) fusion(bf16[8192,2,128]{2,1,0:T(2,128)(2,1)} %reshape.350), kind=kLoop, calls=%fused_computation.168 | loop fusion | bytes 8388608 | tf_op jit(solution)/shard_map/slice | solution.py:196
  60.2 7.0 %fusion.86 = (bf16[8192,1,128]{2,1,0:T(2,128)(2,1)}, bf16[8192,1,128]{2,1,0:T(2,128)(2,1)}) fusion(bf16[8192,2,128]{2,1,0:T(2,128)(2,1)S(1)} %copy-done.2), kind=kLoop, calls=%fused_computation.167 | loop fusion | bytes 8388608 | tf_op jit(solution)/shard_map/slice | solution.py:197
  67.2 1.8 fusion.16
  69.0 3.3 %all-to-all-start.2 = ((bf16[4,8,2560]{2,1,0:T(8,128)(2,1)}), bf16[4,8,2560]{2,1,0:T(8,128)(2,1)S(1)}, u32[]{:S(2)}, u32[]{:S(2)}) async-start(bf16[4,8,2560]{2,1,0:T(8,128)(2,1)} %fusion.16), calls=%async_computation.3 | async-start | bytes 327680 | tf_op jit(solution)/shard_map/all_to_all | solution.py:150
  72.7 4.6 %all-to-all-done.2 = bf16[4,8,2560]{2,1,0:T(8,128)(2,1)S(1)} async-done(((bf16[4,8,2560]{2,1,0:T(8,128)(2,1)}), bf16[4,8,2560]{2,1,0:T(8,128)(2,1)S(1)}, u32[]{:S(2)}, u32[]{:S(2)}) %all-to-all-start.2) | async-done | bytes 163872 | tf_op jit(solution)/shard_map/all_to_all | solution.py:150
  78.5 4.4 %select_reduce_fusion.1 = (f32[32,8]{1,0:T(8,128)S(1)}, f32[32,8,8192]{2,1,0:T(8,128)S(1)}) fusion(pred[32,8192]{1,0:T(8,128)(4,1)S(1)} %bitcast.108, bf16[8192,1,128]{2,1,0:T(2,128)(2,1)} %get-tuple-element.15, bf16[32,16,128]{2,1,0:T(8,128)(2,1)S(1)} %convolution_convert_fusion.6), kind=kOutput, calls=%fused_computation.5 | convolution fusion | flops 543162112 | bytes 10814464 | tf_op jit(solution)/shard_map/rd,td->rt/dot_general | solution.py:60
  83.0 2.5 fusion.8
  85.5 7.3 %fusion = (f32[32,8]{1,0:T(8,128)S(1)}, f32[32,8]{1,0:T(8,128)S(1)}, f32[32,8,8192]{2,1,0:T(8,128)}) fusion(f32[32,8,8192]{2,1,0:T(8,128)S(1)} %get-tuple-element.32, f32[32,8]{1,0:T(8,128)S(1)} %multiply_maximum_fusion.1, pred[32,8192]{1,0:T(8,128)(4,1)S(1)} %bitcast.110, bf16[8192,1,128]{2,1,0:T(2,128)(2,1)S(1)} %copy-done.5, ...), kind=kOutput, calls=%fused_computation.6 | convolution fusion | flops 549453312 | bytes 21317632 | tf_op jit(solution)/shard_map/rd,td->rt/dot_general | solution.py:60
  92.8 5.3 %fusion.2 = f32[32,8]{1,0:T(8,128)S(1)} fusion(f32[32,8,8192]{2,1,0:T(8,128)} %get-tuple-element.33, f32[32,8]{1,0:T(8,128)S(1)} %get-tuple-element.34, pred[32,8192]{1,0:T(8,128)(4,1)S(1)} %bitcast.111), kind=kLoop, calls=%fused_computation.8 | loop fusion | flops 6291200 | bytes 8652800 | tf_op jit(solution)/shard_map/reduce_sum | solution.py:72
  98.6 4.7 %fusion.5 = f32[256,128]{1,0:T(8,128)S(1)} fusion(f32[32,8,8192]{2,1,0:T(8,128)S(1)} %copy-done.3, f32[32,8]{1,0:T(8,128)S(1)} %get-tuple-element.34, pred[32,8192]{1,0:T(8,128)(4,1)S(1)} %bitcast.112, bf16[8192,1,128]{2,1,0:T(2,128)(2,1)} %get-tuple-element.14), kind=kOutput, calls=%fused_computation.13 | convolution fusion | flops 543162368 | bytes 10880000 | tf_op jit(solution)/shard_map/dot_general | solution.py:73
  104.0 7.0 %all_to_all.48 = bf16[4,8,2048]{2,1,0:T(8,128)(2,1)S(1)} all-to-all(bf16[4,8,2048]{2,1,0:T(8,128)(2,1)S(1)} %reshape.332), channel_id=1, replica_groups=mesh['groups'=2,'branch'=4,'head'=4] {'branch'}, dimensions={0} | all-to-all | bytes 262144 | tf_op jit(solution)/shard_map/all_to_all | solution.py:213
  111.2 6.7 %all_gather.13 = bf16[128,2048]{1,0:T(8,128)(2,1)S(1)} all-gather(bf16[32,2048]{1,0:T(8,128)(2,1)S(1)} %convolution_convert_fusion.5), channel_id=1, replica_groups=mesh['groups'=2,'branch'=4,'head'=4] {'branch'}, dimensions={0}, use_global_device_ids=true | all-gather | bytes 655360 | tf_op jit(solution)/shard_map/all_gather | solution.py:220
  118.0 5.5 %convolution_convert_fusion.3 = bf16[128,2048]{1,0:T(8,128)(2,1)} fusion(bf16[128,2048]{1,0:T(8,128)(2,1)S(1)} %all_gather.13, bf16[2048,2048]{1,0:T(8,128)(2,1)} %param.31), kind=kOutput, calls=%fused_computation.24 | convolution fusion | flops 1074003968 | bytes 9437184 | tf_op jit(solution)/shard_map/dot_general | solution.py:219
  123.5 0.9 copy.84
  124.4 3.5 %all-to-all-start = ((bf16[32,4,2048]{2,0,1:T(8,128)(2,1)}), bf16[32,4,2048]{2,0,1:T(8,128)(2,1)S(1)}, u32[]{:S(2)}, u32[]{:S(2)}) async-start(bf16[32,4,2048]{2,0,1:T(8,128)(2,1)} %bitcast.102), calls=%async_computation | async-start | bytes 1048576 | tf_op jit(solution)/shard_map/all_to_all | solution.py:126
  127.9 0.7 dynamic-slice_convert_fusion
  128.6 8.1 %all-to-all-done = bf16[32,4,2048]{2,0,1:T(8,128)(2,1)S(1)} async-done(((bf16[32,4,2048]{2,0,1:T(8,128)(2,1)}), bf16[32,4,2048]{2,0,1:T(8,128)(2,1)S(1)}, u32[]{:S(2)}, u32[]{:S(2)}) %all-to-all-start) | async-done | bytes 524320 | tf_op jit(solution)/shard_map/all_to_all | solution.py:126
  136.6 10.2 %reduce-scatter.7.cloned.1.call-done = bf16[32,2048]{1,0:T(8,128)(2,1)} async-done(((bf16[128,2048]{1,0:T(8,128)(2,1)}), bf16[32,2048]{1,0:T(8,128)(2,1)}) %reduce-scatter.7.cloned.1.call-update) | async-done | bytes 131088 | tf_op jit(solution)/shard_map/reduce_scatter | solution.py:231
  146.8 1.1 multiply_reduce_fusion
  147.9 5.7 %psum.7 = f32[32]{0:T(128)S(1)} all-reduce(f32[32]{0:T(128)S(1)} %multiply_reduce_fusion), channel_id=1, replica_groups=mesh['groups'=2,'branch'=4,'head'=4] {'branch'}, use_global_device_ids=true, to_apply=%region_15.16 | all-reduce | flops 32 | bytes 256 | tf_op jit(solution)/shard_map/psum | solution.py:234
  153.6 1.0 multiply_convert_fusion
  154.6 16.2 %all_gather.14 = bf16[128,2048]{1,0:T(8,128)(2,1)S(1)} all-gather(bf16[32,2048]{1,0:T(8,128)(2,1)S(1)} %multiply_convert_fusion), channel_id=1, replica_groups=mesh['groups'=2,'branch'=4,'head'=4] {'head'}, dimensions={0}, use_global_device_ids=true | all-gather | bytes 655360 | tf_op jit(solution)/shard_map/all_gather | solution.py:238
  170.8 7.7 %convolution_convert_fusion = bf16[128,3840]{1,0:T(8,128)(2,1)S(1)} fusion(bf16[128,2048]{1,0:T(8,128)(2,1)S(1)} %all_gather.14, bf16[2048,3840]{1,0:T(8,128)(2,1)} %param.34), kind=kOutput, calls=%fused_computation.10 | convolution fusion | flops 2013757440 | bytes 17235968 | tf_op jit(solution)/shard_map/dot_general | solution.py:244
  178.5 7.7 %convolution_convert_fusion.1 = bf16[128,3840]{1,0:T(8,128)(2,1)S(1)} fusion(bf16[128,2048]{1,0:T(8,128)(2,1)S(1)} %all_gather.14, bf16[2048,3840]{1,0:T(8,128)(2,1)} %param.33), kind=kOutput, calls=%fused_computation.11 | convolution fusion | flops 2013757440 | bytes 17235968 | tf_op jit(solution)/shard_map/dot_general | solution.py:243
  186.2 1.4 pad_maximum_fusion
  187.7 28.8 %reduce-scatter.9.cloned.1.call-done = bf16[32,7680]{1,0:T(8,128)(2,1)} async-done(((bf16[128,7680]{1,0:T(8,128)(2,1)}), bf16[32,7680]{1,0:T(8,128)(2,1)}) %reduce-scatter.9.cloned.1.call-update) | async-done | bytes 491536 | tf_op jit(solution)/shard_map/reduce_scatter | solution.py:240
  216.5 1.1 convert_element_type.115
  217.8 9.4 %all_gather.15 = bf16[128,3840]{1,0:T(8,128)(2,1)S(1)} all-gather(bf16[32,3840]{1,0:T(8,128)(2,1)S(1)} %fusion.27), channel_id=1, replica_groups=mesh['groups'=2,'branch'=4,'head'=4] {'branch'}, dimensions={0}, use_global_device_ids=true | all-gather | bytes 1228800 | tf_op jit(solution)/shard_map/all_gather | solution.py:255
  227.2 8.8 %convolution_convert_fusion.4 = bf16[128,2048]{1,0:T(8,128)(2,1)} fusion(bf16[128,3840]{1,0:T(8,128)(2,1)S(1)} %all_gather.15, bf16[3840,2048]{1,0:T(8,128)(2,1)} %param.35), kind=kOutput, calls=%fused_computation.25 | convolution fusion | flops 2013528064 | bytes 17235968 | tf_op jit(solution)/shard_map/dot_general | solution.py:254
  236.0 22.2 %reduce-scatter.11.cloned.1.call-done = bf16[32,2048]{1,0:T(8,128)(2,1)} async-done(((bf16[128,2048]{1,0:T(8,128)(2,1)}), bf16[32,2048]{1,0:T(8,128)(2,1)}) %reduce-scatter.11.cloned.1.call-update) | async-done | bytes 131088 | tf_op jit(solution)/shard_map/reduce_scatter | solution.py:259
  258.2 1.6 add_convert_fusion.1
  (72 shorter events, 6.5 us)
Async XLA Ops:
  6.5 27.2 %copy-start = (bf16[2048,256]{1,0:T(8,128)(2,1)S(1)}, bf16[2048,256]{1,0:T(8,128)(2,1)}, u32[]{:S(2)}) copy-start(bf16[2048,256]{1,0:T(8,128)(2,1)} %param.22) | copy-start | bytes 3145732
  10.7 18.3 %all-to-all-start.1 = ((bf16[32,4,2048]{2,0,1:T(8,128)(2,1)}), bf16[32,4,2048]{2,0,1:T(8,128)(2,1)S(1)}, u32[]{:S(2)}, u32[]{:S(2)}) async-start(bf16[32,4,2048]{2,0,1:T(8,128)(2,1)} %bitcast.101), calls=%async_computation.1 | async-start | bytes 1048576 | tf_op jit(solution)/shard_map/all_to_all | solution.py:125
  14.9 52.3 %reduce-scatter.5.cloned.1.call-start = ((), (), s32[]{:S(2)}) async-start(), calls=%async_computation.8 | async-start | bytes 1638400 | tf_op jit(solution)/shard_map/reduce_scatter | solution.py:129
  29.0 5.1 %copy-start.8 = (bf16[2048,256]{1,0:T(8,128)(2,1)S(1)}, bf16[2048,256]{1,0:T(8,128)(2,1)}, u32[]{:S(2)}) copy-start(bf16[2048,256]{1,0:T(8,128)(2,1)} %param.24) | copy-start | bytes 3145732
  50.1 10.1 %copy-start.2 = (bf16[8192,2,128]{2,1,0:T(2,128)(2,1)S(1)}, bf16[8192,2,128]{2,1,0:T(2,128)(2,1)}, u32[]{:S(2)}) copy-start(bf16[8192,2,128]{2,1,0:T(2,128)(2,1)} %reshape.351) | copy-start | bytes 12582916
  69.0 8.3 %all-to-all-start.2 = ((bf16[4,8,2560]{2,1,0:T(8,128)(2,1)}), bf16[4,8,2560]{2,1,0:T(8,128)(2,1)S(1)}, u32[]{:S(2)}, u32[]{:S(2)}) async-start(bf16[4,8,2560]{2,1,0:T(8,128)(2,1)} %fusion.16), calls=%async_computation.3 | async-start | bytes 327680 | tf_op jit(solution)/shard_map/all_to_all | solution.py:150
  72.3 74.5 %reduce-scatter.7.cloned.1.call-start = ((), (), s32[]{:S(2)}) async-start(), calls=%async_computation.9 | async-start | bytes 655360 | tf_op jit(solution)/shard_map/reduce_scatter | solution.py:231
  77.3 5.6 %copy-start.6 = (bf16[8192,1,128]{2,1,0:T(2,128)(2,1)S(1)}, bf16[8192,1,128]{2,1,0:T(2,128)(2,1)}, u32[]{:S(2)}) copy-start(bf16[8192,1,128]{2,1,0:T(2,128)(2,1)} %get-tuple-element.13) | copy-start | bytes 6291460
  83.0 2.5 copy-start.5
  92.8 5.8 %copy-start.3 = (f32[32,8,8192]{2,1,0:T(8,128)S(1)}, f32[32,8,8192]{2,1,0:T(8,128)}, u32[]{:S(2)}) copy-start(f32[32,8,8192]{2,1,0:T(8,128)} %get-tuple-element.33) | copy-start | bytes 25165828
  118.0 5.5 %copy-start.4 = (bf16[32,8192]{1,0:T(8,128)(2,1)S(1)}, bf16[32,8192]{1,0:T(8,128)(2,1)}, u32[]{:S(2)}) copy-start(bf16[32,8192]{1,0:T(8,128)(2,1)} %param.18) | copy-start | bytes 1572868
  124.4 12.3 %all-to-all-start = ((bf16[32,4,2048]{2,0,1:T(8,128)(2,1)}), bf16[32,4,2048]{2,0,1:T(8,128)(2,1)S(1)}, u32[]{:S(2)}, u32[]{:S(2)}) async-start(bf16[32,4,2048]{2,0,1:T(8,128)(2,1)} %bitcast.102), calls=%async_computation | async-start | bytes 1048576 | tf_op jit(solution)/shard_map/all_to_all | solution.py:126
  127.8 88.7 %reduce-scatter.9.cloned.1.call-start = ((), (), s32[]{:S(2)}) async-start(), calls=%async_computation.10 | async-start | bytes 2457600 | tf_op jit(solution)/shard_map/reduce_scatter | solution.py:240
  187.6 70.6 %reduce-scatter.11.cloned.1.call-start = ((), (), s32[]{:S(2)}) async-start(), calls=%async_computation.11 | async-start | bytes 655360 | tf_op jit(solution)/shard_map/reduce_scatter | solution.py:259
  217.8 42.1 %copy-start.1 = (bf16[2048,256]{1,0:T(8,128)(2,1)S(1)}, bf16[2048,256]{1,0:T(8,128)(2,1)}, u32[]{:S(2)}) copy-start(bf16[2048,256]{1,0:T(8,128)(2,1)} %param.22) | copy-start | bytes 3145732
  227.2 31.0 %copy-start.7 = (bf16[32,2048]{1,0:T(8,128)(2,1)S(1)}, bf16[32,2048]{1,0:T(8,128)(2,1)}, u32[]{:S(2)}) copy-start(bf16[32,2048]{1,0:T(8,128)(2,1)} %reduce-scatter.7.cloned.1.call-done) | copy-start | bytes 393220
Sparse Core Ops, SparseCore 0:
  35.8 27.6 reduce-scatter.4
  123.6 23.1 reduce-scatter.6
  187.8 28.7 reduce-scatter.8
  236.1 22.0 reduce-scatter.10
where the time goes:
time: 268 us; the launch traced here: 266 us
  waiting for transfers between devices  74 us (28%)
  matrix products  58 us (22%)
  blocking collectives  50.7 us (19%)
  local copies, waits for them, and re-layouts  36.2 us (14%)
  other arithmetic  22 us (8%)
  between operations  14.2 us (5%)
  starting transfers between devices  11.3 us (4%)
    reduce_scatter x1, waiting for transfers between devices, local(): lax.psum_scatter(jnp.concatenate([jnp.dot(picked, w_gate, preferred_eleme...  28.8 us
    reduce_scatter x1, waiting for transfers between devices, local(): lax.psum_scatter(lowered.astype(jnp.bfloat16), 'head', scatter_dimension=...  22.2 us
    all_gather x1, blocking collectives, local(): normed_ffn = lax.all_gather(normed_share, 'head', axis=0, tiled=True)  16.2 us
    dot_general x2, matrix products, attend_block(): jnp.einsum('rd,td->rt', turned_block.reshape(slots * heads_here, HD), key...  11.7 us
    reduce_scatter x1, waiting for transfers between devices, local(): lax.psum_scatter(mixer.astype(jnp.bfloat16), 'head', scatter_dimension=0,...  10.2 us
    slice x1, local copies, waits for them, and re-layouts, local(): keys_now = cache_keys[:, kv_index, :]  10.1 us
    all_gather x1, blocking collectives, local(): lax.all_gather(activated, 'branch', axis=0, tiled=True)  9.43 us
    dot_general x1, matrix products, local(): jnp.dot(lax.all_gather(activated, 'branch', axis=0, tiled=True), w_down,...  8.76 us
  transfers between devices with their start and end apart: 7, of which 5 were waited for; matrix products, arithmetic and copies ran while one was open for 15% of the time, Pallas kernels for 0%

commit v1 on v0

v1 whole, which is shorter than its diff:
```python
import functools
import math

import jax
import jax.numpy as jnp
import numpy as np
from jax import lax
from jax.experimental import pallas as pl
from jax.experimental.pallas import tpu as pltpu
from jax.sharding import PartitionSpec as P

D = 8192
HD = 128
PAGE = 128
MAXP = 32
POOL = 64
P_DEV = 4
CAP = 8
EXT = 128
CORES = 2

EPS = 1e-06
THETA = 1000000.0
FAR = -1e30
MIB = 1024 * 1024
SPARE = 10 * MIB

F32 = jnp.float32
BF16 = jnp.bfloat16


def hadamard(order_size):
    index = np.arange(order_size)
    common = index[:, None] & index[None, :]
    parity = np.zeros((order_size, order_size), np.int64)
    for bit_level in range(order_size.bit_length() - 1):
        parity = parity ^ (common >> bit_level & 1)
    return ((1 - 2 * parity).astype(np.float32) / np.float32(math.sqrt(order_size))).astype(
        np.float32
    )


SPACES = {"vmem": pltpu.VMEM, "hbm": pltpu.HBM, "any": pl.ANY, "smem": pltpu.SMEM}


def call(kernel, outs, in_spaces, scratch, *args, limit=SPARE, flops=0, moved=0):
    return pl.pallas_call(
        kernel,
        out_shape=[jax.ShapeDtypeStruct(shape, kind) for shape, kind in outs],
        in_specs=[pl.BlockSpec(memory_space=SPACES[space]) for space in in_spaces],
        out_specs=[pl.BlockSpec(memory_space=pltpu.VMEM) for _ in outs],
        scratch_shapes=scratch,
        compiler_params=pltpu.CompilerParams(vmem_limit_bytes=limit),
        cost_estimate=pl.CostEstimate(flops=flops, bytes_accessed=moved, transcendentals=0),
    )(*args)


def fetch_kernel(count, *refs):
    sources, targets, sems = refs[:count], refs[-1 - count : -1], refs[-1]
    copies = [
        pltpu.make_async_copy(source, target, sems.at[at])
        for at, (source, target) in enumerate(zip(sources, targets))
    ]
    for copy in copies:
        copy.start()
    for copy in copies:
        copy.wait()


def fetch(arrays, after, limit=2 * MIB):
    size = sum(array.size * array.dtype.itemsize for array in arrays)
    return pl.pallas_call(
        functools.partial(fetch_kernel, len(arrays)),
        out_shape=[pltpu.VMEM(array.shape, array.dtype) for array in arrays],
        in_specs=[pl.BlockSpec(memory_space=pltpu.HBM)] * len(arrays)
        + [pl.BlockSpec(memory_space=pl.ANY)],
        out_specs=[pl.BlockSpec(memory_space=pltpu.VMEM)] * len(arrays),
        scratch_shapes=[pltpu.SemaphoreType.DMA((len(arrays),))],
        compiler_params=pltpu.CompilerParams(vmem_limit_bytes=limit),
        cost_estimate=pl.CostEstimate(flops=0, bytes_accessed=2 * size, transcendentals=0),
    )(*arrays, after)


def block_width(columns, most):
    best = 128
    for width in range(128, most + 1, 128):
        if columns % width == 0:
            best = width
    return best


class Place:
    def __init__(self, spot, chips, head_count):
        self.chips = chips
        self.head_count = head_count
        self.branch, self.head = spot[0], spot[1]
        self.chip, self.core = self.branch // CORES, self.branch % CORES
        self.steps = [(chip, core) for core in range(CORES) for chip in range(chips)]

    def targets(self):
        return [
            (self.chip + chip) % self.chips * CORES + (self.core + core) % CORES
            for chip, core in self.steps
        ]

    def sources(self):
        return [
            (self.chip + self.chips - chip) % self.chips * CORES + (self.core + core) % CORES
            for chip, core in self.steps
        ]

    def to_heads(self):
        return [(self.head + step) % self.head_count for step in range(self.head_count)]

    def from_heads(self):
        return [
            (self.head + self.head_count - step) % self.head_count
            for step in range(self.head_count)
        ]


def column(devices, length):
    iota = lax.broadcasted_iota(jnp.int32, (length, 1), 0)
    return jnp.concatenate([iota + device * length for device in devices], 0).astype(F32)


def to_row(values):
    size = values.shape[0]
    row_at = lax.broadcasted_iota(jnp.int32, (size, size), 0)
    col_at = lax.broadcasted_iota(jnp.int32, (size, size), 1)
    return jnp.sum(jnp.where(row_at == col_at, values, 0.0), 0, keepdims=True)


def onehot(rows, columns):
    return (rows == to_row(columns)).astype(BF16)


def split_lanes(total):
    rows = total.shape[0]
    high = total.astype(BF16).astype(F32)
    rest = total - high
    middle = rest.astype(BF16).astype(F32)
    low = rest - middle
    lane = lax.broadcasted_iota(jnp.int32, (rows, EXT), 1)
    zero = jnp.zeros((rows, EXT), F32)
    return jnp.where(
        lane == 0, high, jnp.where(lane == 1, middle, jnp.where(lane == 2, low, zero))
    ).astype(BF16)


def dot32(left, right):
    return jnp.dot(left, right, preferred_element_type=F32)


def send_kernel(chips, spot, hidden, parents, *blocks):
    place = Place(spot, chips, 1)
    length, width = hidden.shape[0], blocks[0].shape[1] - EXT
    row_at = lax.broadcasted_iota(jnp.int32, (length, length), 0)
    col_at = lax.broadcasted_iota(jnp.int32, (length, length), 1)
    turned = jnp.sum(
        jnp.where(row_at == col_at, parents[...].astype(F32), 0.0), 1, keepdims=True
    )
    mark = jnp.broadcast_to(turned, (length, EXT)).astype(BF16)
    for ref, device in zip(blocks, place.targets()):
        ref[:, :width] = hidden[:, pl.ds(pl.multiple_of(device * width, width), width)]
        ref[:, width:] = mark


def qkv_kernel(slots, chips, head_count, width, *refs):
    spot = refs[0]
    blocks_n = chips * CORES
    blocks = refs[1 : 1 + blocks_n]
    gain, wq, wk, wv, keep, send, share, codes = refs[1 + blocks_n :]
    place = Place(spot, chips, head_count)
    model_cols = gain.shape[1]
    length = blocks[0].shape[0]
    rows = jnp.concatenate([ref[:, :model_cols] for ref in blocks], 0)
    parent = jnp.concatenate([ref[:, model_cols:] for ref in blocks], 0)[:, :1].astype(F32)
    dest = jnp.floor(parent * (1.0 / P_DEV))
    order = column(place.sources(), length)
    order_row = to_row(order)
    same = (dest == to_row(dest)) & (order_row < order)
    code = dest * slots + jnp.sum(same.astype(F32), 1, keepdims=True)
    lane = lax.broadcasted_iota(jnp.int32, codes.shape, 1)
    codes[...] = jnp.where(lane == 0, code, parent)
    placing = onehot(column(place.targets(), slots), code)
    own = column([place.head], share.shape[0])
    share[...] = dot32((own == order_row).astype(BF16), rows).astype(BF16)
    placed = dot32(placing, rows)
    squares = jnp.sum(placed * placed, 1, keepdims=True)
    scaled = (placed * gain[...]).astype(BF16)
    half = keep.shape[0]
    total_cols = keep.shape[1] - EXT
    keep[:, total_cols:] = jnp.broadcast_to(squares[:half], (half, EXT))
    send[:, total_cols:] = jnp.broadcast_to(squares[half:], (half, EXT))
    at = 0
    for weight in (wq, wk, wv):
        wide = block_width(weight.shape[1], width)
        for step in range(weight.shape[1] // wide):
            product = dot32(scaled, weight[:, step * wide : (step + 1) * wide])
            keep[:, at : at + wide] = product[:half]
            send[:, at : at + wide] = product[half:]
            at += wide


def chip_sum_kernel(slots, keep, got, mine, *others):
    mine[...] = keep[:slots] + got[:slots]
    for at, ref in enumerate(others):
        low, high = (at + 1) * slots, (at + 2) * slots
        total = keep[low:high] + got[low:high]
        ref[:, :-EXT] = total[:, :-EXT].astype(BF16)
        ref[:, -EXT:] = split_lanes(total[:, -EXT:][:, :1])


def attend_kernel(kv_local, group_size, chunk_pages, unroll, received_n, *refs):
    spot, path_pages, mine = refs[:3]
    received = refs[3 : 3 + received_n]
    bq, bk, bv, waves, codes, page_table, turn, kbuf, vbuf = refs[3 + received_n : 12 + received_n]
    out, scores, mixed, sums = refs[12 + received_n :]
    slots = mine.shape[0]
    squares = mine[:, -EXT:][:, :1]
    total = mine[:, :-EXT]
    for ref in received:
        total = total + ref[:, :-EXT].astype(F32)
        squares = squares + jnp.sum(ref[:, -EXT:].astype(F32), 1, keepdims=True)
    bias = jnp.concatenate([ref[...].astype(F32) for ref in (bq, bk, bv)], 1)
    packed = (total * lax.rsqrt(squares * (1.0 / D) + EPS) + bias).astype(BF16).astype(F32)
    heads = kv_local * group_size
    rotation = turn[...]
    code, parent = codes[:, :1], codes[:, 1:2]
    lane = lax.broadcasted_iota(jnp.int32, (1, EXT), 1).astype(F32)
    parent_at = (parent - jnp.floor(parent * (1.0 / P_DEV)) * P_DEV == lane).astype(BF16)
    slot_mark = dot32(onehot(column([spot[0]], slots), code), parent_at)
    wave = jnp.zeros((slots, 2 * HD), F32)
    page_at = lax.broadcasted_iota(jnp.int32, (POOL, MAXP), 0)
    turn_at = lax.broadcasted_iota(jnp.int32, (POOL, MAXP), 1)
    page_mark = jnp.zeros((POOL, EXT), F32)
    for local_parent in range(P_DEV):
        wave = wave + slot_mark[:, local_parent : local_parent + 1] * waves[
            local_parent : local_parent + 1, :
        ]
        live = (page_table[local_parent : local_parent + 1, :] == page_at) & (
            turn_at < path_pages[local_parent]
        )
        owned = jnp.max(live.astype(F32), 1, keepdims=True)
        page_mark = jnp.where(lane == local_parent, (1.0 - owned) * FAR, page_mark)
    page_marks = page_mark.astype(BF16).astype(F32)

    def stacked(first, count):
        return jnp.concatenate(
            [packed[:, (first + at) * HD : (first + at + 1) * HD] for at in range(count)], 0
        )

    def rope(vectors, count):
        cos = jnp.concatenate([wave[:, :HD]] * count, 0)
        sin = jnp.concatenate([wave[:, HD:]] * count, 0)
        return vectors * cos + pltpu.roll(vectors, HD // 2, 1) * sin

    queries = rope(stacked(0, heads), heads)
    new_keys = rope(stacked(heads, kv_local), kv_local)
    turned = jnp.dot(
        queries, rotation, precision=lax.Precision.HIGHEST, preferred_element_type=F32
    ).astype(BF16)
    scale = 1.0 / math.sqrt(HD)
    rate = scale * math.log2(math.e)
    rows = group_size * slots
    chunk = chunk_pages * PAGE
    chunks = POOL // chunk_pages
    marks = jnp.concatenate([slot_mark.astype(BF16)] * group_size, 0)
    sums[:POOL, :] = page_marks
    for kv_at in range(kv_local):
        query_now = queries[kv_at * rows : (kv_at + 1) * rows]
        left = jnp.concatenate([turned[kv_at * rows : (kv_at + 1) * rows], marks], 1)
        key_now = jnp.concatenate([new_keys[kv_at * slots : (kv_at + 1) * slots]] * group_size, 0)
        own_score = jnp.sum(query_now * key_now, 1, keepdims=True)
        span = slice(kv_at * HD, (kv_at + 1) * HD)
        if kv_at > 0:
            sums[:POOL, :] = page_marks

        def first_pass(at, best):
            pages = pl.ds(pl.multiple_of(at * chunk_pages, chunk_pages), chunk_pages)
            page_keys = kbuf[pages, :, span].reshape(chunk, HD)
            mark = jnp.broadcast_to(
                sums[pages, :][:, None, :], (chunk_pages, PAGE, EXT)
            ).reshape(chunk, EXT)
            now = lax.dot_general(
                left,
                jnp.concatenate([page_keys, mark.astype(BF16)], 1),
                (((1,), (1,)), ((), ())),
                preferred_element_type=F32,
            )
            scores[at] = now
            for page in range(chunk_pages):
                best = jnp.maximum(best, now[:, page * PAGE : (page + 1) * PAGE])
            return best

        best = lax.fori_loop(
            0, chunks, first_pass, jnp.full((rows, PAGE), -jnp.inf, F32), unroll=unroll
        )
        top = jnp.maximum(jnp.max(best, 1, keepdims=True), own_score)
        top_rate = top * rate
        sums[...] = jnp.zeros_like(sums)
        mixed[...] = jnp.zeros_like(mixed)

        def second_pass(at, carry):
            pages = pl.ds(pl.multiple_of(at * chunk_pages, chunk_pages), chunk_pages)
            weights = jnp.exp2(scores[at] * rate - top_rate)
            part = weights[:, :PAGE]
            for page in range(1, chunk_pages):
                part = part + weights[:, page * PAGE : (page + 1) * PAGE]
            sums[:rows, :] += part
            page_values = vbuf[pages, :, span].reshape(chunk, HD)
            mixed[...] += dot32(weights.astype(BF16), page_values)
            return carry

        lax.fori_loop(0, chunks, second_pass, 0, unroll=unroll)
        own = jnp.exp2(own_score * rate - top_rate)
        whole = jnp.sum(sums[:rows, :], 1, keepdims=True) + own
        unturned = jnp.dot(
            mixed[...], rotation, precision=lax.Precision.HIGHEST, preferred_element_type=F32
        )
        value_at = (heads + kv_local + kv_at) * HD
        value_now = jnp.concatenate([packed[:, value_at : value_at + HD]] * group_size, 0)
        result = ((unturned + own * value_now) / whole).astype(BF16)
        for head in range(group_size):
            at = (kv_at * group_size + head) * HD
            out[:, at : at + HD] = result[head * slots : (head + 1) * slots]


def spread_rows(rows, order, weight, width, mine, others):
    ordered = dot32(order, rows).astype(BF16)
    share = mine.shape[0]
    for step in range(weight.shape[1] // width):
        span = slice(step * width, (step + 1) * width)
        product = dot32(ordered, weight[:, span])
        mine[:, span] = product[:share]
        for at, ref in enumerate(others):
            ref[:, span] = product[(at + 1) * share : (at + 2) * share].astype(BF16)


def mixer_kernel(slots, local_rows, chips, head_count, width, *refs):
    blocks_n = chips * CORES
    spot, codes = refs[:2]
    blocks = refs[2 : 2 + blocks_n]
    weight, mine = refs[2 + blocks_n : 4 + blocks_n]
    place = Place(spot, chips, head_count)
    sources = place.sources()
    slot_rows = onehot(codes[:, :1], column(sources, slots))
    child_rows = onehot(column(place.to_heads(), mine.shape[0]), column(sources, local_rows))
    order = dot32(child_rows, slot_rows).astype(BF16)
    rows = jnp.concatenate([ref[...] for ref in blocks], 0)
    spread_rows(rows, order, weight, width, mine, refs[4 + blocks_n :])


def lower_kernel(first, last, local_rows, chips, head_count, width, *refs):
    blocks_n = chips * CORES
    spot = refs[0]
    blocks = refs[1 : 1 + blocks_n]
    weight = refs[1 + blocks_n]
    before = None if first == 0 else refs[2 + blocks_n]
    outs = refs[(2 if first == 0 else 3) + blocks_n :]
    place = Place(spot, chips, head_count)
    share_rows = chips * CORES * local_rows // head_count
    order = onehot(column(place.to_heads(), share_rows), column(place.sources(), local_rows))
    rows = jnp.concatenate([ref[...] for ref in blocks], 0)
    ordered = dot32(order, rows).astype(BF16)
    deep = rows.shape[1]
    for step in range(weight.shape[1] // width):
        span = slice(step * width, (step + 1) * width)
        product = dot32(ordered, weight[first : first + deep, span])
        if before is not None:
            product = product + before[:, span]
        if not last:
            outs[0][:, span] = product
            continue
        outs[0][:, span] = product[:share_rows]
        for at, ref in enumerate(outs[1:]):
            ref[:, span] = product[(at + 1) * share_rows : (at + 2) * share_rows].astype(BF16)


def residual_kernel(share, mine, gain, *refs):
    received = refs[:-2]
    residual, scaled = refs[-2:]
    total = mine[...]
    for ref in received:
        total = total + ref[...].astype(F32)
    total = share[...].astype(F32) + total
    residual[...] = total
    scaled[:, :-EXT] = (total * gain[...]).astype(BF16)
    scaled[:, -EXT:] = split_lanes(jnp.sum(total * total, 1, keepdims=True))


def gate_columns(ordered, weights, first, count, width, keep, send):
    half = keep.shape[0]
    scaled = ordered[:, :-EXT]
    at = 0
    for weight in weights:
        for step in range(count // width):
            low = first + step * width
            product = dot32(scaled, weight[:, low : low + width])
            keep[:, at : at + width] = product[:half]
            send[:, at : at + width] = product[half:].astype(BF16)
            at += width


def first_gate_kernel(local_rows, chips, head_count, count, width, *refs):
    spot = refs[0]
    blocks = refs[1 : 1 + head_count]
    w_gate, w_up, keep, send, rest = refs[1 + head_count :]
    place = Place(spot, chips, head_count)
    order = onehot(
        column(place.targets(), local_rows), column(place.from_heads(), blocks[0].shape[0])
    )
    rows = jnp.concatenate([ref[...] for ref in blocks], 0)
    ordered = dot32(order, rows).astype(BF16)
    rest[...] = ordered
    half = keep.shape[0]
    keep[:, -EXT:] = ordered[:half, -EXT:].astype(F32)
    send[:, -EXT:] = ordered[half:, -EXT:]
    gate_columns(ordered, (w_gate, w_up), 0, count, width, keep, send)


def next_gate_kernel(first, count, width, ordered, w_gate, w_up, keep, send):
    gate_columns(ordered[...], (w_gate, w_up), first, count, width, keep, send)


def chip_gate_kernel(local_rows, columns, keep, got, mine, *others):
    mine[...] = keep[:local_rows] + got[:local_rows].astype(F32)
    for at, ref in enumerate(others):
        low, high = (at + 1) * local_rows, (at + 2) * local_rows
        total = keep[low:high] + got[low:high].astype(F32)
        ref[:, :columns] = total[:, :columns].astype(BF16)
        if total.shape[1] > columns:
            ref[:, columns:] = split_lanes(jnp.sum(total[:, columns:], 1, keepdims=True))


def gated(mine, received, columns, scale):
    gate = mine[:, :columns]
    up = mine[:, columns : 2 * columns]
    for ref in received:
        gate = gate + ref[:, :columns].astype(F32)
        up = up + ref[:, columns : 2 * columns].astype(F32)
    gate = gate * scale
    up = up * scale
    return (gate / (1.0 + jnp.exp(-gate)) * up).astype(BF16)


def first_activate_kernel(mine, *refs):
    received, _, out, scale_out = refs[:-3], refs[-3], refs[-2], refs[-1]
    squares = jnp.sum(mine[:, -EXT:], 1, keepdims=True)
    for ref in received:
        squares = squares + jnp.sum(ref[:, -EXT:].astype(F32), 1, keepdims=True)
    scale = lax.rsqrt(squares * (1.0 / D) + EPS)
    scale_out[...] = jnp.broadcast_to(scale, scale_out.shape)
    out[...] = gated(mine, received, out.shape[1], scale)


def next_activate_kernel(scale, mine, *refs):
    out = refs[-1]
    out[...] = gated(mine, refs[:-1], out.shape[1], scale[:, :1])


def final_kernel(residual, mine, *refs):
    received, out = refs[:-1], refs[-1]
    total = mine[...]
    for ref in received:
        total = total + ref[...].astype(F32)
    out[...] = (residual[...] + total).astype(BF16)


def local(
    hidden_in,
    input_gain,
    w_query,
    b_query,
    w_key,
    b_key,
    w_value,
    b_value,
    key_pages,
    value_pages,
    path_pages,
    page_table,
    parent_index,
    w_out,
    post_gain,
    w_gate,
    w_up,
    w_down,
):
    branch_count = lax.axis_size("branch")
    head_count = lax.axis_size("head")
    branch_pos = lax.axis_index("branch")
    head_pos = lax.axis_index("head")
    chips = branch_count // CORES
    local_rows = hidden_in.shape[0]
    all_rows = local_rows * branch_count
    share_rows = all_rows // head_count
    model_cols = w_query.shape[0]
    query_cols = w_query.shape[1]
    kv_cols = w_key.shape[1]
    kv_local = kv_cols // HD
    heads_local = query_cols // HD
    group_size = heads_local // kv_local
    slots = branch_count * CAP
    ff_local = w_gate.shape[1]
    packed_cols = query_cols + 2 * kv_cols
    spot = jnp.stack([branch_pos, head_pos]).astype(jnp.int32)
    steps = [(chip, core) for core in range(CORES) for chip in range(chips)]

    def over_branch(array, chip_step, core_step):
        pairs = []
        for source in range(branch_count):
            chip, core = source // CORES, source % CORES
            to = (chip + chip_step) % chips * CORES + (core + core_step) % CORES
            pairs.append((source, to))
        return lax.ppermute(array, "branch", pairs)

    def over_head(array, step):
        pairs = [(source, (source + step) % head_count) for source in range(head_count)]
        return lax.ppermute(array, "head", pairs)

    def gain_slice(gain):
        return lax.dynamic_slice_in_dim(gain, branch_pos * model_cols, model_cols, 0).astype(F32)[
            None
        ]

    outgoing = call(
        functools.partial(send_kernel, chips),
        [((local_rows, model_cols + EXT), BF16)] * branch_count,
        ["smem", "vmem", "vmem"],
        [],
        spot,
        hidden_in,
        parent_index[None],
    )
    hidden_blocks = [outgoing[0]]
    for block, (chip, core) in zip(outgoing[1:], steps[1:]):
        hidden_blocks.append(over_branch(block, chip, core))
    wq, wk, wv = fetch([w_query, w_key, w_value], outgoing[0], 44 * MIB)
    keep, send, share, codes = call(
        functools.partial(qkv_kernel, slots, chips, head_count, 512),
        [
            ((chips * slots, packed_cols + EXT), F32),
            ((chips * slots, packed_cols + EXT), F32),
            ((share_rows, model_cols), BF16),
            ((all_rows, EXT), F32),
        ],
        ["smem"] + ["vmem"] * (branch_count + 4),
        [],
        spot,
        *hidden_blocks,
        gain_slice(input_gain),
        wq,
        wk,
        wv,
        flops=2 * all_rows * model_cols * packed_cols,
    )
    got = over_branch(send, 0, 1)
    mine, *others = call(
        functools.partial(chip_sum_kernel, slots),
        [((slots, packed_cols + EXT), F32)]
        + [((slots, packed_cols + EXT), BF16)] * (chips - 1),
        ["vmem"] * 2,
        [],
        keep,
        got,
    )
    received = [over_branch(other, at + 1, 0) for at, other in enumerate(others)]
    keys, values = fetch([key_pages, value_pages], others[0])

    freqs = THETA ** (-(jnp.arange(HD // 2, dtype=F32) * 2.0 / HD))
    angle = (path_pages.astype(F32) * PAGE)[:, None] * freqs
    cosine, sine = jnp.cos(angle), jnp.sin(angle)
    waves = jnp.concatenate([cosine, cosine, -sine, sine], 1)
    chunk_pages, unroll = 8, 4
    rows = group_size * slots
    if rows > 512:
        unroll = 1
    score_bytes = 4 * rows * POOL * PAGE
    (attention,) = call(
        functools.partial(attend_kernel, kv_local, group_size, chunk_pages, unroll, chips - 1),
        [((slots, query_cols), BF16)],
        ["smem"] * 2 + ["vmem"] * (chips + 9),
        [
            pltpu.VMEM((POOL // chunk_pages, rows, chunk_pages * PAGE), F32),
            pltpu.VMEM((rows, HD), F32),
            pltpu.VMEM((max(rows, POOL), HD), F32),
        ],
        spot,
        path_pages,
        mine,
        *received,
        b_query[None],
        b_key[None],
        b_value[None],
        waves,
        codes,
        page_table,
        jnp.asarray(hadamard(HD)),
        keys,
        values,
        limit=score_bytes + SPARE + SPARE // 2,
        flops=4 * kv_cols * rows * POOL * PAGE,
    )

    def gather_branch(array):
        near = [array] + [over_branch(array, chip, 0) for chip in range(1, chips)]
        return near + [over_branch(block, 0, 1) for block in near]

    gathered = gather_branch(attention)
    (w_out_near,) = fetch([w_out], attention)
    out_width = block_width(model_cols, 512)
    mixer, *others = call(
        functools.partial(mixer_kernel, slots, local_rows, chips, head_count, out_width),
        [((share_rows, model_cols), F32)] + [((share_rows, model_cols), BF16)] * (head_count - 1),
        ["smem"] + ["vmem"] * (branch_count + 2),
        [],
        spot,
        codes,
        *gathered,
        w_out_near,
        flops=2 * all_rows * w_out.size,
    )
    received = [over_head(other, at + 1) for at, other in enumerate(others)]
    (w_gate_near,) = fetch([w_gate], mixer)
    residual, scaled = call(
        residual_kernel,
        [((share_rows, model_cols), F32), ((share_rows, model_cols + EXT), BF16)],
        ["vmem"] * (head_count + 2),
        [],
        share,
        mixer,
        gain_slice(post_gain),
        *received,
    )
    scaled_blocks = [scaled] + [over_head(scaled, step) for step in range(1, head_count)]
    (w_up_near,) = fetch([w_up], scaled)
    tiles = ff_local // 128
    cuts = [0, (tiles + 1) // 2 * 128, ff_local]
    counts = [high - low for low, high in zip(cuts, cuts[1:])]

    def gate_outs(extra):
        return [((chips * local_rows, extra), F32), ((chips * local_rows, extra), BF16)]

    keep, send, ordered = call(
        functools.partial(
            first_gate_kernel,
            local_rows,
            chips,
            head_count,
            counts[0],
            block_width(counts[0], 768),
        ),
        gate_outs(2 * counts[0] + EXT) + [((all_rows, model_cols + EXT), BF16)],
        ["smem"] + ["vmem"] * (head_count + 2),
        [],
        spot,
        *scaled_blocks,
        w_gate_near,
        w_up_near,
        flops=4 * all_rows * model_cols * counts[0],
    )
    parts = [(keep, over_branch(send, 0, 1))]
    keep, send = call(
        functools.partial(next_gate_kernel, cuts[1], counts[1], block_width(counts[1], 768)),
        gate_outs(2 * counts[1]),
        ["vmem"] * 3,
        [],
        ordered,
        w_gate_near,
        w_up_near,
        flops=4 * all_rows * model_cols * counts[1],
    )
    parts.append((keep, over_branch(send, 0, 1)))
    sums = []
    for (keep, got), count in zip(parts, counts):
        wide = keep.shape[1]
        mine, *others = call(
            functools.partial(chip_gate_kernel, local_rows, 2 * count),
            [((local_rows, wide), F32)] + [((local_rows, wide), BF16)] * (chips - 1),
            ["vmem"] * 2,
            [],
            keep,
            got,
        )
        sums.append((mine, [over_branch(other, at + 1, 0) for at, other in enumerate(others)], others))
    (w_down_near,) = fetch([w_down], sums[1][2][0], 32 * MIB)
    activated, scale = call(
        first_activate_kernel,
        [((local_rows, counts[0]), BF16), ((local_rows, EXT), F32)],
        ["vmem"] * chips + ["any"],
        [],
        sums[0][0],
        *sums[0][1],
        w_down_near,
    )
    gathered = gather_branch(activated)
    (activated,) = call(
        next_activate_kernel,
        [((local_rows, counts[1]), BF16)],
        ["vmem"] * (chips + 1),
        [],
        scale,
        sums[1][0],
        *sums[1][1],
    )
    gathered_next = gather_branch(activated)
    (partial,) = call(
        functools.partial(lower_kernel, 0, False, local_rows, chips, head_count, out_width),
        [((all_rows, model_cols), F32)],
        ["smem"] + ["vmem"] * (branch_count + 1),
        [],
        spot,
        *gathered,
        w_down_near,
        flops=2 * all_rows * model_cols * counts[0],
    )
    lowered, *others = call(
        functools.partial(lower_kernel, cuts[1], True, local_rows, chips, head_count, out_width),
        [((share_rows, model_cols), F32)] + [((share_rows, model_cols), BF16)] * (head_count - 1),
        ["smem"] + ["vmem"] * (branch_count + 2),
        [],
        spot,
        *gathered_next,
        w_down_near,
        partial,
        flops=2 * all_rows * model_cols * counts[1],
    )
    received = [over_head(other, at + 1) for at, other in enumerate(others)]
    (final,) = call(
        final_kernel,
        [((share_rows, model_cols), BF16)],
        ["vmem"] * (head_count + 1),
        [],
        residual,
        lowered,
        *received,
    )
    return final


def solution(mesh):
    placed = (
        P(("groups", "branch"), None),
        P(),
        P("branch", "head"),
        P("head"),
        P("branch", "head"),
        P("head"),
        P("branch", "head"),
        P("head"),
        P(("groups", "branch"), None, "head"),
        P(("groups", "branch"), None, "head"),
        P(("groups", "branch")),
        P(("groups", "branch"), None),
        P(("groups", "branch")),
        P("head", "branch"),
        P(),
        P("branch", "head"),
        P("branch", "head"),
        P("head", "branch"),
    )
    return jax.shard_map(
        local,
        mesh=mesh,
        in_specs=placed,
        out_specs=P(("groups", "head"), "branch"),
        check_vma=False,
    )
```

time: 268 us -> 115 us (0.43)
  matrix products: 58 us -> 0 us
  blocking collectives: 50.7 us -> 0 us
  waiting for transfers between devices: 74 us -> 33.6 us
  Pallas kernels: 0 us -> 38.7 us
  local copies, waits for them, and re-layouts: 36.2 us -> 7.91 us
  starting transfers between devices: 11.3 us -> 31.9 us
  other arithmetic: 22 us -> 1.81 us
  between operations: 14.2 us -> 0.35 us
    reduce_scatter x4 -> x0, waiting for transfers between devices: 61.3 us -> none  [the longest x1 28.8 us: local(): lax.psum_scatter(jnp.concatenate([jnp.dot(picked, w_gate, preferred_eleme...]
    dot_general x19 -> x0, matrix products: 58 us -> none  [the longest x2 11.7 us: attend_block(): jnp.einsum('rd,td->rt', turned_block.reshape(slots * heads_here, HD), key...]
    pallas_call x0 -> x21, Pallas kernels: none -> 38.7 us  [the longest x15 25.9 us: call(): pl.pallas_call(kernel, out_shape=[jax.ShapeDtypeStruct(shape, kind) for s...]
    ppermute x0 -> x27, waiting for transfers between devices: none -> 33.6 us  [the longest x18 17.6 us: over_branch(): return lax.ppermute(array, 'branch', pairs)]
    all_gather x3 -> x0, blocking collectives: 32.4 us -> none  [the longest x1 16.2 us: local(): normed_ffn = lax.all_gather(normed_share, 'head', axis=0, tiled=True)]
    ppermute x0 -> x27, starting transfers between devices: none -> 31.9 us  [the longest x9 17.5 us: over_head(): return lax.ppermute(array, 'head', pairs)]
    slice x3 -> x0, local copies, waits for them, and re-layouts: 17.1 us -> none  [the longest x1 10.1 us: local(): keys_now = cache_keys[:, kv_index, :]]
    reshape x7 -> x0, local copies, waits for them, and re-layouts: 14.2 us -> none  [the longest x1 7.01 us: local(): cache_values = value_pages.reshape(POOL * PAGE, kv_local, HD)]
  transfers between devices with their start and end apart: 7 -> 27, of which waited for: 5 -> 14; matrix products, arithmetic and copies ran while one was open for 15% -> 2% of each run, Pallas kernels for 0% -> 16%
where the time goes in v1:
time: 115 us; the launch traced here: 114 us
  Pallas kernels  38.7 us (34%)
  waiting for transfers between devices  33.6 us (29%)
  starting transfers between devices  31.9 us (28%)
  local copies, waits for them, and re-layouts  7.91 us (7%)
  other arithmetic  1.81 us (2%)
    pallas_call x15, Pallas kernels, call(): pl.pallas_call(kernel, out_shape=[jax.ShapeDtypeStruct(shape, kind) for s...  25.9 us
    ppermute x18, waiting for transfers between devices, over_branch(): return lax.ppermute(array, 'branch', pairs)  17.6 us
    ppermute x9, starting transfers between devices, over_head(): return lax.ppermute(array, 'head', pairs)  17.5 us
    ppermute x9, waiting for transfers between devices, over_head(): return lax.ppermute(array, 'head', pairs)  16 us
    ppermute x18, starting transfers between devices, over_branch(): return lax.ppermute(array, 'branch', pairs)  14.3 us
    pallas_call x6, Pallas kernels, fetch(): pl.pallas_call(functools.partial(fetch_kernel, len(arrays)), out_shape=[p...  12.8 us
    unnamed x38, local copies, waits for them, and re-layouts  7.89 us
  transfers between devices with their start and end apart: 27, of which 14 were waited for; matrix products, arithmetic and copies ran while one was open for 2% of the time, Pallas kernels for 16%

profile of v1, /device:TPU:0, one launch (start us, length us, event | category | flops | bytes accessed | tf_op | source)
XLA Modules:
  0.0 114.3 jit_solution(9521201077616110439)
XLA Ops:
  0.1 1.0 copy-done.5
  1.1 0.7 copy-done.9
  1.8 0.6 shard_map.181
  2.4 0.6 copy-done.3
  3.1 2.9 %collective-permute-start = (bf16[32,2176]{1,0:T(8,128)(2,1)S(1)}, bf16[32,2176]{1,0:T(8,128)(2,1)S(1)}, u32[]{:S(2)}, u32[]{:S(2)}) collective-permute-start(bf16[32,2176]{1,0:T(8,128)(2,1)S(1)} %get-tuple-element.42), channel_id=1, source_target_pairs={{0,8},{4,12},{8,0},{12,4},{1,9},{5,13},{9,1},{13,5},{2,10},{6,14},... | collective-permute-start | bytes 417800 | tf_op jit(solution)/shard_map/ppermute | solution.py:517
  6.1 4.1 %shard_map.182 = (bf16[2048,2048]{1,0:T(8,128)(2,1)S(1)}, bf16[2048,256]{1,0:T(8,128)(2,1)S(1)}, bf16[2048,256]{1,0:T(8,128)(2,1)S(1)}) custom-call(bf16[2048,2048]{1,0:T(8,128)(2,1)} %refs_0_.6, bf16[2048,256]{1,0:T(8,128)(2,1)} %refs_1_.3, bf16[2048,256]{1,0:T(8,128)(2,1)} %refs_2_.1, bf16[32,2176]{1,0:T(8,128)(2,1)} %copy-done.3), custom_call_target="tpu_custom_call" | custom-call | bytes 20971520 | tf_op jit(solution)/shard_map/pallas_call | solution.py:72
  10.2 0.8 dynamic-slice_convert_fusion.1
  11.1 0.9 collective-permute-done.2.refs_4_
  12.0 2.5 %shard_map.183 = (f32[64,2688]{1,0:T(8,128)S(1)}, f32[64,2688]{1,0:T(8,128)S(1)}, bf16[32,2048]{1,0:T(8,128)(2,1)S(1)}, f32[128,128]{1,0:T(8,128)S(1)}) custom-call(s32[2]{0:T(128)S(1)} %pad_add_fusion.spot.refs_0_, bf16[32,2176]{1,0:T(8,128)(2,1)S(1)} %copy-done.4, bf16[32,2176]{1,0:T(8,128)(2,1)S(1)} %collective-permute-done.refs_2_, ...), custom_call_target="tpu_custom_call" | custom-call | flops 1342177280 | tf_op jit(solution)/shard_map/pallas_call | solution.py:47
  15.1 1.7 %collective-permute-done.3.got = f32[64,2688]{1,0:T(8,128)S(1)} collective-permute-done((f32[64,2688]{1,0:T(8,128)S(1)}, f32[64,2688]{1,0:T(8,128)S(1)}, u32[]{:S(2)}, u32[]{:S(2)}) %collective-permute-start.3) | collective-permute-done | bytes 688160 | tf_op jit(solution)/shard_map/ppermute | solution.py:517
  16.9 1.8 %collective-permute-start.4 = (bf16[32,2688]{1,0:T(8,128)(2,1)S(1)}, bf16[32,2688]{1,0:T(8,128)(2,1)S(1)}, u32[]{:S(2)}, u32[]{:S(2)}) collective-permute-start(bf16[32,2688]{1,0:T(8,128)(2,1)S(1)} %get-tuple-element.53.refs_2_), channel_id=1, source_target_pairs={{0,8},{4,12},{8,0},{12,4},{1,9},{5,13},{9,1},{13,5},{2,10},{6,14},... | collective-permute-start | bytes 516104 | tf_op jit(solution)/shard_map/ppermute | solution.py:517
  19.0 0.6 shard_map.185
  19.6 4.0 %collective-permute-done.4.refs_3_ = bf16[32,2688]{1,0:T(8,128)(2,1)S(1)} collective-permute-done((bf16[32,2688]{1,0:T(8,128)(2,1)S(1)}, bf16[32,2688]{1,0:T(8,128)(2,1)S(1)}, u32[]{:S(2)}, u32[]{:S(2)}) %collective-permute-start.4) | collective-permute-done | bytes 172064 | tf_op jit(solution)/shard_map/ppermute | solution.py:517
  23.7 8.8 %shard_map.186.refs_1_.refs_2_ = bf16[32,2048]{1,0:T(8,128)(2,1)S(1)} custom-call(s32[2]{0:T(128)S(1)} %pad_add_fusion.spot.refs_0_, s32[4]{0:T(128)S(1)} %copy-done.8, f32[32,2688]{1,0:T(8,128)S(1)} %get-tuple-element.52.refs_2_, bf16[32,2688]{1,0:T(8,128)(2,1)S(1)} %collective-permute-done.4.refs_3_, bf16[1,2048]{1,0:T(2,128)(2,1)S(1)} %broadcast_in_dim.27.refs_4_, ...), custom_call_target="tpu_custom_call" | custom-call | flops 2147483648 | tf_op jit(solution)/shard_map/pallas_call | solution.py:47
  32.5 1.8 %collective-permute-start.5 = (bf16[32,2048]{1,0:T(8,128)(2,1)S(1)}, bf16[32,2048]{1,0:T(8,128)(2,1)S(1)}, u32[]{:S(2)}, u32[]{:S(2)}) collective-permute-start(bf16[32,2048]{1,0:T(8,128)(2,1)S(1)} %shard_map.186.refs_1_.refs_2_), channel_id=1, source_target_pairs={{0,8},{4,12},{8,0},{12,4},{1,9},{5,13},{9,1},{13,5},{2,10},{6,14},... | collective-permute-start | bytes 393224 | tf_op jit(solution)/shard_map/ppermute | solution.py:517
  34.3 3.2 %collective-permute-done.5.refs_3_ = bf16[32,2048]{1,0:T(8,128)(2,1)S(1)} collective-permute-done((bf16[32,2048]{1,0:T(8,128)(2,1)S(1)}, bf16[32,2048]{1,0:T(8,128)(2,1)S(1)}, u32[]{:S(2)}, u32[]{:S(2)}) %collective-permute-start.5) | collective-permute-done | bytes 131104 | tf_op jit(solution)/shard_map/ppermute | solution.py:517
  37.5 0.6 shard_map.187.refs_6_
  38.1 0.7 collective-permute-done.7.refs_5_
  38.8 2.2 %shard_map.188 = (f32[32,2048]{1,0:T(8,128)S(1)}, bf16[32,2048]{1,0:T(8,128)(2,1)S(1)}, bf16[32,2048]{1,0:T(8,128)(2,1)S(1)}, bf16[32,2048]{1,0:T(8,128)(2,1)S(1)}) custom-call(s32[2]{0:T(128)S(1)} %pad_add_fusion.spot.refs_0_, f32[128,128]{1,0:T(8,128)S(1)} %get-tuple-element.49.refs_8_.refs_1_, bf16[32,2048]{1,0:T(8,128)(2,1)S(1)} %shard_map.186.refs_1_.refs_2_, ...), custom_call_target="tpu_custom_call" | custom-call | flops 1073741824 | tf_op jit(solution)/shard_map/pallas_call | solution.py:47
  41.0 1.9 %collective-permute-start.8 = (bf16[32,2048]{1,0:T(8,128)(2,1)S(1)}, bf16[32,2048]{1,0:T(8,128)(2,1)S(1)}, u32[]{:S(2)}, u32[]{:S(2)}) collective-permute-start(bf16[32,2048]{1,0:T(8,128)(2,1)S(1)} %get-tuple-element.57), channel_id=1, source_target_pairs={{0,1},{1,2},{2,3},{3,0},{4,5},{5,6},{6,7},{7,4},{8,9},{9,10},{10,1... | collective-permute-start | bytes 393224 | tf_op jit(solution)/shard_map/ppermute | solution.py:521
  42.9 2.6 %collective-permute-start.9 = (bf16[32,2048]{1,0:T(8,128)(2,1)S(1)}, bf16[32,2048]{1,0:T(8,128)(2,1)S(1)}, u32[]{:S(2)}, u32[]{:S(2)}) collective-permute-start(bf16[32,2048]{1,0:T(8,128)(2,1)S(1)} %get-tuple-element.58), channel_id=1, source_target_pairs={{0,2},{1,3},{2,0},{3,1},{4,6},{5,7},{6,4},{7,5},{8,10},{9,11},{10,... | collective-permute-start | bytes 393224 | tf_op jit(solution)/shard_map/ppermute | solution.py:521
  45.5 1.3 %collective-permute-start.10 = (bf16[32,2048]{1,0:T(8,128)(2,1)S(1)}, bf16[32,2048]{1,0:T(8,128)(2,1)S(1)}, u32[]{:S(2)}, u32[]{:S(2)}) collective-permute-start(bf16[32,2048]{1,0:T(8,128)(2,1)S(1)} %get-tuple-element.59), channel_id=1, source_target_pairs={{0,3},{1,0},{2,1},{3,2},{4,7},{5,4},{6,5},{7,6},{8,11},{9,8},{10,9... | collective-permute-start | bytes 393224 | tf_op jit(solution)/shard_map/ppermute | solution.py:521
  46.8 0.7 dynamic-slice_convert_fusion
  47.5 1.8 %collective-permute-done.8.refs_0_ = bf16[32,2048]{1,0:T(8,128)(2,1)S(1)} collective-permute-done((bf16[32,2048]{1,0:T(8,128)(2,1)S(1)}, bf16[32,2048]{1,0:T(8,128)(2,1)S(1)}, u32[]{:S(2)}, u32[]{:S(2)}) %collective-permute-start.8) | collective-permute-done | bytes 131104 | tf_op jit(solution)/shard_map/ppermute | solution.py:521
  49.3 5.1 %collective-permute-done.9.refs_1_ = bf16[32,2048]{1,0:T(8,128)(2,1)S(1)} collective-permute-done((bf16[32,2048]{1,0:T(8,128)(2,1)S(1)}, bf16[32,2048]{1,0:T(8,128)(2,1)S(1)}, u32[]{:S(2)}, u32[]{:S(2)}) %collective-permute-start.9) | collective-permute-done | bytes 131104 | tf_op jit(solution)/shard_map/ppermute | solution.py:521
  54.6 3.3 %collective-permute-start.11 = (bf16[32,2176]{1,0:T(8,128)(2,1)S(1)}, bf16[32,2176]{1,0:T(8,128)(2,1)S(1)}, u32[]{:S(2)}, u32[]{:S(2)}) collective-permute-start(bf16[32,2176]{1,0:T(8,128)(2,1)S(1)} %get-tuple-element.61.refs_1_), channel_id=1, source_target_pairs={{0,1},{1,2},{2,3},{3,0},{4,5},{5,6},{6,7},{7,4},{8,9},{9,10},{10,1... | collective-permute-start | bytes 417800 | tf_op jit(solution)/shard_map/ppermute | solution.py:521
  58.0 1.6 %collective-permute-start.12 = (bf16[32,2176]{1,0:T(8,128)(2,1)S(1)}, bf16[32,2176]{1,0:T(8,128)(2,1)S(1)}, u32[]{:S(2)}, u32[]{:S(2)}) collective-permute-start(bf16[32,2176]{1,0:T(8,128)(2,1)S(1)} %get-tuple-element.61.refs_1_), channel_id=1, source_target_pairs={{0,2},{1,3},{2,0},{3,1},{4,6},{5,7},{6,4},{7,5},{8,10},{9,11},{10,... | collective-permute-start | bytes 417800 | tf_op jit(solution)/shard_map/ppermute | solution.py:521
  59.6 0.8 collective-permute-start.13
  60.4 1.1 shard_map.190.refs_5_.w_gate
  61.5 5.5 %copy-done = bf16[2048,3840]{1,0:T(8,128)(2,1)S(1)} copy-done((bf16[2048,3840]{1,0:T(8,128)(2,1)S(1)}, bf16[2048,3840]{1,0:T(8,128)(2,1)}, u32[]{:S(2)}) %copy-start) | copy-done | bytes 15728664
  67.0 1.1 shard_map.191.refs_6_.w_up
  68.2 3.5 %shard_map.192 = (f32[64,3968]{1,0:T(8,128)S(1)}, bf16[64,3968]{1,0:T(8,128)(2,1)S(1)}, bf16[128,2176]{1,0:T(8,128)(2,1)S(1)}) custom-call(s32[2]{0:T(128)S(1)} %pad_add_fusion.spot.refs_0_, bf16[32,2176]{1,0:T(8,128)(2,1)S(1)} %get-tuple-element.61.refs_1_, bf16[32,2176]{1,0:T(8,128)(2,1)S(1)} %collective-permute-done.11.refs_2_, ...), custom_call_target="tpu_custom_call" | custom-call | flops 2013265920 | tf_op jit(solution)/shard_map/pallas_call | solution.py:47
  71.8 2.7 %shard_map.194 = (f32[64,3840]{1,0:T(8,128)S(1)}, bf16[64,3840]{1,0:T(8,128)(2,1)S(1)}) custom-call(bf16[128,2176]{1,0:T(8,128)(2,1)S(1)} %get-tuple-element.66.ordered, bf16[2048,3840]{1,0:T(8,128)(2,1)S(1)} %shard_map.190.refs_5_.w_gate, bf16[2048,3840]{1,0:T(8,128)(2,1)S(1)} %shard_map.191.refs_6_.w_up), custom_call_target="tpu_custom_call" | custom-call | flops 2013265920 | tf_op jit(solution)/shard_map/pallas_call | solution.py:47
  75.2 1.5 %collective-permute-start.15 = (bf16[32,3968]{1,0:T(8,128)(2,1)S(1)}, bf16[32,3968]{1,0:T(8,128)(2,1)S(1)}, u32[]{:S(2)}, u32[]{:S(2)}) collective-permute-start(bf16[32,3968]{1,0:T(8,128)(2,1)S(1)} %get-tuple-element.65), channel_id=1, source_target_pairs={{0,8},{4,12},{8,0},{12,4},{1,9},{5,13},{9,1},{13,5},{2,10},{6,14},... | collective-permute-start | bytes 761864 | tf_op jit(solution)/shard_map/ppermute | solution.py:517
  76.9 1.3 %collective-permute-start.17 = (bf16[32,3840]{1,0:T(8,128)(2,1)S(1)}, bf16[32,3840]{1,0:T(8,128)(2,1)S(1)}, u32[]{:S(2)}, u32[]{:S(2)}) collective-permute-start(bf16[32,3840]{1,0:T(8,128)(2,1)S(1)} %get-tuple-element.69.refs_1_), channel_id=1, source_target_pairs={{0,8},{4,12},{8,0},{12,4},{1,9},{5,13},{9,1},{13,5},{2,10},{6,14},... | collective-permute-start | bytes 737288 | tf_op jit(solution)/shard_map/ppermute | solution.py:517
  78.2 5.5 %shard_map.196.refs_1_.refs_5_ = bf16[3840,2048]{1,0:T(8,128)(2,1)S(1)} custom-call(bf16[3840,2048]{1,0:T(8,128)(2,1)} %refs_0_.11, bf16[32,3840]{1,0:T(8,128)(2,1)S(1)} %get-tuple-element.69.refs_1_), custom_call_target="tpu_custom_call" | custom-call | bytes 31457280 | tf_op jit(solution)/shard_map/pallas_call | solution.py:72
  84.5 1.5 %collective-permute-start.21 = (bf16[32,1920]{1,0:T(8,128)(2,1)S(1)}, bf16[32,1920]{1,0:T(8,128)(2,1)S(1)}, u32[]{:S(2)}, u32[]{:S(2)}) collective-permute-start(bf16[32,1920]{1,0:T(8,128)(2,1)S(1)} %get-tuple-element.72.refs_1_), channel_id=1, source_target_pairs={{0,8},{4,12},{8,0},{12,4},{1,9},{5,13},{9,1},{13,5},{2,10},{6,14},... | collective-permute-start | bytes 368648 | tf_op jit(solution)/shard_map/ppermute | solution.py:517
  86.0 3.5 %collective-permute-done.17.refs_0_ = bf16[32,3840]{1,0:T(8,128)(2,1)S(1)} collective-permute-done((bf16[32,3840]{1,0:T(8,128)(2,1)S(1)}, bf16[32,3840]{1,0:T(8,128)(2,1)S(1)}, u32[]{:S(2)}, u32[]{:S(2)}) %collective-permute-start.17) | collective-permute-done | bytes 245792 | tf_op jit(solution)/shard_map/ppermute | solution.py:517
  89.7 1.5 %collective-permute-start.18 = (bf16[32,1920]{1,0:T(8,128)(2,1)S(1)}, bf16[32,1920]{1,0:T(8,128)(2,1)S(1)}, u32[]{:S(2)}, u32[]{:S(2)}) collective-permute-start(bf16[32,1920]{1,0:T(8,128)(2,1)S(1)} %shard_map.198.refs_1_), channel_id=1, source_target_pairs={{0,8},{4,12},{8,0},{12,4},{1,9},{5,13},{9,1},{13,5},{2,10},{6,14},... | collective-permute-start | bytes 368648 | tf_op jit(solution)/shard_map/ppermute | solution.py:517
  91.2 0.6 collective-permute-done.21.refs_2_
  92.3 2.3 %collective-permute-done.18.refs_2_ = bf16[32,1920]{1,0:T(8,128)(2,1)S(1)} collective-permute-done((bf16[32,1920]{1,0:T(8,128)(2,1)S(1)}, bf16[32,1920]{1,0:T(8,128)(2,1)S(1)}, u32[]{:S(2)}, u32[]{:S(2)}) %collective-permute-start.18) | collective-permute-done | bytes 122912 | tf_op jit(solution)/shard_map/ppermute | solution.py:517
  94.7 2.0 %shard_map.199.refs_6_ = f32[128,2048]{1,0:T(8,128)S(1)} custom-call(s32[2]{0:T(128)S(1)} %pad_add_fusion.spot.refs_0_, bf16[32,1920]{1,0:T(8,128)(2,1)S(1)} %get-tuple-element.72.refs_1_, bf16[32,1920]{1,0:T(8,128)(2,1)S(1)} %collective-permute-done.21.refs_2_, bf16[32,1920]{1,0:T(8,128)(2,1)S(1)} %collective-permute-done.22.refs_3_, ...), custom_call_target="tpu_custom_call" | custom-call | flops 1006632960 | tf_op jit(solution)/shard_map/pallas_call | solution.py:47
  96.7 2.0 %shard_map.200 = (f32[32,2048]{1,0:T(8,128)S(1)}, bf16[32,2048]{1,0:T(8,128)(2,1)S(1)}, bf16[32,2048]{1,0:T(8,128)(2,1)S(1)}, bf16[32,2048]{1,0:T(8,128)(2,1)S(1)}) custom-call(s32[2]{0:T(128)S(1)} %pad_add_fusion.spot.refs_0_, bf16[32,1920]{1,0:T(8,128)(2,1)S(1)} %shard_map.198.refs_1_, bf16[32,1920]{1,0:T(8,128)(2,1)S(1)} %collective-permute-done.18.refs_2_, ...), custom_call_target="tpu_custom_call" | custom-call | flops 1006632960 | tf_op jit(solution)/shard_map/pallas_call | solution.py:47
  98.7 3.5 %collective-permute-start.24 = (bf16[32,2048]{1,0:T(8,128)(2,1)S(1)}, bf16[32,2048]{1,0:T(8,128)(2,1)S(1)}, u32[]{:S(2)}, u32[]{:S(2)}) collective-permute-start(bf16[32,2048]{1,0:T(8,128)(2,1)S(1)} %get-tuple-element.74), channel_id=1, source_target_pairs={{0,1},{1,2},{2,3},{3,0},{4,5},{5,6},{6,7},{7,4},{8,9},{9,10},{10,1... | collective-permute-start | bytes 393224 | tf_op jit(solution)/shard_map/ppermute | solution.py:521
  102.2 2.0 %collective-permute-start.25 = (bf16[32,2048]{1,0:T(8,128)(2,1)S(1)}, bf16[32,2048]{1,0:T(8,128)(2,1)S(1)}, u32[]{:S(2)}, u32[]{:S(2)}) collective-permute-start(bf16[32,2048]{1,0:T(8,128)(2,1)S(1)} %get-tuple-element.75), channel_id=1, source_target_pairs={{0,2},{1,3},{2,0},{3,1},{4,6},{5,7},{6,4},{7,5},{8,10},{9,11},{10,... | collective-permute-start | bytes 393224 | tf_op jit(solution)/shard_map/ppermute | solution.py:521
  104.7 3.4 %collective-permute-done.24.refs_0_ = bf16[32,2048]{1,0:T(8,128)(2,1)S(1)} collective-permute-done((bf16[32,2048]{1,0:T(8,128)(2,1)S(1)}, bf16[32,2048]{1,0:T(8,128)(2,1)S(1)}, u32[]{:S(2)}, u32[]{:S(2)}) %collective-permute-start.24) | collective-permute-done | bytes 131104 | tf_op jit(solution)/shard_map/ppermute | solution.py:521
  108.1 5.4 %collective-permute-done.25.refs_1_ = bf16[32,2048]{1,0:T(8,128)(2,1)S(1)} collective-permute-done((bf16[32,2048]{1,0:T(8,128)(2,1)S(1)}, bf16[32,2048]{1,0:T(8,128)(2,1)S(1)}, u32[]{:S(2)}, u32[]{:S(2)}) %collective-permute-start.25) | collective-permute-done | bytes 131104 | tf_op jit(solution)/shard_map/ppermute | solution.py:521
  113.5 0.7 shard_map.201
  (77 shorter events, 4.3 us)
Async XLA Ops:
  0.1 1.0 copy-start.5
  1.1 0.7 copy-start.9
  2.4 0.7 copy-start.3
  3.1 9.0 %copy-start.4 = (bf16[32,2176]{1,0:T(8,128)(2,1)S(1)}, bf16[32,2176]{1,0:T(8,128)(2,1)}, u32[]{:S(2)}) copy-start(bf16[32,2176]{1,0:T(8,128)(2,1)} %copy-done.3) | copy-start | bytes 417796
  3.1 8.0 %collective-permute-start = (bf16[32,2176]{1,0:T(8,128)(2,1)S(1)}, bf16[32,2176]{1,0:T(8,128)(2,1)S(1)}, u32[]{:S(2)}, u32[]{:S(2)}) collective-permute-start(bf16[32,2176]{1,0:T(8,128)(2,1)S(1)} %get-tuple-element.42), channel_id=1, source_target_pairs={{0,8},{4,12},{8,0},{12,4},{1,9},{5,13},{9,1},{13,5},{2,10},{6,14},... | collective-permute-start | bytes 417800 | tf_op jit(solution)/shard_map/ppermute | solution.py:517
  6.0 5.1 %collective-permute-start.1 = (bf16[32,2176]{1,0:T(8,128)(2,1)S(1)}, bf16[32,2176]{1,0:T(8,128)(2,1)S(1)}, u32[]{:S(2)}, u32[]{:S(2)}) collective-permute-start(bf16[32,2176]{1,0:T(8,128)(2,1)S(1)} %get-tuple-element.43), channel_id=1, source_target_pairs={{0,4},{4,0},{8,12},{12,8},{1,5},{5,1},{9,13},{13,9},{2,6},{6,2},{1... | collective-permute-start | bytes 417800 | tf_op jit(solution)/shard_map/ppermute | solution.py:517
  6.0 6.0 %collective-permute-start.2 = (bf16[32,2176]{1,0:T(8,128)(2,1)S(1)}, bf16[32,2176]{1,0:T(8,128)(2,1)S(1)}, u32[]{:S(2)}, u32[]{:S(2)}) collective-permute-start(bf16[32,2176]{1,0:T(8,128)(2,1)S(1)} %get-tuple-element.44), channel_id=1, source_target_pairs={{0,12},{4,8},{8,4},{12,0},{1,13},{5,9},{9,5},{13,1},{2,14},{6,10},... | collective-permute-start | bytes 417800 | tf_op jit(solution)/shard_map/ppermute | solution.py:517
  6.1 9.0 %copy-start.8 = (s32[4]{0:T(128)S(1)}, s32[4]{0:T(128)}, u32[]{:S(2)}) copy-start(s32[4]{0:T(128)} %refs_1_.5) | copy-start | bytes 52
  10.2 8.7 %copy-start.10 = (bf16[2048]{0:T(1024)(128)(2,1)S(1)}, bf16[2048]{0:T(1024)(128)(2,1)}, u32[]{:S(2)}) copy-start(bf16[2048]{0:T(1024)(128)(2,1)} %param.22) | copy-start | bytes 12292
  10.2 8.7 %copy-start.11 = (bf16[256]{0:T(256)(128)(2,1)S(1)}, bf16[256]{0:T(256)(128)(2,1)}, u32[]{:S(2)}) copy-start(bf16[256]{0:T(256)(128)(2,1)} %param.24) | copy-start | bytes 1540
  10.2 8.7 %copy-start.12 = (bf16[256]{0:T(256)(128)(2,1)S(1)}, bf16[256]{0:T(256)(128)(2,1)}, u32[]{:S(2)}) copy-start(bf16[256]{0:T(256)(128)(2,1)} %param.26) | copy-start | bytes 1540
  10.2 8.8 %copy-start.1 = (bf16[64,128,256]{2,1,0:T(8,128)(2,1)S(1)}, bf16[64,128,256]{2,1,0:T(8,128)(2,1)}, u32[]{:S(2)}) copy-start(bf16[64,128,256]{2,1,0:T(8,128)(2,1)} %refs_0_.7) | copy-start | bytes 12582916
  10.2 8.8 %copy-start.2 = (bf16[64,128,256]{2,1,0:T(8,128)(2,1)S(1)}, bf16[64,128,256]{2,1,0:T(8,128)(2,1)}, u32[]{:S(2)}) copy-start(bf16[64,128,256]{2,1,0:T(8,128)(2,1)} %refs_1_.4) | copy-start | bytes 12582916
  12.0 11.6 %copy-start.6 = (f32[128,128]{1,0:T(8,128)S(1)}, f32[128,128]{1,0:T(8,128)}, u32[]{:S(2)}) copy-start(f32[128,128]{1,0:T(8,128)} %constant.24.clone.refs_10_) | copy-start | bytes 196612
  12.0 11.6 %copy-start.7 = (s32[4,32]{1,0:T(4,128)S(1)}, s32[4,32]{1,0:T(4,128)}, u32[]{:S(2)}) copy-start(s32[4,32]{1,0:T(4,128)} %refs_9_.1) | copy-start | bytes 1540
  14.6 2.3 %collective-permute-start.3 = (f32[64,2688]{1,0:T(8,128)S(1)}, f32[64,2688]{1,0:T(8,128)S(1)}, u32[]{:S(2)}, u32[]{:S(2)}) collective-permute-start(f32[64,2688]{1,0:T(8,128)S(1)} %get-tuple-element.51), channel_id=1, source_target_pairs={{0,4},{4,0},{8,12},{12,8},{1,5},{5,1},{9,13},{13,9},{2,6},{6,2},{1... | collective-permute-start | bytes 2064392 | tf_op jit(solution)/shard_map/ppermute | solution.py:517
  16.9 20.7 %slice-start.4 = ((s8[8388608]{0:T(1024)(128)(4,1)}), s8[4194304]{0:T(1024)(128)(4,1)S(1)}, s32[]{:S(2)}) async-start(s8[8388608]{0:T(1024)(128)(4,1)} %bitcast.7), calls=%async_computation.4 | async-start | bytes 8388608
  16.9 6.7 %collective-permute-start.4 = (bf16[32,2688]{1,0:T(8,128)(2,1)S(1)}, bf16[32,2688]{1,0:T(8,128)(2,1)S(1)}, u32[]{:S(2)}, u32[]{:S(2)}) collective-permute-start(bf16[32,2688]{1,0:T(8,128)(2,1)S(1)} %get-tuple-element.53.refs_2_), channel_id=1, source_target_pairs={{0,8},{4,12},{8,0},{12,4},{1,9},{5,13},{9,1},{13,5},{2,10},{6,14},... | collective-permute-start | bytes 516104 | tf_op jit(solution)/shard_map/ppermute | solution.py:517
  19.0 18.5 %slice-start.5 = ((s8[8388608]{0:T(1024)(128)(4,1)}), s8[4194304]{0:T(1024)(128)(4,1)S(1)}, s32[]{:S(2)}) async-start(s8[8388608]{0:T(1024)(128)(4,1)} %bitcast.7), calls=%async_computation.5 | async-start | bytes 8388608
  23.7 36.7 %slice-start = ((s8[15728640]{0:T(1024)(128)(4,1)}), s8[3145728]{0:T(1024)(128)(4,1)S(1)}, s32[]{:S(2)}) async-start(s8[15728640]{0:T(1024)(128)(4,1)} %bitcast.5), calls=%async_computation | async-start | bytes 6291456
  23.7 36.7 %slice-start.1 = ((s8[15728640]{0:T(1024)(128)(4,1)}), s8[4194304]{0:T(1024)(128)(4,1)S(1)}, s32[]{:S(2)}) async-start(s8[15728640]{0:T(1024)(128)(4,1)} %bitcast.5), calls=%async_computation.1 | async-start | bytes 8388608
  32.4 28.0 %slice-start.2 = ((s8[15728640]{0:T(1024)(128)(4,1)}), s8[4194304]{0:T(1024)(128)(4,1)S(1)}, s32[]{:S(2)}) async-start(s8[15728640]{0:T(1024)(128)(4,1)} %bitcast.5), calls=%async_computation.2 | async-start | bytes 8388608
  32.5 5.0 %collective-permute-start.5 = (bf16[32,2048]{1,0:T(8,128)(2,1)S(1)}, bf16[32,2048]{1,0:T(8,128)(2,1)S(1)}, u32[]{:S(2)}, u32[]{:S(2)}) collective-permute-start(bf16[32,2048]{1,0:T(8,128)(2,1)S(1)} %shard_map.186.refs_1_.refs_2_), channel_id=1, source_target_pairs={{0,8},{4,12},{8,0},{12,4},{1,9},{5,13},{9,1},{13,5},{2,10},{6,14},... | collective-permute-start | bytes 393224 | tf_op jit(solution)/shard_map/ppermute | solution.py:517
  34.3 3.8 %collective-permute-start.6 = (bf16[32,2048]{1,0:T(8,128)(2,1)S(1)}, bf16[32,2048]{1,0:T(8,128)(2,1)S(1)}, u32[]{:S(2)}, u32[]{:S(2)}) collective-permute-start(bf16[32,2048]{1,0:T(8,128)(2,1)S(1)} %shard_map.186.refs_1_.refs_2_), channel_id=1, source_target_pairs={{0,4},{4,0},{8,12},{12,8},{1,5},{5,1},{9,13},{13,9},{2,6},{6,2},{1... | collective-permute-start | bytes 393224 | tf_op jit(solution)/shard_map/ppermute | solution.py:517
  37.5 1.3 %collective-permute-start.7 = (bf16[32,2048]{1,0:T(8,128)(2,1)S(1)}, bf16[32,2048]{1,0:T(8,128)(2,1)S(1)}, u32[]{:S(2)}, u32[]{:S(2)}) collective-permute-start(bf16[32,2048]{1,0:T(8,128)(2,1)S(1)} %collective-permute-done.5.refs_3_), channel_id=1, source_target_pairs={{0,4},{4,0},{8,12},{12,8},{1,5},{5,1},{9,13},{13,9},{2,6},{6,2},{1... | collective-permute-start | bytes 393224 | tf_op jit(solution)/shard_map/ppermute | solution.py:517
  38.1 22.3 %slice-start.3 = ((s8[15728640]{0:T(1024)(128)(4,1)}), s8[4194304]{0:T(1024)(128)(4,1)S(1)}, s32[]{:S(2)}) async-start(s8[15728640]{0:T(1024)(128)(4,1)} %bitcast.5), calls=%async_computation.3 | async-start | bytes 8388608
  41.0 8.3 %collective-permute-start.8 = (bf16[32,2048]{1,0:T(8,128)(2,1)S(1)}, bf16[32,2048]{1,0:T(8,128)(2,1)S(1)}, u32[]{:S(2)}, u32[]{:S(2)}) collective-permute-start(bf16[32,2048]{1,0:T(8,128)(2,1)S(1)} %get-tuple-element.57), channel_id=1, source_target_pairs={{0,1},{1,2},{2,3},{3,0},{4,5},{5,6},{6,7},{7,4},{8,9},{9,10},{10,1... | collective-permute-start | bytes 393224 | tf_op jit(solution)/shard_map/ppermute | solution.py:521
  42.9 11.6 %collective-permute-start.9 = (bf16[32,2048]{1,0:T(8,128)(2,1)S(1)}, bf16[32,2048]{1,0:T(8,128)(2,1)S(1)}, u32[]{:S(2)}, u32[]{:S(2)}) collective-permute-start(bf16[32,2048]{1,0:T(8,128)(2,1)S(1)} %get-tuple-element.58), channel_id=1, source_target_pairs={{0,2},{1,3},{2,0},{3,1},{4,6},{5,7},{6,4},{7,5},{8,10},{9,11},{10,... | collective-permute-start | bytes 393224 | tf_op jit(solution)/shard_map/ppermute | solution.py:521
  45.5 9.0 %collective-permute-start.10 = (bf16[32,2048]{1,0:T(8,128)(2,1)S(1)}, bf16[32,2048]{1,0:T(8,128)(2,1)S(1)}, u32[]{:S(2)}, u32[]{:S(2)}) collective-permute-start(bf16[32,2048]{1,0:T(8,128)(2,1)S(1)} %get-tuple-element.59), channel_id=1, source_target_pairs={{0,3},{1,0},{2,1},{3,2},{4,7},{5,4},{6,5},{7,6},{8,11},{9,8},{10,9... | collective-permute-start | bytes 393224 | tf_op jit(solution)/shard_map/ppermute | solution.py:521
  54.6 13.4 %collective-permute-start.11 = (bf16[32,2176]{1,0:T(8,128)(2,1)S(1)}, bf16[32,2176]{1,0:T(8,128)(2,1)S(1)}, u32[]{:S(2)}, u32[]{:S(2)}) collective-permute-start(bf16[32,2176]{1,0:T(8,128)(2,1)S(1)} %get-tuple-element.61.refs_1_), channel_id=1, source_target_pairs={{0,1},{1,2},{2,3},{3,0},{4,5},{5,6},{6,7},{7,4},{8,9},{9,10},{10,1... | collective-permute-start | bytes 417800 | tf_op jit(solution)/shard_map/ppermute | solution.py:521
  58.0 10.3 %collective-permute-start.12 = (bf16[32,2176]{1,0:T(8,128)(2,1)S(1)}, bf16[32,2176]{1,0:T(8,128)(2,1)S(1)}, u32[]{:S(2)}, u32[]{:S(2)}) collective-permute-start(bf16[32,2176]{1,0:T(8,128)(2,1)S(1)} %get-tuple-element.61.refs_1_), channel_id=1, source_target_pairs={{0,2},{1,3},{2,0},{3,1},{4,6},{5,7},{6,4},{7,5},{8,10},{9,11},{10,... | collective-permute-start | bytes 417800 | tf_op jit(solution)/shard_map/ppermute | solution.py:521
  59.6 8.7 %collective-permute-start.13 = (bf16[32,2176]{1,0:T(8,128)(2,1)S(1)}, bf16[32,2176]{1,0:T(8,128)(2,1)S(1)}, u32[]{:S(2)}, u32[]{:S(2)}) collective-permute-start(bf16[32,2176]{1,0:T(8,128)(2,1)S(1)} %get-tuple-element.61.refs_1_), channel_id=1, source_target_pairs={{0,3},{1,0},{2,1},{3,2},{4,7},{5,4},{6,5},{7,6},{8,11},{9,8},{10,9... | collective-permute-start | bytes 417800 | tf_op jit(solution)/shard_map/ppermute | solution.py:521
  61.5 5.5 %copy-start = (bf16[2048,3840]{1,0:T(8,128)(2,1)S(1)}, bf16[2048,3840]{1,0:T(8,128)(2,1)}, u32[]{:S(2)}) copy-start(bf16[2048,3840]{1,0:T(8,128)(2,1)} %refs_0_.10) | copy-start | bytes 47185924
  71.7 3.3 %collective-permute-start.14 = (bf16[64,3968]{1,0:T(8,128)(2,1)S(1)}, bf16[64,3968]{1,0:T(8,128)(2,1)S(1)}, u32[]{:S(2)}, u32[]{:S(2)}) collective-permute-start(bf16[64,3968]{1,0:T(8,128)(2,1)S(1)} %get-tuple-element.63), channel_id=1, source_target_pairs={{0,4},{4,0},{8,12},{12,8},{1,5},{5,1},{9,13},{13,9},{2,6},{6,2},{1... | collective-permute-start | bytes 1523720 | tf_op jit(solution)/shard_map/ppermute | solution.py:517
  74.5 2.3 %collective-permute-start.16 = (bf16[64,3840]{1,0:T(8,128)(2,1)S(1)}, bf16[64,3840]{1,0:T(8,128)(2,1)S(1)}, u32[]{:S(2)}, u32[]{:S(2)}) collective-permute-start(bf16[64,3840]{1,0:T(8,128)(2,1)S(1)} %get-tuple-element.68), channel_id=1, source_target_pairs={{0,4},{4,0},{8,12},{12,8},{1,5},{5,1},{9,13},{13,9},{2,6},{6,2},{1... | collective-permute-start | bytes 1474568 | tf_op jit(solution)/shard_map/ppermute | solution.py:517
  75.2 9.1 %collective-permute-start.15 = (bf16[32,3968]{1,0:T(8,128)(2,1)S(1)}, bf16[32,3968]{1,0:T(8,128)(2,1)S(1)}, u32[]{:S(2)}, u32[]{:S(2)}) collective-permute-start(bf16[32,3968]{1,0:T(8,128)(2,1)S(1)} %get-tuple-element.65), channel_id=1, source_target_pairs={{0,8},{4,12},{8,0},{12,4},{1,9},{5,13},{9,1},{13,5},{2,10},{6,14},... | collective-permute-start | bytes 761864 | tf_op jit(solution)/shard_map/ppermute | solution.py:517
  76.9 12.6 %collective-permute-start.17 = (bf16[32,3840]{1,0:T(8,128)(2,1)S(1)}, bf16[32,3840]{1,0:T(8,128)(2,1)S(1)}, u32[]{:S(2)}, u32[]{:S(2)}) collective-permute-start(bf16[32,3840]{1,0:T(8,128)(2,1)S(1)} %get-tuple-element.69.refs_1_), channel_id=1, source_target_pairs={{0,8},{4,12},{8,0},{12,4},{1,9},{5,13},{9,1},{13,5},{2,10},{6,14},... | collective-permute-start | bytes 737288 | tf_op jit(solution)/shard_map/ppermute | solution.py:517
  84.5 7.3 %collective-permute-start.21 = (bf16[32,1920]{1,0:T(8,128)(2,1)S(1)}, bf16[32,1920]{1,0:T(8,128)(2,1)S(1)}, u32[]{:S(2)}, u32[]{:S(2)}) collective-permute-start(bf16[32,1920]{1,0:T(8,128)(2,1)S(1)} %get-tuple-element.72.refs_1_), channel_id=1, source_target_pairs={{0,8},{4,12},{8,0},{12,4},{1,9},{5,13},{9,1},{13,5},{2,10},{6,14},... | collective-permute-start | bytes 368648 | tf_op jit(solution)/shard_map/ppermute | solution.py:517
  89.7 4.9 %collective-permute-start.18 = (bf16[32,1920]{1,0:T(8,128)(2,1)S(1)}, bf16[32,1920]{1,0:T(8,128)(2,1)S(1)}, u32[]{:S(2)}, u32[]{:S(2)}) collective-permute-start(bf16[32,1920]{1,0:T(8,128)(2,1)S(1)} %shard_map.198.refs_1_), channel_id=1, source_target_pairs={{0,8},{4,12},{8,0},{12,4},{1,9},{5,13},{9,1},{13,5},{2,10},{6,14},... | collective-permute-start | bytes 368648 | tf_op jit(solution)/shard_map/ppermute | solution.py:517
  91.2 3.4 %collective-permute-start.22 = (bf16[32,1920]{1,0:T(8,128)(2,1)S(1)}, bf16[32,1920]{1,0:T(8,128)(2,1)S(1)}, u32[]{:S(2)}, u32[]{:S(2)}) collective-permute-start(bf16[32,1920]{1,0:T(8,128)(2,1)S(1)} %get-tuple-element.72.refs_1_), channel_id=1, source_target_pairs={{0,4},{4,0},{8,12},{12,8},{1,5},{5,1},{9,13},{13,9},{2,6},{6,2},{1... | collective-permute-start | bytes 368648 | tf_op jit(solution)/shard_map/ppermute | solution.py:517
  91.8 2.8 %collective-permute-start.23 = (bf16[32,1920]{1,0:T(8,128)(2,1)S(1)}, bf16[32,1920]{1,0:T(8,128)(2,1)S(1)}, u32[]{:S(2)}, u32[]{:S(2)}) collective-permute-start(bf16[32,1920]{1,0:T(8,128)(2,1)S(1)} %collective-permute-done.21.refs_2_), channel_id=1, source_target_pairs={{0,4},{4,0},{8,12},{12,8},{1,5},{5,1},{9,13},{13,9},{2,6},{6,2},{1... | collective-permute-start | bytes 368648 | tf_op jit(solution)/shard_map/ppermute | solution.py:517
  91.8 4.9 %collective-permute-start.19 = (bf16[32,1920]{1,0:T(8,128)(2,1)S(1)}, bf16[32,1920]{1,0:T(8,128)(2,1)S(1)}, u32[]{:S(2)}, u32[]{:S(2)}) collective-permute-start(bf16[32,1920]{1,0:T(8,128)(2,1)S(1)} %shard_map.198.refs_1_), channel_id=1, source_target_pairs={{0,4},{4,0},{8,12},{12,8},{1,5},{5,1},{9,13},{13,9},{2,6},{6,2},{1... | collective-permute-start | bytes 368648 | tf_op jit(solution)/shard_map/ppermute | solution.py:517
  94.6 2.0 %collective-permute-start.20 = (bf16[32,1920]{1,0:T(8,128)(2,1)S(1)}, bf16[32,1920]{1,0:T(8,128)(2,1)S(1)}, u32[]{:S(2)}, u32[]{:S(2)}) collective-permute-start(bf16[32,1920]{1,0:T(8,128)(2,1)S(1)} %collective-permute-done.18.refs_2_), channel_id=1, source_target_pairs={{0,4},{4,0},{8,12},{12,8},{1,5},{5,1},{9,13},{13,9},{2,6},{6,2},{1... | collective-permute-start | bytes 368648 | tf_op jit(solution)/shard_map/ppermute | solution.py:517
  98.7 9.4 %collective-permute-start.24 = (bf16[32,2048]{1,0:T(8,128)(2,1)S(1)}, bf16[32,2048]{1,0:T(8,128)(2,1)S(1)}, u32[]{:S(2)}, u32[]{:S(2)}) collective-permute-start(bf16[32,2048]{1,0:T(8,128)(2,1)S(1)} %get-tuple-element.74), channel_id=1, source_target_pairs={{0,1},{1,2},{2,3},{3,0},{4,5},{5,6},{6,7},{7,4},{8,9},{9,10},{10,1... | collective-permute-start | bytes 393224 | tf_op jit(solution)/shard_map/ppermute | solution.py:521
  102.2 11.3 %collective-permute-start.25 = (bf16[32,2048]{1,0:T(8,128)(2,1)S(1)}, bf16[32,2048]{1,0:T(8,128)(2,1)S(1)}, u32[]{:S(2)}, u32[]{:S(2)}) collective-permute-start(bf16[32,2048]{1,0:T(8,128)(2,1)S(1)} %get-tuple-element.75), channel_id=1, source_target_pairs={{0,2},{1,3},{2,0},{3,1},{4,6},{5,7},{6,4},{7,5},{8,10},{9,11},{10,... | collective-permute-start | bytes 393224 | tf_op jit(solution)/shard_map/ppermute | solution.py:521
  104.2 9.3 %collective-permute-start.26 = (bf16[32,2048]{1,0:T(8,128)(2,1)S(1)}, bf16[32,2048]{1,0:T(8,128)(2,1)S(1)}, u32[]{:S(2)}, u32[]{:S(2)}) collective-permute-start(bf16[32,2048]{1,0:T(8,128)(2,1)S(1)} %get-tuple-element.76), channel_id=1, source_target_pairs={{0,3},{1,0},{2,1},{3,2},{4,7},{5,4},{6,5},{7,6},{8,11},{9,8},{10,9... | collective-permute-start | bytes 393224 | tf_op jit(solution)/shard_map/ppermute | solution.py:521

commit v2 on v1

--- a/solution.py
+++ b/solution.py
@@ -24,6 +24,7 @@
 FAR = -1e30
 MIB = 1024 * 1024
 SPARE = 10 * MIB
+SEND_LIMIT = 63 * MIB
 
 F32 = jnp.float32
 BF16 = jnp.bfloat16
@@ -43,10 +44,13 @@
 SPACES = {"vmem": pltpu.VMEM, "hbm": pltpu.HBM, "any": pl.ANY, "smem": pltpu.SMEM}
 
 
-def call(kernel, outs, in_spaces, scratch, *args, limit=SPARE, flops=0, moved=0):
+def call(kernel, outs, in_spaces, scratch, *args, limit=SPARE, flops=0, moved=0, near=False):
     return pl.pallas_call(
         kernel,
-        out_shape=[jax.ShapeDtypeStruct(shape, kind) for shape, kind in outs],
+        out_shape=[
+            pltpu.VMEM(shape, kind) if near else jax.ShapeDtypeStruct(shape, kind)
+            for shape, kind in outs
+        ],
         in_specs=[pl.BlockSpec(memory_space=SPACES[space]) for space in in_spaces],
         out_specs=[pl.BlockSpec(memory_space=pltpu.VMEM) for _ in outs],
         scratch_shapes=scratch,
@@ -152,18 +156,25 @@
     return jnp.dot(left, right, preferred_element_type=F32)
 
 
-def send_kernel(chips, spot, hidden, parents, *blocks):
-    place = Place(spot, chips, 1)
+def send_kernel(chips, hidden, parents, *refs):
+    blocks, (listed, sems) = refs[:-2], refs[-2:]
+    place = Place((lax.axis_index("branch"), 0), chips, 1)
     length, width = hidden.shape[0], blocks[0].shape[1] - EXT
+    copies = [pltpu.make_async_copy(parents, listed, sems.at[0])]
+    for at, (ref, device) in enumerate(zip(blocks, place.targets())):
+        source = hidden.at[:, pl.ds(pl.multiple_of(device * width, width), width)]
+        copies.append(pltpu.make_async_copy(source, ref.at[:, :width], sems.at[at + 1]))
+    for copy in copies:
+        copy.start()
+    copies[0].wait()
     row_at = lax.broadcasted_iota(jnp.int32, (length, length), 0)
     col_at = lax.broadcasted_iota(jnp.int32, (length, length), 1)
-    turned = jnp.sum(
-        jnp.where(row_at == col_at, parents[...].astype(F32), 0.0), 1, keepdims=True
-    )
+    turned = jnp.sum(jnp.where(row_at == col_at, listed[...].astype(F32), 0.0), 1, keepdims=True)
     mark = jnp.broadcast_to(turned, (length, EXT)).astype(BF16)
-    for ref, device in zip(blocks, place.targets()):
-        ref[:, :width] = hidden[:, pl.ds(pl.multiple_of(device * width, width), width)]
+    for ref in blocks:
         ref[:, width:] = mark
+    for copy in copies[1:]:
+        copy.wait()
 
 
 def qkv_kernel(slots, chips, head_count, width, *refs):
@@ -216,7 +227,7 @@
     spot, path_pages, mine = refs[:3]
     received = refs[3 : 3 + received_n]
     bq, bk, bv, waves, codes, page_table, turn, kbuf, vbuf = refs[3 + received_n : 12 + received_n]
-    out, scores, mixed, sums = refs[12 + received_n :]
+    out, scores, mixed, page_marks = refs[12 + received_n :]
     slots = mine.shape[0]
     squares = mine[:, -EXT:][:, :1]
     total = mine[:, :-EXT]
@@ -244,7 +255,6 @@
         )
         owned = jnp.max(live.astype(F32), 1, keepdims=True)
         page_mark = jnp.where(lane == local_parent, (1.0 - owned) * FAR, page_mark)
-    page_marks = page_mark.astype(BF16).astype(F32)
 
     def stacked(first, count):
         return jnp.concatenate(
@@ -267,61 +277,58 @@
     chunk = chunk_pages * PAGE
     chunks = POOL // chunk_pages
     marks = jnp.concatenate([slot_mark.astype(BF16)] * group_size, 0)
-    sums[:POOL, :] = page_marks
+    page_marks[...] = page_mark
     for kv_at in range(kv_local):
         query_now = queries[kv_at * rows : (kv_at + 1) * rows]
         left = jnp.concatenate([turned[kv_at * rows : (kv_at + 1) * rows], marks], 1)
         key_now = jnp.concatenate([new_keys[kv_at * slots : (kv_at + 1) * slots]] * group_size, 0)
         own_score = jnp.sum(query_now * key_now, 1, keepdims=True)
+        own_row = jnp.broadcast_to(own_score, (rows, HD)).T[:1]
         span = slice(kv_at * HD, (kv_at + 1) * HD)
-        if kv_at > 0:
-            sums[:POOL, :] = page_marks
 
         def first_pass(at, best):
             pages = pl.ds(pl.multiple_of(at * chunk_pages, chunk_pages), chunk_pages)
             page_keys = kbuf[pages, :, span].reshape(chunk, HD)
             mark = jnp.broadcast_to(
-                sums[pages, :][:, None, :], (chunk_pages, PAGE, EXT)
+                page_marks[pages, :][:, None, :], (chunk_pages, PAGE, EXT)
             ).reshape(chunk, EXT)
             now = lax.dot_general(
+                jnp.concatenate([page_keys, mark.astype(BF16)], 1),
                 left,
-                jnp.concatenate([page_keys, mark.astype(BF16)], 1),
                 (((1,), (1,)), ((), ())),
                 preferred_element_type=F32,
             )
             scores[at] = now
-            for page in range(chunk_pages):
-                best = jnp.maximum(best, now[:, page * PAGE : (page + 1) * PAGE])
-            return best
+            return jnp.maximum(best, jnp.max(now.reshape(chunk // 8, 8, rows), 0))
 
         best = lax.fori_loop(
-            0, chunks, first_pass, jnp.full((rows, PAGE), -jnp.inf, F32), unroll=unroll
+            0, chunks, first_pass, jnp.full((8, rows), -jnp.inf, F32), unroll=unroll
         )
-        top = jnp.maximum(jnp.max(best, 1, keepdims=True), own_score)
+        top = jnp.maximum(jnp.max(best, 0, keepdims=True), own_row)
         top_rate = top * rate
-        sums[...] = jnp.zeros_like(sums)
         mixed[...] = jnp.zeros_like(mixed)
 
-        def second_pass(at, carry):
+        def second_pass(at, sums):
             pages = pl.ds(pl.multiple_of(at * chunk_pages, chunk_pages), chunk_pages)
             weights = jnp.exp2(scores[at] * rate - top_rate)
-            part = weights[:, :PAGE]
-            for page in range(1, chunk_pages):
-                part = part + weights[:, page * PAGE : (page + 1) * PAGE]
-            sums[:rows, :] += part
             page_values = vbuf[pages, :, span].reshape(chunk, HD)
-            mixed[...] += dot32(weights.astype(BF16), page_values)
-            return carry
-
-        lax.fori_loop(0, chunks, second_pass, 0, unroll=unroll)
-        own = jnp.exp2(own_score * rate - top_rate)
-        whole = jnp.sum(sums[:rows, :], 1, keepdims=True) + own
+            mixed[...] += lax.dot_general(
+                page_values,
+                weights.astype(BF16),
+                (((0,), (0,)), ((), ())),
+                preferred_element_type=F32,
+            )
+            return sums + jnp.sum(weights.reshape(chunk // 8, 8, rows), 0)
+
+        sums = lax.fori_loop(0, chunks, second_pass, jnp.zeros((8, rows), F32), unroll=unroll)
+        own = jnp.exp2(own_row * rate - top_rate)
+        whole = jnp.sum(sums, 0, keepdims=True) + own
         unturned = jnp.dot(
-            mixed[...], rotation, precision=lax.Precision.HIGHEST, preferred_element_type=F32
+            rotation, mixed[...], precision=lax.Precision.HIGHEST, preferred_element_type=F32
         )
         value_at = (heads + kv_local + kv_at) * HD
         value_now = jnp.concatenate([packed[:, value_at : value_at + HD]] * group_size, 0)
-        result = ((unturned + own * value_now) / whole).astype(BF16)
+        result = ((unturned + own * value_now.T) / whole).T.astype(BF16)
         for head in range(group_size):
             at = (kv_at * group_size + head) * HD
             out[:, at : at + HD] = result[head * slots : (head + 1) * slots]
@@ -528,11 +535,12 @@
     outgoing = call(
         functools.partial(send_kernel, chips),
         [((local_rows, model_cols + EXT), BF16)] * branch_count,
-        ["smem", "vmem", "vmem"],
-        [],
-        spot,
+        ["hbm", "hbm"],
+        [pltpu.VMEM((1, local_rows), jnp.int32), pltpu.SemaphoreType.DMA((branch_count + 1,))],
         hidden_in,
         parent_index[None],
+        limit=SEND_LIMIT,
+        near=True,
     )
     hidden_blocks = [outgoing[0]]
     for block, (chip, core) in zip(outgoing[1:], steps[1:]):
@@ -573,19 +581,17 @@
     angle = (path_pages.astype(F32) * PAGE)[:, None] * freqs
     cosine, sine = jnp.cos(angle), jnp.sin(angle)
     waves = jnp.concatenate([cosine, cosine, -sine, sine], 1)
-    chunk_pages, unroll = 8, 4
     rows = group_size * slots
-    if rows > 512:
-        unroll = 1
+    chunk_pages, unroll = (16, 2) if rows <= 512 else (4, 1)
     score_bytes = 4 * rows * POOL * PAGE
     (attention,) = call(
         functools.partial(attend_kernel, kv_local, group_size, chunk_pages, unroll, chips - 1),
         [((slots, query_cols), BF16)],
         ["smem"] * 2 + ["vmem"] * (chips + 9),
         [
-            pltpu.VMEM((POOL // chunk_pages, rows, chunk_pages * PAGE), F32),
-            pltpu.VMEM((rows, HD), F32),
-            pltpu.VMEM((max(rows, POOL), HD), F32),
+            pltpu.VMEM((POOL // chunk_pages, chunk_pages * PAGE, rows), F32),
+            pltpu.VMEM((HD, rows), F32),
+            pltpu.VMEM((POOL, EXT), F32),
         ],
         spot,
         path_pages,

time: 115 us -> 113 us (0.983)
  local copies, waits for them, and re-layouts: 7.91 us -> 6.22 us
    unnamed x38 -> x34, local copies, waits for them, and re-layouts: 7.89 us -> 6.2 us
where the time goes in v2:
time: 113 us; the launch traced here: 112 us
  Pallas kernels  38.7 us (34%)
  waiting for transfers between devices  33.4 us (30%)
  starting transfers between devices  32 us (28%)
  local copies, waits for them, and re-layouts  6.22 us (6%)
  other arithmetic  1.81 us (2%)
    pallas_call x15, Pallas kernels, call(): pl.pallas_call(kernel, out_shape=[pltpu.VMEM(shape, kind) if near else ja...  25.9 us
    ppermute x9, starting transfers between devices, over_head(): return lax.ppermute(array, 'head', pairs)  17.5 us
    ppermute x18, waiting for transfers between devices, over_branch(): return lax.ppermute(array, 'branch', pairs)  17.5 us
    ppermute x9, waiting for transfers between devices, over_head(): return lax.ppermute(array, 'head', pairs)  16 us
    ppermute x18, starting transfers between devices, over_branch(): return lax.ppermute(array, 'branch', pairs)  14.4 us
    pallas_call x6, Pallas kernels, fetch(): pl.pallas_call(functools.partial(fetch_kernel, len(arrays)), out_shape=[p...  12.8 us
    unnamed x34, local copies, waits for them, and re-layouts  6.2 us
  transfers between devices with their start and end apart: 27, of which 14 were waited for; matrix products, arithmetic and copies ran while one was open for 2% of the time, Pallas kernels for 16%

profile of v2, /device:TPU:0, one launch (start us, length us, event | category | flops | bytes accessed | tf_op | source)
XLA Modules:
  0.0 112.5 jit_solution(10653413087926008924)
XLA Ops:
  0.0 1.2 %shard_map.181 = (bf16[32,2176]{1,0:T(8,128)(2,1)S(1)}, bf16[32,2176]{1,0:T(8,128)(2,1)S(1)}, bf16[32,2176]{1,0:T(8,128)(2,1)S(1)}, bf16[32,2176]{1,0:T(8,128)(2,1)S(1)}) custom-call(bf16[32,8192]{1,0:T(8,128)(2,1)} %hidden.1, s32[1,32]{1,0:T(1,128)} %bitcast.11), custom_call_target="tpu_custom_call" | custom-call | tf_op jit(solution)/shard_map/pallas_call | solution.py:48
  1.2 0.7 copy-done.3
  1.8 2.9 %collective-permute-start = (bf16[32,2176]{1,0:T(8,128)(2,1)S(1)}, bf16[32,2176]{1,0:T(8,128)(2,1)S(1)}, u32[]{:S(2)}, u32[]{:S(2)}) collective-permute-start(bf16[32,2176]{1,0:T(8,128)(2,1)S(1)} %get-tuple-element.42), channel_id=1, source_target_pairs={{0,8},{4,12},{8,0},{12,4},{1,9},{5,13},{9,1},{13,5},{2,10},{6,14},... | collective-permute-start | bytes 417800 | tf_op jit(solution)/shard_map/ppermute | solution.py:524
  5.0 4.1 %shard_map.182 = (bf16[2048,2048]{1,0:T(8,128)(2,1)S(1)}, bf16[2048,256]{1,0:T(8,128)(2,1)S(1)}, bf16[2048,256]{1,0:T(8,128)(2,1)S(1)}) custom-call(bf16[2048,2048]{1,0:T(8,128)(2,1)} %refs_0_.6, bf16[2048,256]{1,0:T(8,128)(2,1)} %refs_1_.3, bf16[2048,256]{1,0:T(8,128)(2,1)} %refs_2_.1, bf16[32,2176]{1,0:T(8,128)(2,1)} %copy-done.3), custom_call_target="tpu_custom_call" | custom-call | bytes 20971520 | tf_op jit(solution)/shard_map/pallas_call | solution.py:76
  9.1 0.8 dynamic-slice_convert_fusion.1
  9.9 0.9 collective-permute-done.2.refs_4_
  10.8 2.5 %shard_map.183 = (f32[64,2688]{1,0:T(8,128)S(1)}, f32[64,2688]{1,0:T(8,128)S(1)}, bf16[32,2048]{1,0:T(8,128)(2,1)S(1)}, f32[128,128]{1,0:T(8,128)S(1)}) custom-call(s32[2]{0:T(128)S(1)} %pad_add_fusion.refs_0_, bf16[32,2176]{1,0:T(8,128)(2,1)S(1)} %copy-done.4, bf16[32,2176]{1,0:T(8,128)(2,1)S(1)} %collective-permute-done.refs_2_, ...), custom_call_target="tpu_custom_call" | custom-call | flops 1342177280 | tf_op jit(solution)/shard_map/pallas_call | solution.py:48
  13.9 1.7 %collective-permute-done.3.got = f32[64,2688]{1,0:T(8,128)S(1)} collective-permute-done((f32[64,2688]{1,0:T(8,128)S(1)}, f32[64,2688]{1,0:T(8,128)S(1)}, u32[]{:S(2)}, u32[]{:S(2)}) %collective-permute-start.3) | collective-permute-done | bytes 688160 | tf_op jit(solution)/shard_map/ppermute | solution.py:524
  15.7 1.8 %collective-permute-start.4 = (bf16[32,2688]{1,0:T(8,128)(2,1)S(1)}, bf16[32,2688]{1,0:T(8,128)(2,1)S(1)}, u32[]{:S(2)}, u32[]{:S(2)}) collective-permute-start(bf16[32,2688]{1,0:T(8,128)(2,1)S(1)} %get-tuple-element.53.refs_2_), channel_id=1, source_target_pairs={{0,8},{4,12},{8,0},{12,4},{1,9},{5,13},{9,1},{13,5},{2,10},{6,14},... | collective-permute-start | bytes 516104 | tf_op jit(solution)/shard_map/ppermute | solution.py:524
  17.8 0.6 shard_map.185
  18.4 4.0 %collective-permute-done.4.refs_3_ = bf16[32,2688]{1,0:T(8,128)(2,1)S(1)} collective-permute-done((bf16[32,2688]{1,0:T(8,128)(2,1)S(1)}, bf16[32,2688]{1,0:T(8,128)(2,1)S(1)}, u32[]{:S(2)}, u32[]{:S(2)}) %collective-permute-start.4) | collective-permute-done | bytes 172064 | tf_op jit(solution)/shard_map/ppermute | solution.py:524
  22.4 8.2 %shard_map.186.refs_1_.refs_2_ = bf16[32,2048]{1,0:T(8,128)(2,1)S(1)} custom-call(s32[2]{0:T(128)S(1)} %pad_add_fusion.refs_0_, s32[4]{0:T(128)S(1)} %copy-done.7, f32[32,2688]{1,0:T(8,128)S(1)} %get-tuple-element.52.refs_2_, bf16[32,2688]{1,0:T(8,128)(2,1)S(1)} %collective-permute-done.4.refs_3_, bf16[1,2048]{1,0:T(2,128)(2,1)S(1)} %broadcast_in_dim.27.refs_4_, ...), custom_call_target="tpu_custom_call" | custom-call | flops 2147483648 | tf_op jit(solution)/shard_map/pallas_call | solution.py:48
  30.7 1.8 %collective-permute-start.5 = (bf16[32,2048]{1,0:T(8,128)(2,1)S(1)}, bf16[32,2048]{1,0:T(8,128)(2,1)S(1)}, u32[]{:S(2)}, u32[]{:S(2)}) collective-permute-start(bf16[32,2048]{1,0:T(8,128)(2,1)S(1)} %shard_map.186.refs_1_.refs_2_), channel_id=1, source_target_pairs={{0,8},{4,12},{8,0},{12,4},{1,9},{5,13},{9,1},{13,5},{2,10},{6,14},... | collective-permute-start | bytes 393224 | tf_op jit(solution)/shard_map/ppermute | solution.py:524
  32.5 3.2 %collective-permute-done.5.refs_3_ = bf16[32,2048]{1,0:T(8,128)(2,1)S(1)} collective-permute-done((bf16[32,2048]{1,0:T(8,128)(2,1)S(1)}, bf16[32,2048]{1,0:T(8,128)(2,1)S(1)}, u32[]{:S(2)}, u32[]{:S(2)}) %collective-permute-start.5) | collective-permute-done | bytes 131104 | tf_op jit(solution)/shard_map/ppermute | solution.py:524
  35.7 0.6 shard_map.187.refs_6_
  36.3 0.7 collective-permute-done.7.refs_5_
  37.1 2.2 %shard_map.188 = (f32[32,2048]{1,0:T(8,128)S(1)}, bf16[32,2048]{1,0:T(8,128)(2,1)S(1)}, bf16[32,2048]{1,0:T(8,128)(2,1)S(1)}, bf16[32,2048]{1,0:T(8,128)(2,1)S(1)}) custom-call(s32[2]{0:T(128)S(1)} %pad_add_fusion.refs_0_, f32[128,128]{1,0:T(8,128)S(1)} %get-tuple-element.49.refs_8_.refs_1_, bf16[32,2048]{1,0:T(8,128)(2,1)S(1)} %shard_map.186.refs_1_.refs_2_, ...), custom_call_target="tpu_custom_call" | custom-call | flops 1073741824 | tf_op jit(solution)/shard_map/pallas_call | solution.py:48
  39.2 1.9 %collective-permute-start.8 = (bf16[32,2048]{1,0:T(8,128)(2,1)S(1)}, bf16[32,2048]{1,0:T(8,128)(2,1)S(1)}, u32[]{:S(2)}, u32[]{:S(2)}) collective-permute-start(bf16[32,2048]{1,0:T(8,128)(2,1)S(1)} %get-tuple-element.57), channel_id=1, source_target_pairs={{0,1},{1,2},{2,3},{3,0},{4,5},{5,6},{6,7},{7,4},{8,9},{9,10},{10,1... | collective-permute-start | bytes 393224 | tf_op jit(solution)/shard_map/ppermute | solution.py:528
  41.1 2.6 %collective-permute-start.9 = (bf16[32,2048]{1,0:T(8,128)(2,1)S(1)}, bf16[32,2048]{1,0:T(8,128)(2,1)S(1)}, u32[]{:S(2)}, u32[]{:S(2)}) collective-permute-start(bf16[32,2048]{1,0:T(8,128)(2,1)S(1)} %get-tuple-element.58), channel_id=1, source_target_pairs={{0,2},{1,3},{2,0},{3,1},{4,6},{5,7},{6,4},{7,5},{8,10},{9,11},{10,... | collective-permute-start | bytes 393224 | tf_op jit(solution)/shard_map/ppermute | solution.py:528
  43.7 1.3 %collective-permute-start.10 = (bf16[32,2048]{1,0:T(8,128)(2,1)S(1)}, bf16[32,2048]{1,0:T(8,128)(2,1)S(1)}, u32[]{:S(2)}, u32[]{:S(2)}) collective-permute-start(bf16[32,2048]{1,0:T(8,128)(2,1)S(1)} %get-tuple-element.59), channel_id=1, source_target_pairs={{0,3},{1,0},{2,1},{3,2},{4,7},{5,4},{6,5},{7,6},{8,11},{9,8},{10,9... | collective-permute-start | bytes 393224 | tf_op jit(solution)/shard_map/ppermute | solution.py:528
  45.1 0.7 dynamic-slice_convert_fusion
  45.7 1.8 %collective-permute-done.8.refs_0_ = bf16[32,2048]{1,0:T(8,128)(2,1)S(1)} collective-permute-done((bf16[32,2048]{1,0:T(8,128)(2,1)S(1)}, bf16[32,2048]{1,0:T(8,128)(2,1)S(1)}, u32[]{:S(2)}, u32[]{:S(2)}) %collective-permute-start.8) | collective-permute-done | bytes 131104 | tf_op jit(solution)/shard_map/ppermute | solution.py:528
  47.5 5.1 %collective-permute-done.9.refs_1_ = bf16[32,2048]{1,0:T(8,128)(2,1)S(1)} collective-permute-done((bf16[32,2048]{1,0:T(8,128)(2,1)S(1)}, bf16[32,2048]{1,0:T(8,128)(2,1)S(1)}, u32[]{:S(2)}, u32[]{:S(2)}) %collective-permute-start.9) | collective-permute-done | bytes 131104 | tf_op jit(solution)/shard_map/ppermute | solution.py:528
  52.8 3.3 %collective-permute-start.11 = (bf16[32,2176]{1,0:T(8,128)(2,1)S(1)}, bf16[32,2176]{1,0:T(8,128)(2,1)S(1)}, u32[]{:S(2)}, u32[]{:S(2)}) collective-permute-start(bf16[32,2176]{1,0:T(8,128)(2,1)S(1)} %get-tuple-element.61.refs_1_), channel_id=1, source_target_pairs={{0,1},{1,2},{2,3},{3,0},{4,5},{5,6},{6,7},{7,4},{8,9},{9,10},{10,1... | collective-permute-start | bytes 417800 | tf_op jit(solution)/shard_map/ppermute | solution.py:528
  56.2 1.6 %collective-permute-start.12 = (bf16[32,2176]{1,0:T(8,128)(2,1)S(1)}, bf16[32,2176]{1,0:T(8,128)(2,1)S(1)}, u32[]{:S(2)}, u32[]{:S(2)}) collective-permute-start(bf16[32,2176]{1,0:T(8,128)(2,1)S(1)} %get-tuple-element.61.refs_1_), channel_id=1, source_target_pairs={{0,2},{1,3},{2,0},{3,1},{4,6},{5,7},{6,4},{7,5},{8,10},{9,11},{10,... | collective-permute-start | bytes 417800 | tf_op jit(solution)/shard_map/ppermute | solution.py:528
  57.8 0.8 collective-permute-start.13
  58.6 1.1 shard_map.190.refs_5_.w_gate
  59.7 5.5 %copy-done = bf16[2048,3840]{1,0:T(8,128)(2,1)S(1)} copy-done((bf16[2048,3840]{1,0:T(8,128)(2,1)S(1)}, bf16[2048,3840]{1,0:T(8,128)(2,1)}, u32[]{:S(2)}) %copy-start) | copy-done | bytes 15728664
  65.2 1.1 shard_map.191.refs_6_.w_up
  66.5 3.5 %shard_map.192 = (f32[64,3968]{1,0:T(8,128)S(1)}, bf16[64,3968]{1,0:T(8,128)(2,1)S(1)}, bf16[128,2176]{1,0:T(8,128)(2,1)S(1)}) custom-call(s32[2]{0:T(128)S(1)} %pad_add_fusion.refs_0_, bf16[32,2176]{1,0:T(8,128)(2,1)S(1)} %get-tuple-element.61.refs_1_, bf16[32,2176]{1,0:T(8,128)(2,1)S(1)} %collective-permute-done.11.refs_2_, ...), custom_call_target="tpu_custom_call" | custom-call | flops 2013265920 | tf_op jit(solution)/shard_map/pallas_call | solution.py:48
  70.0 2.7 %shard_map.194 = (f32[64,3840]{1,0:T(8,128)S(1)}, bf16[64,3840]{1,0:T(8,128)(2,1)S(1)}) custom-call(bf16[128,2176]{1,0:T(8,128)(2,1)S(1)} %get-tuple-element.66.ordered, bf16[2048,3840]{1,0:T(8,128)(2,1)S(1)} %shard_map.190.refs_5_.w_gate, bf16[2048,3840]{1,0:T(8,128)(2,1)S(1)} %shard_map.191.refs_6_.w_up), custom_call_target="tpu_custom_call" | custom-call | flops 2013265920 | tf_op jit(solution)/shard_map/pallas_call | solution.py:48
  72.7 0.6 collective-permute-start.16
  73.4 1.6 %collective-permute-start.15 = (bf16[32,3968]{1,0:T(8,128)(2,1)S(1)}, bf16[32,3968]{1,0:T(8,128)(2,1)S(1)}, u32[]{:S(2)}, u32[]{:S(2)}) collective-permute-start(bf16[32,3968]{1,0:T(8,128)(2,1)S(1)} %get-tuple-element.65), channel_id=1, source_target_pairs={{0,8},{4,12},{8,0},{12,4},{1,9},{5,13},{9,1},{13,5},{2,10},{6,14},... | collective-permute-start | bytes 761864 | tf_op jit(solution)/shard_map/ppermute | solution.py:524
  75.1 1.3 %collective-permute-start.17 = (bf16[32,3840]{1,0:T(8,128)(2,1)S(1)}, bf16[32,3840]{1,0:T(8,128)(2,1)S(1)}, u32[]{:S(2)}, u32[]{:S(2)}) collective-permute-start(bf16[32,3840]{1,0:T(8,128)(2,1)S(1)} %get-tuple-element.69.refs_1_), channel_id=1, source_target_pairs={{0,8},{4,12},{8,0},{12,4},{1,9},{5,13},{9,1},{13,5},{2,10},{6,14},... | collective-permute-start | bytes 737288 | tf_op jit(solution)/shard_map/ppermute | solution.py:524
  76.5 5.5 %shard_map.196.refs_1_.refs_5_ = bf16[3840,2048]{1,0:T(8,128)(2,1)S(1)} custom-call(bf16[3840,2048]{1,0:T(8,128)(2,1)} %refs_0_.11, bf16[32,3840]{1,0:T(8,128)(2,1)S(1)} %get-tuple-element.69.refs_1_), custom_call_target="tpu_custom_call" | custom-call | bytes 31457280 | tf_op jit(solution)/shard_map/pallas_call | solution.py:76
  82.0 0.5 collective-permute-done.15.refs_0_
  82.7 1.6 %collective-permute-start.21 = (bf16[32,1920]{1,0:T(8,128)(2,1)S(1)}, bf16[32,1920]{1,0:T(8,128)(2,1)S(1)}, u32[]{:S(2)}, u32[]{:S(2)}) collective-permute-start(bf16[32,1920]{1,0:T(8,128)(2,1)S(1)} %get-tuple-element.72.refs_1_), channel_id=1, source_target_pairs={{0,8},{4,12},{8,0},{12,4},{1,9},{5,13},{9,1},{13,5},{2,10},{6,14},... | collective-permute-start | bytes 368648 | tf_op jit(solution)/shard_map/ppermute | solution.py:524
  84.3 3.5 %collective-permute-done.17.refs_0_ = bf16[32,3840]{1,0:T(8,128)(2,1)S(1)} collective-permute-done((bf16[32,3840]{1,0:T(8,128)(2,1)S(1)}, bf16[32,3840]{1,0:T(8,128)(2,1)S(1)}, u32[]{:S(2)}, u32[]{:S(2)}) %collective-permute-start.17) | collective-permute-done | bytes 245792 | tf_op jit(solution)/shard_map/ppermute | solution.py:524
  87.9 1.6 %collective-permute-start.18 = (bf16[32,1920]{1,0:T(8,128)(2,1)S(1)}, bf16[32,1920]{1,0:T(8,128)(2,1)S(1)}, u32[]{:S(2)}, u32[]{:S(2)}) collective-permute-start(bf16[32,1920]{1,0:T(8,128)(2,1)S(1)} %shard_map.198.refs_1_), channel_id=1, source_target_pairs={{0,8},{4,12},{8,0},{12,4},{1,9},{5,13},{9,1},{13,5},{2,10},{6,14},... | collective-permute-start | bytes 368648 | tf_op jit(solution)/shard_map/ppermute | solution.py:524
  89.5 0.5 collective-permute-done.21.refs_2_
  90.5 2.3 %collective-permute-done.18.refs_2_ = bf16[32,1920]{1,0:T(8,128)(2,1)S(1)} collective-permute-done((bf16[32,1920]{1,0:T(8,128)(2,1)S(1)}, bf16[32,1920]{1,0:T(8,128)(2,1)S(1)}, u32[]{:S(2)}, u32[]{:S(2)}) %collective-permute-start.18) | collective-permute-done | bytes 122912 | tf_op jit(solution)/shard_map/ppermute | solution.py:524
  92.9 2.0 %shard_map.199.refs_6_ = f32[128,2048]{1,0:T(8,128)S(1)} custom-call(s32[2]{0:T(128)S(1)} %pad_add_fusion.refs_0_, bf16[32,1920]{1,0:T(8,128)(2,1)S(1)} %get-tuple-element.72.refs_1_, bf16[32,1920]{1,0:T(8,128)(2,1)S(1)} %collective-permute-done.21.refs_2_, bf16[32,1920]{1,0:T(8,128)(2,1)S(1)} %collective-permute-done.22.refs_3_, ...), custom_call_target="tpu_custom_call" | custom-call | flops 1006632960 | tf_op jit(solution)/shard_map/pallas_call | solution.py:48
  94.9 2.0 %shard_map.200 = (f32[32,2048]{1,0:T(8,128)S(1)}, bf16[32,2048]{1,0:T(8,128)(2,1)S(1)}, bf16[32,2048]{1,0:T(8,128)(2,1)S(1)}, bf16[32,2048]{1,0:T(8,128)(2,1)S(1)}) custom-call(s32[2]{0:T(128)S(1)} %pad_add_fusion.refs_0_, bf16[32,1920]{1,0:T(8,128)(2,1)S(1)} %shard_map.198.refs_1_, bf16[32,1920]{1,0:T(8,128)(2,1)S(1)} %collective-permute-done.18.refs_2_, ...), custom_call_target="tpu_custom_call" | custom-call | flops 1006632960 | tf_op jit(solution)/shard_map/pallas_call | solution.py:48
  96.9 3.5 %collective-permute-start.24 = (bf16[32,2048]{1,0:T(8,128)(2,1)S(1)}, bf16[32,2048]{1,0:T(8,128)(2,1)S(1)}, u32[]{:S(2)}, u32[]{:S(2)}) collective-permute-start(bf16[32,2048]{1,0:T(8,128)(2,1)S(1)} %get-tuple-element.74), channel_id=1, source_target_pairs={{0,1},{1,2},{2,3},{3,0},{4,5},{5,6},{6,7},{7,4},{8,9},{9,10},{10,1... | collective-permute-start | bytes 393224 | tf_op jit(solution)/shard_map/ppermute | solution.py:528
  100.4 2.0 %collective-permute-start.25 = (bf16[32,2048]{1,0:T(8,128)(2,1)S(1)}, bf16[32,2048]{1,0:T(8,128)(2,1)S(1)}, u32[]{:S(2)}, u32[]{:S(2)}) collective-permute-start(bf16[32,2048]{1,0:T(8,128)(2,1)S(1)} %get-tuple-element.75), channel_id=1, source_target_pairs={{0,2},{1,3},{2,0},{3,1},{4,6},{5,7},{6,4},{7,5},{8,10},{9,11},{10,... | collective-permute-start | bytes 393224 | tf_op jit(solution)/shard_map/ppermute | solution.py:528
  102.9 3.4 %collective-permute-done.24.refs_0_ = bf16[32,2048]{1,0:T(8,128)(2,1)S(1)} collective-permute-done((bf16[32,2048]{1,0:T(8,128)(2,1)S(1)}, bf16[32,2048]{1,0:T(8,128)(2,1)S(1)}, u32[]{:S(2)}, u32[]{:S(2)}) %collective-permute-start.24) | collective-permute-done | bytes 131104 | tf_op jit(solution)/shard_map/ppermute | solution.py:528
  106.3 5.4 %collective-permute-done.25.refs_1_ = bf16[32,2048]{1,0:T(8,128)(2,1)S(1)} collective-permute-done((bf16[32,2048]{1,0:T(8,128)(2,1)S(1)}, bf16[32,2048]{1,0:T(8,128)(2,1)S(1)}, u32[]{:S(2)}, u32[]{:S(2)}) %collective-permute-start.25) | collective-permute-done | bytes 131104 | tf_op jit(solution)/shard_map/ppermute | solution.py:528
  111.7 0.7 shard_map.201
  (73 shorter events, 3.1 us)
Async XLA Ops:
  1.2 0.7 copy-start.3
  1.8 9.0 %copy-start.4 = (bf16[32,2176]{1,0:T(8,128)(2,1)S(1)}, bf16[32,2176]{1,0:T(8,128)(2,1)}, u32[]{:S(2)}) copy-start(bf16[32,2176]{1,0:T(8,128)(2,1)} %copy-done.3) | copy-start | bytes 417796
  1.8 8.1 %collective-permute-start = (bf16[32,2176]{1,0:T(8,128)(2,1)S(1)}, bf16[32,2176]{1,0:T(8,128)(2,1)S(1)}, u32[]{:S(2)}, u32[]{:S(2)}) collective-permute-start(bf16[32,2176]{1,0:T(8,128)(2,1)S(1)} %get-tuple-element.42), channel_id=1, source_target_pairs={{0,8},{4,12},{8,0},{12,4},{1,9},{5,13},{9,1},{13,5},{2,10},{6,14},... | collective-permute-start | bytes 417800 | tf_op jit(solution)/shard_map/ppermute | solution.py:524
  4.8 5.2 %collective-permute-start.1 = (bf16[32,2176]{1,0:T(8,128)(2,1)S(1)}, bf16[32,2176]{1,0:T(8,128)(2,1)S(1)}, u32[]{:S(2)}, u32[]{:S(2)}) collective-permute-start(bf16[32,2176]{1,0:T(8,128)(2,1)S(1)} %get-tuple-element.43), channel_id=1, source_target_pairs={{0,4},{4,0},{8,12},{12,8},{1,5},{5,1},{9,13},{13,9},{2,6},{6,2},{1... | collective-permute-start | bytes 417800 | tf_op jit(solution)/shard_map/ppermute | solution.py:524
  4.8 6.0 %collective-permute-start.2 = (bf16[32,2176]{1,0:T(8,128)(2,1)S(1)}, bf16[32,2176]{1,0:T(8,128)(2,1)S(1)}, u32[]{:S(2)}, u32[]{:S(2)}) collective-permute-start(bf16[32,2176]{1,0:T(8,128)(2,1)S(1)} %get-tuple-element.44), channel_id=1, source_target_pairs={{0,12},{4,8},{8,4},{12,0},{1,13},{5,9},{9,5},{13,1},{2,14},{6,10},... | collective-permute-start | bytes 417800 | tf_op jit(solution)/shard_map/ppermute | solution.py:524
  5.0 8.9 %copy-start.7 = (s32[4]{0:T(128)S(1)}, s32[4]{0:T(128)}, u32[]{:S(2)}) copy-start(s32[4]{0:T(128)} %refs_1_.5) | copy-start | bytes 52
  9.0 8.6 %copy-start.8 = (bf16[2048]{0:T(1024)(128)(2,1)S(1)}, bf16[2048]{0:T(1024)(128)(2,1)}, u32[]{:S(2)}) copy-start(bf16[2048]{0:T(1024)(128)(2,1)} %param.22) | copy-start | bytes 12292
  9.0 8.6 %copy-start.9 = (bf16[256]{0:T(256)(128)(2,1)S(1)}, bf16[256]{0:T(256)(128)(2,1)}, u32[]{:S(2)}) copy-start(bf16[256]{0:T(256)(128)(2,1)} %param.24) | copy-start | bytes 1540
  9.0 8.6 %copy-start.10 = (bf16[256]{0:T(256)(128)(2,1)S(1)}, bf16[256]{0:T(256)(128)(2,1)}, u32[]{:S(2)}) copy-start(bf16[256]{0:T(256)(128)(2,1)} %param.26) | copy-start | bytes 1540
  9.1 8.7 %copy-start.1 = (bf16[64,128,256]{2,1,0:T(8,128)(2,1)S(1)}, bf16[64,128,256]{2,1,0:T(8,128)(2,1)}, u32[]{:S(2)}) copy-start(bf16[64,128,256]{2,1,0:T(8,128)(2,1)} %refs_0_.7) | copy-start | bytes 12582916
  9.1 8.7 %copy-start.2 = (bf16[64,128,256]{2,1,0:T(8,128)(2,1)S(1)}, bf16[64,128,256]{2,1,0:T(8,128)(2,1)}, u32[]{:S(2)}) copy-start(bf16[64,128,256]{2,1,0:T(8,128)(2,1)} %refs_1_.4) | copy-start | bytes 12582916
  10.8 11.6 %copy-start.5 = (f32[128,128]{1,0:T(8,128)S(1)}, f32[128,128]{1,0:T(8,128)}, u32[]{:S(2)}) copy-start(f32[128,128]{1,0:T(8,128)} %constant.24.clone.refs_10_) | copy-start | bytes 196612
  10.8 11.6 %copy-start.6 = (s32[4,32]{1,0:T(4,128)S(1)}, s32[4,32]{1,0:T(4,128)}, u32[]{:S(2)}) copy-start(s32[4,32]{1,0:T(4,128)} %refs_9_.1) | copy-start | bytes 1540
  13.3 2.3 %collective-permute-start.3 = (f32[64,2688]{1,0:T(8,128)S(1)}, f32[64,2688]{1,0:T(8,128)S(1)}, u32[]{:S(2)}, u32[]{:S(2)}) collective-permute-start(f32[64,2688]{1,0:T(8,128)S(1)} %get-tuple-element.51), channel_id=1, source_target_pairs={{0,4},{4,0},{8,12},{12,8},{1,5},{5,1},{9,13},{13,9},{2,6},{6,2},{1... | collective-permute-start | bytes 2064392 | tf_op jit(solution)/shard_map/ppermute | solution.py:524
  15.6 20.1 %slice-start.4 = ((s8[8388608]{0:T(1024)(128)(4,1)}), s8[4194304]{0:T(1024)(128)(4,1)S(1)}, s32[]{:S(2)}) async-start(s8[8388608]{0:T(1024)(128)(4,1)} %bitcast.7), calls=%async_computation.4 | async-start | bytes 8388608
  15.7 6.7 %collective-permute-start.4 = (bf16[32,2688]{1,0:T(8,128)(2,1)S(1)}, bf16[32,2688]{1,0:T(8,128)(2,1)S(1)}, u32[]{:S(2)}, u32[]{:S(2)}) collective-permute-start(bf16[32,2688]{1,0:T(8,128)(2,1)S(1)} %get-tuple-element.53.refs_2_), channel_id=1, source_target_pairs={{0,8},{4,12},{8,0},{12,4},{1,9},{5,13},{9,1},{13,5},{2,10},{6,14},... | collective-permute-start | bytes 516104 | tf_op jit(solution)/shard_map/ppermute | solution.py:524
  17.8 17.9 %slice-start.5 = ((s8[8388608]{0:T(1024)(128)(4,1)}), s8[4194304]{0:T(1024)(128)(4,1)S(1)}, s32[]{:S(2)}) async-start(s8[8388608]{0:T(1024)(128)(4,1)} %bitcast.7), calls=%async_computation.5 | async-start | bytes 8388608
  22.4 36.2 %slice-start = ((s8[15728640]{0:T(1024)(128)(4,1)}), s8[3145728]{0:T(1024)(128)(4,1)S(1)}, s32[]{:S(2)}) async-start(s8[15728640]{0:T(1024)(128)(4,1)} %bitcast.5), calls=%async_computation | async-start | bytes 6291456
  22.4 36.2 %slice-start.1 = ((s8[15728640]{0:T(1024)(128)(4,1)}), s8[4194304]{0:T(1024)(128)(4,1)S(1)}, s32[]{:S(2)}) async-start(s8[15728640]{0:T(1024)(128)(4,1)} %bitcast.5), calls=%async_computation.1 | async-start | bytes 8388608
  30.7 27.9 %slice-start.2 = ((s8[15728640]{0:T(1024)(128)(4,1)}), s8[4194304]{0:T(1024)(128)(4,1)S(1)}, s32[]{:S(2)}) async-start(s8[15728640]{0:T(1024)(128)(4,1)} %bitcast.5), calls=%async_computation.2 | async-start | bytes 8388608
  30.7 5.0 %collective-permute-start.5 = (bf16[32,2048]{1,0:T(8,128)(2,1)S(1)}, bf16[32,2048]{1,0:T(8,128)(2,1)S(1)}, u32[]{:S(2)}, u32[]{:S(2)}) collective-permute-start(bf16[32,2048]{1,0:T(8,128)(2,1)S(1)} %shard_map.186.refs_1_.refs_2_), channel_id=1, source_target_pairs={{0,8},{4,12},{8,0},{12,4},{1,9},{5,13},{9,1},{13,5},{2,10},{6,14},... | collective-permute-start | bytes 393224 | tf_op jit(solution)/shard_map/ppermute | solution.py:524
  32.5 3.8 %collective-permute-start.6 = (bf16[32,2048]{1,0:T(8,128)(2,1)S(1)}, bf16[32,2048]{1,0:T(8,128)(2,1)S(1)}, u32[]{:S(2)}, u32[]{:S(2)}) collective-permute-start(bf16[32,2048]{1,0:T(8,128)(2,1)S(1)} %shard_map.186.refs_1_.refs_2_), channel_id=1, source_target_pairs={{0,4},{4,0},{8,12},{12,8},{1,5},{5,1},{9,13},{13,9},{2,6},{6,2},{1... | collective-permute-start | bytes 393224 | tf_op jit(solution)/shard_map/ppermute | solution.py:524
  35.7 1.3 %collective-permute-start.7 = (bf16[32,2048]{1,0:T(8,128)(2,1)S(1)}, bf16[32,2048]{1,0:T(8,128)(2,1)S(1)}, u32[]{:S(2)}, u32[]{:S(2)}) collective-permute-start(bf16[32,2048]{1,0:T(8,128)(2,1)S(1)} %collective-permute-done.5.refs_3_), channel_id=1, source_target_pairs={{0,4},{4,0},{8,12},{12,8},{1,5},{5,1},{9,13},{13,9},{2,6},{6,2},{1... | collective-permute-start | bytes 393224 | tf_op jit(solution)/shard_map/ppermute | solution.py:524
  36.3 22.3 %slice-start.3 = ((s8[15728640]{0:T(1024)(128)(4,1)}), s8[4194304]{0:T(1024)(128)(4,1)S(1)}, s32[]{:S(2)}) async-start(s8[15728640]{0:T(1024)(128)(4,1)} %bitcast.5), calls=%async_computation.3 | async-start | bytes 8388608
  39.2 8.3 %collective-permute-start.8 = (bf16[32,2048]{1,0:T(8,128)(2,1)S(1)}, bf16[32,2048]{1,0:T(8,128)(2,1)S(1)}, u32[]{:S(2)}, u32[]{:S(2)}) collective-permute-start(bf16[32,2048]{1,0:T(8,128)(2,1)S(1)} %get-tuple-element.57), channel_id=1, source_target_pairs={{0,1},{1,2},{2,3},{3,0},{4,5},{5,6},{6,7},{7,4},{8,9},{9,10},{10,1... | collective-permute-start | bytes 393224 | tf_op jit(solution)/shard_map/ppermute | solution.py:528
  41.1 11.6 %collective-permute-start.9 = (bf16[32,2048]{1,0:T(8,128)(2,1)S(1)}, bf16[32,2048]{1,0:T(8,128)(2,1)S(1)}, u32[]{:S(2)}, u32[]{:S(2)}) collective-permute-start(bf16[32,2048]{1,0:T(8,128)(2,1)S(1)} %get-tuple-element.58), channel_id=1, source_target_pairs={{0,2},{1,3},{2,0},{3,1},{4,6},{5,7},{6,4},{7,5},{8,10},{9,11},{10,... | collective-permute-start | bytes 393224 | tf_op jit(solution)/shard_map/ppermute | solution.py:528
  43.7 9.0 %collective-permute-start.10 = (bf16[32,2048]{1,0:T(8,128)(2,1)S(1)}, bf16[32,2048]{1,0:T(8,128)(2,1)S(1)}, u32[]{:S(2)}, u32[]{:S(2)}) collective-permute-start(bf16[32,2048]{1,0:T(8,128)(2,1)S(1)} %get-tuple-element.59), channel_id=1, source_target_pairs={{0,3},{1,0},{2,1},{3,2},{4,7},{5,4},{6,5},{7,6},{8,11},{9,8},{10,9... | collective-permute-start | bytes 393224 | tf_op jit(solution)/shard_map/ppermute | solution.py:528
  52.8 13.4 %collective-permute-start.11 = (bf16[32,2176]{1,0:T(8,128)(2,1)S(1)}, bf16[32,2176]{1,0:T(8,128)(2,1)S(1)}, u32[]{:S(2)}, u32[]{:S(2)}) collective-permute-start(bf16[32,2176]{1,0:T(8,128)(2,1)S(1)} %get-tuple-element.61.refs_1_), channel_id=1, source_target_pairs={{0,1},{1,2},{2,3},{3,0},{4,5},{5,6},{6,7},{7,4},{8,9},{9,10},{10,1... | collective-permute-start | bytes 417800 | tf_op jit(solution)/shard_map/ppermute | solution.py:528
  56.2 10.3 %collective-permute-start.12 = (bf16[32,2176]{1,0:T(8,128)(2,1)S(1)}, bf16[32,2176]{1,0:T(8,128)(2,1)S(1)}, u32[]{:S(2)}, u32[]{:S(2)}) collective-permute-start(bf16[32,2176]{1,0:T(8,128)(2,1)S(1)} %get-tuple-element.61.refs_1_), channel_id=1, source_target_pairs={{0,2},{1,3},{2,0},{3,1},{4,6},{5,7},{6,4},{7,5},{8,10},{9,11},{10,... | collective-permute-start | bytes 417800 | tf_op jit(solution)/shard_map/ppermute | solution.py:528
  57.8 8.7 %collective-permute-start.13 = (bf16[32,2176]{1,0:T(8,128)(2,1)S(1)}, bf16[32,2176]{1,0:T(8,128)(2,1)S(1)}, u32[]{:S(2)}, u32[]{:S(2)}) collective-permute-start(bf16[32,2176]{1,0:T(8,128)(2,1)S(1)} %get-tuple-element.61.refs_1_), channel_id=1, source_target_pairs={{0,3},{1,0},{2,1},{3,2},{4,7},{5,4},{6,5},{7,6},{8,11},{9,8},{10,9... | collective-permute-start | bytes 417800 | tf_op jit(solution)/shard_map/ppermute | solution.py:528
  59.7 5.5 %copy-start = (bf16[2048,3840]{1,0:T(8,128)(2,1)S(1)}, bf16[2048,3840]{1,0:T(8,128)(2,1)}, u32[]{:S(2)}) copy-start(bf16[2048,3840]{1,0:T(8,128)(2,1)} %refs_0_.10) | copy-start | bytes 47185924
  69.9 3.3 %collective-permute-start.14 = (bf16[64,3968]{1,0:T(8,128)(2,1)S(1)}, bf16[64,3968]{1,0:T(8,128)(2,1)S(1)}, u32[]{:S(2)}, u32[]{:S(2)}) collective-permute-start(bf16[64,3968]{1,0:T(8,128)(2,1)S(1)} %get-tuple-element.63), channel_id=1, source_target_pairs={{0,4},{4,0},{8,12},{12,8},{1,5},{5,1},{9,13},{13,9},{2,6},{6,2},{1... | collective-permute-start | bytes 1523720 | tf_op jit(solution)/shard_map/ppermute | solution.py:524
  72.7 2.3 %collective-permute-start.16 = (bf16[64,3840]{1,0:T(8,128)(2,1)S(1)}, bf16[64,3840]{1,0:T(8,128)(2,1)S(1)}, u32[]{:S(2)}, u32[]{:S(2)}) collective-permute-start(bf16[64,3840]{1,0:T(8,128)(2,1)S(1)} %get-tuple-element.68), channel_id=1, source_target_pairs={{0,4},{4,0},{8,12},{12,8},{1,5},{5,1},{9,13},{13,9},{2,6},{6,2},{1... | collective-permute-start | bytes 1474568 | tf_op jit(solution)/shard_map/ppermute | solution.py:524
  73.4 9.1 %collective-permute-start.15 = (bf16[32,3968]{1,0:T(8,128)(2,1)S(1)}, bf16[32,3968]{1,0:T(8,128)(2,1)S(1)}, u32[]{:S(2)}, u32[]{:S(2)}) collective-permute-start(bf16[32,3968]{1,0:T(8,128)(2,1)S(1)} %get-tuple-element.65), channel_id=1, source_target_pairs={{0,8},{4,12},{8,0},{12,4},{1,9},{5,13},{9,1},{13,5},{2,10},{6,14},... | collective-permute-start | bytes 761864 | tf_op jit(solution)/shard_map/ppermute | solution.py:524
  75.1 12.6 %collective-permute-start.17 = (bf16[32,3840]{1,0:T(8,128)(2,1)S(1)}, bf16[32,3840]{1,0:T(8,128)(2,1)S(1)}, u32[]{:S(2)}, u32[]{:S(2)}) collective-permute-start(bf16[32,3840]{1,0:T(8,128)(2,1)S(1)} %get-tuple-element.69.refs_1_), channel_id=1, source_target_pairs={{0,8},{4,12},{8,0},{12,4},{1,9},{5,13},{9,1},{13,5},{2,10},{6,14},... | collective-permute-start | bytes 737288 | tf_op jit(solution)/shard_map/ppermute | solution.py:524
  82.7 7.3 %collective-permute-start.21 = (bf16[32,1920]{1,0:T(8,128)(2,1)S(1)}, bf16[32,1920]{1,0:T(8,128)(2,1)S(1)}, u32[]{:S(2)}, u32[]{:S(2)}) collective-permute-start(bf16[32,1920]{1,0:T(8,128)(2,1)S(1)} %get-tuple-element.72.refs_1_), channel_id=1, source_target_pairs={{0,8},{4,12},{8,0},{12,4},{1,9},{5,13},{9,1},{13,5},{2,10},{6,14},... | collective-permute-start | bytes 368648 | tf_op jit(solution)/shard_map/ppermute | solution.py:524
  87.9 4.9 %collective-permute-start.18 = (bf16[32,1920]{1,0:T(8,128)(2,1)S(1)}, bf16[32,1920]{1,0:T(8,128)(2,1)S(1)}, u32[]{:S(2)}, u32[]{:S(2)}) collective-permute-start(bf16[32,1920]{1,0:T(8,128)(2,1)S(1)} %shard_map.198.refs_1_), channel_id=1, source_target_pairs={{0,8},{4,12},{8,0},{12,4},{1,9},{5,13},{9,1},{13,5},{2,10},{6,14},... | collective-permute-start | bytes 368648 | tf_op jit(solution)/shard_map/ppermute | solution.py:524
  89.5 3.4 %collective-permute-start.22 = (bf16[32,1920]{1,0:T(8,128)(2,1)S(1)}, bf16[32,1920]{1,0:T(8,128)(2,1)S(1)}, u32[]{:S(2)}, u32[]{:S(2)}) collective-permute-start(bf16[32,1920]{1,0:T(8,128)(2,1)S(1)} %get-tuple-element.72.refs_1_), channel_id=1, source_target_pairs={{0,4},{4,0},{8,12},{12,8},{1,5},{5,1},{9,13},{13,9},{2,6},{6,2},{1... | collective-permute-start | bytes 368648 | tf_op jit(solution)/shard_map/ppermute | solution.py:524
  90.0 2.8 %collective-permute-start.23 = (bf16[32,1920]{1,0:T(8,128)(2,1)S(1)}, bf16[32,1920]{1,0:T(8,128)(2,1)S(1)}, u32[]{:S(2)}, u32[]{:S(2)}) collective-permute-start(bf16[32,1920]{1,0:T(8,128)(2,1)S(1)} %collective-permute-done.21.refs_2_), channel_id=1, source_target_pairs={{0,4},{4,0},{8,12},{12,8},{1,5},{5,1},{9,13},{13,9},{2,6},{6,2},{1... | collective-permute-start | bytes 368648 | tf_op jit(solution)/shard_map/ppermute | solution.py:524
  90.0 4.9 %collective-permute-start.19 = (bf16[32,1920]{1,0:T(8,128)(2,1)S(1)}, bf16[32,1920]{1,0:T(8,128)(2,1)S(1)}, u32[]{:S(2)}, u32[]{:S(2)}) collective-permute-start(bf16[32,1920]{1,0:T(8,128)(2,1)S(1)} %shard_map.198.refs_1_), channel_id=1, source_target_pairs={{0,4},{4,0},{8,12},{12,8},{1,5},{5,1},{9,13},{13,9},{2,6},{6,2},{1... | collective-permute-start | bytes 368648 | tf_op jit(solution)/shard_map/ppermute | solution.py:524
  92.9 2.0 %collective-permute-start.20 = (bf16[32,1920]{1,0:T(8,128)(2,1)S(1)}, bf16[32,1920]{1,0:T(8,128)(2,1)S(1)}, u32[]{:S(2)}, u32[]{:S(2)}) collective-permute-start(bf16[32,1920]{1,0:T(8,128)(2,1)S(1)} %collective-permute-done.18.refs_2_), channel_id=1, source_target_pairs={{0,4},{4,0},{8,12},{12,8},{1,5},{5,1},{9,13},{13,9},{2,6},{6,2},{1... | collective-permute-start | bytes 368648 | tf_op jit(solution)/shard_map/ppermute | solution.py:524
  96.9 9.4 %collective-permute-start.24 = (bf16[32,2048]{1,0:T(8,128)(2,1)S(1)}, bf16[32,2048]{1,0:T(8,128)(2,1)S(1)}, u32[]{:S(2)}, u32[]{:S(2)}) collective-permute-start(bf16[32,2048]{1,0:T(8,128)(2,1)S(1)} %get-tuple-element.74), channel_id=1, source_target_pairs={{0,1},{1,2},{2,3},{3,0},{4,5},{5,6},{6,7},{7,4},{8,9},{9,10},{10,1... | collective-permute-start | bytes 393224 | tf_op jit(solution)/shard_map/ppermute | solution.py:528
  100.4 11.3 %collective-permute-start.25 = (bf16[32,2048]{1,0:T(8,128)(2,1)S(1)}, bf16[32,2048]{1,0:T(8,128)(2,1)S(1)}, u32[]{:S(2)}, u32[]{:S(2)}) collective-permute-start(bf16[32,2048]{1,0:T(8,128)(2,1)S(1)} %get-tuple-element.75), channel_id=1, source_target_pairs={{0,2},{1,3},{2,0},{3,1},{4,6},{5,7},{6,4},{7,5},{8,10},{9,11},{10,... | collective-permute-start | bytes 393224 | tf_op jit(solution)/shard_map/ppermute | solution.py:528
  102.4 9.3 %collective-permute-start.26 = (bf16[32,2048]{1,0:T(8,128)(2,1)S(1)}, bf16[32,2048]{1,0:T(8,128)(2,1)S(1)}, u32[]{:S(2)}, u32[]{:S(2)}) collective-permute-start(bf16[32,2048]{1,0:T(8,128)(2,1)S(1)} %get-tuple-element.76), channel_id=1, source_target_pairs={{0,3},{1,0},{2,1},{3,2},{4,7},{5,4},{6,5},{7,6},{8,11},{9,8},{10,9... | collective-permute-start | bytes 393224 | tf_op jit(solution)/shard_map/ppermute | solution.py:528

commit v3 on v2

--- a/solution.py
+++ b/solution.py
@@ -223,21 +223,30 @@
         ref[:, -EXT:] = split_lanes(total[:, -EXT:][:, :1])
 
 
-def attend_kernel(kv_local, group_size, chunk_pages, unroll, received_n, *refs):
-    spot, path_pages, mine = refs[:3]
-    received = refs[3 : 3 + received_n]
-    bq, bk, bv, waves, codes, page_table, turn, kbuf, vbuf = refs[3 + received_n : 12 + received_n]
-    out, scores, mixed, page_marks = refs[12 + received_n :]
-    slots = mine.shape[0]
-    squares = mine[:, -EXT:][:, :1]
-    total = mine[:, :-EXT]
-    for ref in received:
-        total = total + ref[:, :-EXT].astype(F32)
-        squares = squares + jnp.sum(ref[:, -EXT:].astype(F32), 1, keepdims=True)
-    bias = jnp.concatenate([ref[...].astype(F32) for ref in (bq, bk, bv)], 1)
-    packed = (total * lax.rsqrt(squares * (1.0 / D) + EPS) + bias).astype(BF16).astype(F32)
-    heads = kv_local * group_size
-    rotation = turn[...]
+def marks_kernel(
+    slots,
+    local_rows,
+    chips,
+    head_count,
+    spot,
+    path_pages,
+    page_table,
+    codes,
+    waves,
+    bq,
+    bk,
+    bv,
+    _,
+    wave_out,
+    slot_out,
+    page_out,
+    bias_out,
+    mixer_order,
+    gate_order,
+    lower_order,
+):
+    place = Place(spot, chips, head_count)
+    share_rows = chips * CORES * local_rows // head_count
     code, parent = codes[:, :1], codes[:, 1:2]
     lane = lax.broadcasted_iota(jnp.int32, (1, EXT), 1).astype(F32)
     parent_at = (parent - jnp.floor(parent * (1.0 / P_DEV)) * P_DEV == lane).astype(BF16)
@@ -255,7 +264,34 @@
         )
         owned = jnp.max(live.astype(F32), 1, keepdims=True)
         page_mark = jnp.where(lane == local_parent, (1.0 - owned) * FAR, page_mark)
-
+    wave_out[...] = wave
+    slot_out[...] = slot_mark.astype(BF16)
+    page_out[...] = page_mark
+    bias_out[...] = jnp.concatenate([ref[...].astype(F32) for ref in (bq, bk, bv)], 1)
+    child_at = column(place.sources(), local_rows)
+    lower = onehot(column(place.to_heads(), share_rows), child_at)
+    lower_order[...] = lower
+    slot_rows = onehot(code, column(place.sources(), slots))
+    mixer_order[...] = dot32(lower, slot_rows).astype(BF16)
+    gate_order[...] = onehot(
+        column(place.targets(), local_rows), column(place.from_heads(), share_rows)
+    )
+
+
+def attend_kernel(kv_local, group_size, chunk_pages, unroll, received_n, *refs):
+    mine = refs[0]
+    received = refs[1 : 1 + received_n]
+    bias, wave, slot_mark, page_marks, turn, kbuf, vbuf = refs[1 + received_n : 8 + received_n]
+    out, scores, mixed = refs[8 + received_n :]
+    slots = mine.shape[0]
+    squares = mine[:, -EXT:][:, :1]
+    total = mine[:, :-EXT]
+    for ref in received:
+        total = total + ref[:, :-EXT].astype(F32)
+        squares = squares + jnp.sum(ref[:, -EXT:].astype(F32), 1, keepdims=True)
+    packed = (total * lax.rsqrt(squares * (1.0 / D) + EPS) + bias[...]).astype(BF16).astype(F32)
+    heads = kv_local * group_size
+    rotation = turn[...]
     def stacked(first, count):
         return jnp.concatenate(
             [packed[:, (first + at) * HD : (first + at + 1) * HD] for at in range(count)], 0
@@ -276,8 +312,7 @@
     rows = group_size * slots
     chunk = chunk_pages * PAGE
     chunks = POOL // chunk_pages
-    marks = jnp.concatenate([slot_mark.astype(BF16)] * group_size, 0)
-    page_marks[...] = page_mark
+    marks = jnp.concatenate([slot_mark[...]] * group_size, 0)
     for kv_at in range(kv_local):
         query_now = queries[kv_at * rows : (kv_at + 1) * rows]
         left = jnp.concatenate([turned[kv_at * rows : (kv_at + 1) * rows], marks], 1)
@@ -345,32 +380,21 @@
             ref[:, span] = product[(at + 1) * share : (at + 2) * share].astype(BF16)
 
 
-def mixer_kernel(slots, local_rows, chips, head_count, width, *refs):
-    blocks_n = chips * CORES
-    spot, codes = refs[:2]
-    blocks = refs[2 : 2 + blocks_n]
-    weight, mine = refs[2 + blocks_n : 4 + blocks_n]
-    place = Place(spot, chips, head_count)
-    sources = place.sources()
-    slot_rows = onehot(codes[:, :1], column(sources, slots))
-    child_rows = onehot(column(place.to_heads(), mine.shape[0]), column(sources, local_rows))
-    order = dot32(child_rows, slot_rows).astype(BF16)
+def mixer_kernel(blocks_n, width, order, *refs):
+    blocks = refs[:blocks_n]
+    weight, mine = refs[blocks_n : 2 + blocks_n]
     rows = jnp.concatenate([ref[...] for ref in blocks], 0)
-    spread_rows(rows, order, weight, width, mine, refs[4 + blocks_n :])
-
-
-def lower_kernel(first, last, local_rows, chips, head_count, width, *refs):
-    blocks_n = chips * CORES
-    spot = refs[0]
+    spread_rows(rows, order[...], weight, width, mine, refs[2 + blocks_n :])
+
+
+def lower_kernel(first, last, blocks_n, share_rows, width, *refs):
+    order = refs[0]
     blocks = refs[1 : 1 + blocks_n]
     weight = refs[1 + blocks_n]
     before = None if first == 0 else refs[2 + blocks_n]
     outs = refs[(2 if first == 0 else 3) + blocks_n :]
-    place = Place(spot, chips, head_count)
-    share_rows = chips * CORES * local_rows // head_count
-    order = onehot(column(place.to_heads(), share_rows), column(place.sources(), local_rows))
     rows = jnp.concatenate([ref[...] for ref in blocks], 0)
-    ordered = dot32(order, rows).astype(BF16)
+    ordered = dot32(order[...], rows).astype(BF16)
     deep = rows.shape[1]
     for step in range(weight.shape[1] // width):
         span = slice(step * width, (step + 1) * width)
@@ -410,16 +434,12 @@
             at += width
 
 
-def first_gate_kernel(local_rows, chips, head_count, count, width, *refs):
-    spot = refs[0]
+def first_gate_kernel(head_count, count, width, *refs):
+    order = refs[0]
     blocks = refs[1 : 1 + head_count]
     w_gate, w_up, keep, send, rest = refs[1 + head_count :]
-    place = Place(spot, chips, head_count)
-    order = onehot(
-        column(place.targets(), local_rows), column(place.from_heads(), blocks[0].shape[0])
-    )
     rows = jnp.concatenate([ref[...] for ref in blocks], 0)
-    ordered = dot32(order, rows).astype(BF16)
+    ordered = dot32(order[...], rows).astype(BF16)
     rest[...] = ordered
     half = keep.shape[0]
     keep[:, -EXT:] = ordered[:half, -EXT:].astype(F32)
@@ -581,28 +601,48 @@
     angle = (path_pages.astype(F32) * PAGE)[:, None] * freqs
     cosine, sine = jnp.cos(angle), jnp.sin(angle)
     waves = jnp.concatenate([cosine, cosine, -sine, sine], 1)
+    order_out = ((all_rows, all_rows), BF16)
+    wave, slot_mark, page_mark, biases, mixer_order, gate_order, lower_order = call(
+        functools.partial(marks_kernel, slots, local_rows, chips, head_count),
+        [
+            ((slots, 2 * HD), F32),
+            ((slots, EXT), BF16),
+            ((POOL, EXT), F32),
+            ((1, packed_cols), F32),
+            ((all_rows, slots * branch_count), BF16),
+            order_out,
+            order_out,
+        ],
+        ["smem"] * 2 + ["vmem"] * 6 + ["any"],
+        [],
+        spot,
+        path_pages,
+        page_table,
+        codes,
+        waves,
+        b_query[None],
+        b_key[None],
+        b_value[None],
+        others[0],
+        moved=MIB,
+    )
     rows = group_size * slots
     chunk_pages, unroll = (16, 2) if rows <= 512 else (4, 1)
     score_bytes = 4 * rows * POOL * PAGE
     (attention,) = call(
         functools.partial(attend_kernel, kv_local, group_size, chunk_pages, unroll, chips - 1),
         [((slots, query_cols), BF16)],
-        ["smem"] * 2 + ["vmem"] * (chips + 9),
+        ["vmem"] * (chips + 7),
         [
             pltpu.VMEM((POOL // chunk_pages, chunk_pages * PAGE, rows), F32),
             pltpu.VMEM((HD, rows), F32),
-            pltpu.VMEM((POOL, EXT), F32),
         ],
-        spot,
-        path_pages,
         mine,
         *received,
-        b_query[None],
-        b_key[None],
-        b_value[None],
-        waves,
-        codes,
-        page_table,
+        biases,
+        wave,
+        slot_mark,
+        page_mark,
         jnp.asarray(hadamard(HD)),
         keys,
         values,
@@ -618,12 +658,11 @@
     (w_out_near,) = fetch([w_out], attention)
     out_width = block_width(model_cols, 512)
     mixer, *others = call(
-        functools.partial(mixer_kernel, slots, local_rows, chips, head_count, out_width),
+        functools.partial(mixer_kernel, branch_count, out_width),
         [((share_rows, model_cols), F32)] + [((share_rows, model_cols), BF16)] * (head_count - 1),
-        ["smem"] + ["vmem"] * (branch_count + 2),
-        [],
-        spot,
-        codes,
+        ["vmem"] * (branch_count + 2),
+        [],
+        mixer_order,
         *gathered,
         w_out_near,
         flops=2 * all_rows * w_out.size,
@@ -652,16 +691,14 @@
     keep, send, ordered = call(
         functools.partial(
             first_gate_kernel,
-            local_rows,
-            chips,
             head_count,
             counts[0],
             block_width(counts[0], 768),
         ),
         gate_outs(2 * counts[0] + EXT) + [((all_rows, model_cols + EXT), BF16)],
-        ["smem"] + ["vmem"] * (head_count + 2),
-        [],
-        spot,
+        ["vmem"] * (head_count + 3),
+        [],
+        gate_order,
         *scaled_blocks,
         w_gate_near,
         w_up_near,
@@ -713,21 +750,21 @@
     )
     gathered_next = gather_branch(activated)
     (partial,) = call(
-        functools.partial(lower_kernel, 0, False, local_rows, chips, head_count, out_width),
+        functools.partial(lower_kernel, 0, False, branch_count, share_rows, out_width),
         [((all_rows, model_cols), F32)],
-        ["smem"] + ["vmem"] * (branch_count + 1),
-        [],
-        spot,
+        ["vmem"] * (branch_count + 2),
+        [],
+        lower_order,
         *gathered,
         w_down_near,
         flops=2 * all_rows * model_cols * counts[0],
     )
     lowered, *others = call(
-        functools.partial(lower_kernel, cuts[1], True, local_rows, chips, head_count, out_width),
+        functools.partial(lower_kernel, cuts[1], True, branch_count, share_rows, out_width),
         [((share_rows, model_cols), F32)] + [((share_rows, model_cols), BF16)] * (head_count - 1),
-        ["smem"] + ["vmem"] * (branch_count + 2),
-        [],
-        spot,
+        ["vmem"] * (branch_count + 3),
+        [],
+        lower_order,
         *gathered_next,
         w_down_near,
         partial,

time: 113 us -> 110 us (0.973)
  Pallas kernels: 38.7 us -> 36.3 us
    pallas_call x15 -> x16, Pallas kernels: 25.9 us -> 23.5 us  [call(): pl.pallas_call(kernel, out_shape=[pltpu.VMEM(shape, kind) if near else ja...]
  transfers between devices with their start and end apart: 27 -> 27, of which waited for: 14 -> 14; matrix products, arithmetic and copies ran while one was open for 2% -> 2% of each run, Pallas kernels for 16% -> 17%
where the time goes in v3:
time: 110 us; the launch traced here: 109 us
  Pallas kernels  36.3 us (33%)
  waiting for transfers between devices  32.6 us (30%)
  starting transfers between devices  31.9 us (29%)
  local copies, waits for them, and re-layouts  6.2 us (6%)
  other arithmetic  1.81 us (2%)
    pallas_call x16, Pallas kernels, call(): pl.pallas_call(kernel, out_shape=[pltpu.VMEM(shape, kind) if near else ja...  23.5 us
    ppermute x9, starting transfers between devices, over_head(): return lax.ppermute(array, 'head', pairs)  17.5 us
    ppermute x18, waiting for transfers between devices, over_branch(): return lax.ppermute(array, 'branch', pairs)  16.6 us
    ppermute x9, waiting for transfers between devices, over_head(): return lax.ppermute(array, 'head', pairs)  16 us
    ppermute x18, starting transfers between devices, over_branch(): return lax.ppermute(array, 'branch', pairs)  14.3 us
    pallas_call x6, Pallas kernels, fetch(): pl.pallas_call(functools.partial(fetch_kernel, len(arrays)), out_shape=[p...  12.8 us
    unnamed x34, local copies, waits for them, and re-layouts  6.18 us
  transfers between devices with their start and end apart: 27, of which 14 were waited for; matrix products, arithmetic and copies ran while one was open for 2% of the time, Pallas kernels for 17%

profile of v3, /device:TPU:0, one launch (start us, length us, event | category | flops | bytes accessed | tf_op | source)
XLA Modules:
  0.0 109.1 jit_solution(16444778395776928608)
XLA Ops:
  0.0 1.2 %shard_map.181 = (bf16[32,2176]{1,0:T(8,128)(2,1)S(1)}, bf16[32,2176]{1,0:T(8,128)(2,1)S(1)}, bf16[32,2176]{1,0:T(8,128)(2,1)S(1)}, bf16[32,2176]{1,0:T(8,128)(2,1)S(1)}) custom-call(bf16[32,8192]{1,0:T(8,128)(2,1)} %hidden.1, s32[1,32]{1,0:T(1,128)} %bitcast.11), custom_call_target="tpu_custom_call" | custom-call | tf_op jit(solution)/shard_map/pallas_call | solution.py:48
  1.2 0.6 copy-done.3
  1.8 2.9 %collective-permute-start = (bf16[32,2176]{1,0:T(8,128)(2,1)S(1)}, bf16[32,2176]{1,0:T(8,128)(2,1)S(1)}, u32[]{:S(2)}, u32[]{:S(2)}) collective-permute-start(bf16[32,2176]{1,0:T(8,128)(2,1)S(1)} %get-tuple-element.49), channel_id=1, source_target_pairs={{0,8},{4,12},{8,0},{12,4},{1,9},{5,13},{9,1},{13,5},{2,10},{6,14},... | collective-permute-start | bytes 417800 | tf_op jit(solution)/shard_map/ppermute | solution.py:544
  5.0 4.1 %shard_map.182 = (bf16[2048,2048]{1,0:T(8,128)(2,1)S(1)}, bf16[2048,256]{1,0:T(8,128)(2,1)S(1)}, bf16[2048,256]{1,0:T(8,128)(2,1)S(1)}) custom-call(bf16[2048,2048]{1,0:T(8,128)(2,1)} %refs_0_.6, bf16[2048,256]{1,0:T(8,128)(2,1)} %refs_1_.2, bf16[2048,256]{1,0:T(8,128)(2,1)} %refs_2_.1, bf16[32,2176]{1,0:T(8,128)(2,1)} %copy-done.3), custom_call_target="tpu_custom_call" | custom-call | bytes 20971520 | tf_op jit(solution)/shard_map/pallas_call | solution.py:76
  9.1 0.8 dynamic-slice_convert_fusion.1
  9.9 0.9 collective-permute-done.2.refs_4_
  10.8 2.5 %shard_map.183 = (f32[64,2688]{1,0:T(8,128)S(1)}, f32[64,2688]{1,0:T(8,128)S(1)}, bf16[32,2048]{1,0:T(8,128)(2,1)S(1)}, f32[128,128]{1,0:T(8,128)S(1)}) custom-call(s32[2]{0:T(128)S(1)} %pad_add_fusion.refs_0_.spot, bf16[32,2176]{1,0:T(8,128)(2,1)S(1)} %copy-done.4, bf16[32,2176]{1,0:T(8,128)(2,1)S(1)} %collective-permute-done.refs_2_, ...), custom_call_target="tpu_custom_call" | custom-call | flops 1342177280 | tf_op jit(solution)/shard_map/pallas_call | solution.py:48
  13.9 1.7 %collective-permute-done.3.got = f32[64,2688]{1,0:T(8,128)S(1)} collective-permute-done((f32[64,2688]{1,0:T(8,128)S(1)}, f32[64,2688]{1,0:T(8,128)S(1)}, u32[]{:S(2)}, u32[]{:S(2)}) %collective-permute-start.3) | collective-permute-done | bytes 688160 | tf_op jit(solution)/shard_map/ppermute | solution.py:544
  15.7 1.8 %collective-permute-start.4 = (bf16[32,2688]{1,0:T(8,128)(2,1)S(1)}, bf16[32,2688]{1,0:T(8,128)(2,1)S(1)}, u32[]{:S(2)}, u32[]{:S(2)}) collective-permute-start(bf16[32,2688]{1,0:T(8,128)(2,1)S(1)} %get-tuple-element.59._.refs_2_), channel_id=1, source_target_pairs={{0,8},{4,12},{8,0},{12,4},{1,9},{5,13},{9,1},{13,5},{2,10},{6,14},... | collective-permute-start | bytes 516104 | tf_op jit(solution)/shard_map/ppermute | solution.py:544
  17.8 0.6 shard_map.186
  18.4 0.9 shard_map.185
  19.3 3.1 %collective-permute-done.4.refs_1_ = bf16[32,2688]{1,0:T(8,128)(2,1)S(1)} collective-permute-done((bf16[32,2688]{1,0:T(8,128)(2,1)S(1)}, bf16[32,2688]{1,0:T(8,128)(2,1)S(1)}, u32[]{:S(2)}, u32[]{:S(2)}) %collective-permute-start.4) | collective-permute-done | bytes 172064 | tf_op jit(solution)/shard_map/ppermute | solution.py:544
  22.4 7.5 %shard_map.187.refs_1_.refs_0_ = bf16[32,2048]{1,0:T(8,128)(2,1)S(1)} custom-call(f32[32,2688]{1,0:T(8,128)S(1)} %get-tuple-element.61.refs_0_, bf16[32,2688]{1,0:T(8,128)(2,1)S(1)} %collective-permute-done.4.refs_1_, f32[1,2560]{1,0:T(1,128)S(1)} %get-tuple-element.62.refs_2_, f32[32,256]{1,0:T(8,128)S(1)} %get-tuple-element.63.refs_3_, ...), custom_call_target="tpu_custom_call" | custom-call | flops 2147483648 | tf_op jit(solution)/shard_map/pallas_call | solution.py:48
  29.9 1.8 %collective-permute-start.5 = (bf16[32,2048]{1,0:T(8,128)(2,1)S(1)}, bf16[32,2048]{1,0:T(8,128)(2,1)S(1)}, u32[]{:S(2)}, u32[]{:S(2)}) collective-permute-start(bf16[32,2048]{1,0:T(8,128)(2,1)S(1)} %shard_map.187.refs_1_.refs_0_), channel_id=1, source_target_pairs={{0,8},{4,12},{8,0},{12,4},{1,9},{5,13},{9,1},{13,5},{2,10},{6,14},... | collective-permute-start | bytes 393224 | tf_op jit(solution)/shard_map/ppermute | solution.py:544
  31.7 3.2 %collective-permute-done.5.refs_1_ = bf16[32,2048]{1,0:T(8,128)(2,1)S(1)} collective-permute-done((bf16[32,2048]{1,0:T(8,128)(2,1)S(1)}, bf16[32,2048]{1,0:T(8,128)(2,1)S(1)}, u32[]{:S(2)}, u32[]{:S(2)}) %collective-permute-start.5) | collective-permute-done | bytes 131104 | tf_op jit(solution)/shard_map/ppermute | solution.py:544
  35.0 0.6 shard_map.188.refs_4_
  35.6 0.7 collective-permute-done.7.refs_3_
  36.3 1.4 %shard_map.189 = (f32[32,2048]{1,0:T(8,128)S(1)}, bf16[32,2048]{1,0:T(8,128)(2,1)S(1)}, bf16[32,2048]{1,0:T(8,128)(2,1)S(1)}, bf16[32,2048]{1,0:T(8,128)(2,1)S(1)}) custom-call(bf16[128,128]{1,0:T(8,128)(2,1)S(1)} %get-tuple-element.60.order, bf16[32,2048]{1,0:T(8,128)(2,1)S(1)} %shard_map.187.refs_1_.refs_0_, ...), custom_call_target="tpu_custom_call" | custom-call | flops 1073741824 | tf_op jit(solution)/shard_map/pallas_call | solution.py:48
  37.7 1.9 %collective-permute-start.8 = (bf16[32,2048]{1,0:T(8,128)(2,1)S(1)}, bf16[32,2048]{1,0:T(8,128)(2,1)S(1)}, u32[]{:S(2)}, u32[]{:S(2)}) collective-permute-start(bf16[32,2048]{1,0:T(8,128)(2,1)S(1)} %get-tuple-element.69), channel_id=1, source_target_pairs={{0,1},{1,2},{2,3},{3,0},{4,5},{5,6},{6,7},{7,4},{8,9},{9,10},{10,1... | collective-permute-start | bytes 393224 | tf_op jit(solution)/shard_map/ppermute | solution.py:548
  39.6 2.6 %collective-permute-start.9 = (bf16[32,2048]{1,0:T(8,128)(2,1)S(1)}, bf16[32,2048]{1,0:T(8,128)(2,1)S(1)}, u32[]{:S(2)}, u32[]{:S(2)}) collective-permute-start(bf16[32,2048]{1,0:T(8,128)(2,1)S(1)} %get-tuple-element.70), channel_id=1, source_target_pairs={{0,2},{1,3},{2,0},{3,1},{4,6},{5,7},{6,4},{7,5},{8,10},{9,11},{10,... | collective-permute-start | bytes 393224 | tf_op jit(solution)/shard_map/ppermute | solution.py:548
  42.2 1.3 %collective-permute-start.10 = (bf16[32,2048]{1,0:T(8,128)(2,1)S(1)}, bf16[32,2048]{1,0:T(8,128)(2,1)S(1)}, u32[]{:S(2)}, u32[]{:S(2)}) collective-permute-start(bf16[32,2048]{1,0:T(8,128)(2,1)S(1)} %get-tuple-element.71), channel_id=1, source_target_pairs={{0,3},{1,0},{2,1},{3,2},{4,7},{5,4},{6,5},{7,6},{8,11},{9,8},{10,9... | collective-permute-start | bytes 393224 | tf_op jit(solution)/shard_map/ppermute | solution.py:548
  43.5 0.7 dynamic-slice_convert_fusion
  44.2 1.8 %collective-permute-done.8.refs_0_ = bf16[32,2048]{1,0:T(8,128)(2,1)S(1)} collective-permute-done((bf16[32,2048]{1,0:T(8,128)(2,1)S(1)}, bf16[32,2048]{1,0:T(8,128)(2,1)S(1)}, u32[]{:S(2)}, u32[]{:S(2)}) %collective-permute-start.8) | collective-permute-done | bytes 131104 | tf_op jit(solution)/shard_map/ppermute | solution.py:548
  46.0 5.1 %collective-permute-done.9.refs_1_ = bf16[32,2048]{1,0:T(8,128)(2,1)S(1)} collective-permute-done((bf16[32,2048]{1,0:T(8,128)(2,1)S(1)}, bf16[32,2048]{1,0:T(8,128)(2,1)S(1)}, u32[]{:S(2)}, u32[]{:S(2)}) %collective-permute-start.9) | collective-permute-done | bytes 131104 | tf_op jit(solution)/shard_map/ppermute | solution.py:548
  51.3 3.3 %collective-permute-start.11 = (bf16[32,2176]{1,0:T(8,128)(2,1)S(1)}, bf16[32,2176]{1,0:T(8,128)(2,1)S(1)}, u32[]{:S(2)}, u32[]{:S(2)}) collective-permute-start(bf16[32,2176]{1,0:T(8,128)(2,1)S(1)} %get-tuple-element.75.refs_1_), channel_id=1, source_target_pairs={{0,1},{1,2},{2,3},{3,0},{4,5},{5,6},{6,7},{7,4},{8,9},{9,10},{10,1... | collective-permute-start | bytes 417800 | tf_op jit(solution)/shard_map/ppermute | solution.py:548
  54.6 1.6 %collective-permute-start.12 = (bf16[32,2176]{1,0:T(8,128)(2,1)S(1)}, bf16[32,2176]{1,0:T(8,128)(2,1)S(1)}, u32[]{:S(2)}, u32[]{:S(2)}) collective-permute-start(bf16[32,2176]{1,0:T(8,128)(2,1)S(1)} %get-tuple-element.75.refs_1_), channel_id=1, source_target_pairs={{0,2},{1,3},{2,0},{3,1},{4,6},{5,7},{6,4},{7,5},{8,10},{9,11},{10,... | collective-permute-start | bytes 417800 | tf_op jit(solution)/shard_map/ppermute | solution.py:548
  56.3 0.8 collective-permute-start.13
  57.1 1.1 shard_map.191.refs_5_.w_gate
  58.2 5.5 %copy-done = bf16[2048,3840]{1,0:T(8,128)(2,1)S(1)} copy-done((bf16[2048,3840]{1,0:T(8,128)(2,1)S(1)}, bf16[2048,3840]{1,0:T(8,128)(2,1)}, u32[]{:S(2)}) %copy-start) | copy-done | bytes 15728664
  63.6 1.1 shard_map.192.refs_6_.w_up
  64.9 2.8 %shard_map.193 = (f32[64,3968]{1,0:T(8,128)S(1)}, bf16[64,3968]{1,0:T(8,128)(2,1)S(1)}, bf16[128,2176]{1,0:T(8,128)(2,1)S(1)}) custom-call(bf16[128,128]{1,0:T(8,128)(2,1)S(1)} %get-tuple-element.74.refs_0_, bf16[32,2176]{1,0:T(8,128)(2,1)S(1)} %get-tuple-element.75.refs_1_, bf16[32,2176]{1,0:T(8,128)(2,1)S(1)} %collective-permute-done.11.refs_2_, ...), custom_call_target="tpu_custom_call" | custom-call | flops 2013265920 | tf_op jit(solution)/shard_map/pallas_call | solution.py:48
  67.8 2.8 %shard_map.195 = (f32[64,3840]{1,0:T(8,128)S(1)}, bf16[64,3840]{1,0:T(8,128)(2,1)S(1)}) custom-call(bf16[128,2176]{1,0:T(8,128)(2,1)S(1)} %get-tuple-element.80.ordered, bf16[2048,3840]{1,0:T(8,128)(2,1)S(1)} %shard_map.191.refs_5_.w_gate, bf16[2048,3840]{1,0:T(8,128)(2,1)S(1)} %shard_map.192.refs_6_.w_up), custom_call_target="tpu_custom_call" | custom-call | flops 2013265920 | tf_op jit(solution)/shard_map/pallas_call | solution.py:48
  70.6 0.6 collective-permute-start.16
  71.3 1.6 %collective-permute-start.15 = (bf16[32,3968]{1,0:T(8,128)(2,1)S(1)}, bf16[32,3968]{1,0:T(8,128)(2,1)S(1)}, u32[]{:S(2)}, u32[]{:S(2)}) collective-permute-start(bf16[32,3968]{1,0:T(8,128)(2,1)S(1)} %get-tuple-element.79), channel_id=1, source_target_pairs={{0,8},{4,12},{8,0},{12,4},{1,9},{5,13},{9,1},{13,5},{2,10},{6,14},... | collective-permute-start | bytes 761864 | tf_op jit(solution)/shard_map/ppermute | solution.py:544
  73.0 1.3 %collective-permute-start.17 = (bf16[32,3840]{1,0:T(8,128)(2,1)S(1)}, bf16[32,3840]{1,0:T(8,128)(2,1)S(1)}, u32[]{:S(2)}, u32[]{:S(2)}) collective-permute-start(bf16[32,3840]{1,0:T(8,128)(2,1)S(1)} %get-tuple-element.83.refs_1_), channel_id=1, source_target_pairs={{0,8},{4,12},{8,0},{12,4},{1,9},{5,13},{9,1},{13,5},{2,10},{6,14},... | collective-permute-start | bytes 737288 | tf_op jit(solution)/shard_map/ppermute | solution.py:544
  74.4 5.5 %shard_map.197.refs_1_.refs_5_ = bf16[3840,2048]{1,0:T(8,128)(2,1)S(1)} custom-call(bf16[3840,2048]{1,0:T(8,128)(2,1)} %refs_0_.11, bf16[32,3840]{1,0:T(8,128)(2,1)S(1)} %get-tuple-element.83.refs_1_), custom_call_target="tpu_custom_call" | custom-call | bytes 31457280 | tf_op jit(solution)/shard_map/pallas_call | solution.py:76
  80.6 1.6 %collective-permute-start.21 = (bf16[32,1920]{1,0:T(8,128)(2,1)S(1)}, bf16[32,1920]{1,0:T(8,128)(2,1)S(1)}, u32[]{:S(2)}, u32[]{:S(2)}) collective-permute-start(bf16[32,1920]{1,0:T(8,128)(2,1)S(1)} %get-tuple-element.86.refs_1_), channel_id=1, source_target_pairs={{0,8},{4,12},{8,0},{12,4},{1,9},{5,13},{9,1},{13,5},{2,10},{6,14},... | collective-permute-start | bytes 368648 | tf_op jit(solution)/shard_map/ppermute | solution.py:544
  82.1 3.5 %collective-permute-done.17.refs_0_ = bf16[32,3840]{1,0:T(8,128)(2,1)S(1)} collective-permute-done((bf16[32,3840]{1,0:T(8,128)(2,1)S(1)}, bf16[32,3840]{1,0:T(8,128)(2,1)S(1)}, u32[]{:S(2)}, u32[]{:S(2)}) %collective-permute-start.17) | collective-permute-done | bytes 245792 | tf_op jit(solution)/shard_map/ppermute | solution.py:544
  85.8 1.6 %collective-permute-start.18 = (bf16[32,1920]{1,0:T(8,128)(2,1)S(1)}, bf16[32,1920]{1,0:T(8,128)(2,1)S(1)}, u32[]{:S(2)}, u32[]{:S(2)}) collective-permute-start(bf16[32,1920]{1,0:T(8,128)(2,1)S(1)} %shard_map.199.refs_1_), channel_id=1, source_target_pairs={{0,8},{4,12},{8,0},{12,4},{1,9},{5,13},{9,1},{13,5},{2,10},{6,14},... | collective-permute-start | bytes 368648 | tf_op jit(solution)/shard_map/ppermute | solution.py:544
  87.4 0.6 collective-permute-done.21.refs_2_
  88.4 2.3 %collective-permute-done.18.refs_2_ = bf16[32,1920]{1,0:T(8,128)(2,1)S(1)} collective-permute-done((bf16[32,1920]{1,0:T(8,128)(2,1)S(1)}, bf16[32,1920]{1,0:T(8,128)(2,1)S(1)}, u32[]{:S(2)}, u32[]{:S(2)}) %collective-permute-start.18) | collective-permute-done | bytes 122912 | tf_op jit(solution)/shard_map/ppermute | solution.py:544
  90.8 1.4 %shard_map.200.refs_6_ = f32[128,2048]{1,0:T(8,128)S(1)} custom-call(bf16[128,128]{1,0:T(8,128)(2,1)S(1)} %get-tuple-element.73.refs_0_, bf16[32,1920]{1,0:T(8,128)(2,1)S(1)} %get-tuple-element.86.refs_1_, bf16[32,1920]{1,0:T(8,128)(2,1)S(1)} %collective-permute-done.21.refs_2_, bf16[32,1920]{1,0:T(8,128)(2,1)S(1)} %collective-permute-done.22.refs_3_, ...), custom_call_target="tpu_custom_call" | custom-call | flops 1006632960 | tf_op jit(solution)/shard_map/pallas_call | solution.py:48
  92.2 1.4 %shard_map.201 = (f32[32,2048]{1,0:T(8,128)S(1)}, bf16[32,2048]{1,0:T(8,128)(2,1)S(1)}, bf16[32,2048]{1,0:T(8,128)(2,1)S(1)}, bf16[32,2048]{1,0:T(8,128)(2,1)S(1)}) custom-call(bf16[128,128]{1,0:T(8,128)(2,1)S(1)} %get-tuple-element.73.refs_0_, bf16[32,1920]{1,0:T(8,128)(2,1)S(1)} %shard_map.199.refs_1_, ...), custom_call_target="tpu_custom_call" | custom-call | flops 1006632960 | tf_op jit(solution)/shard_map/pallas_call | solution.py:48
  93.6 3.5 %collective-permute-start.24 = (bf16[32,2048]{1,0:T(8,128)(2,1)S(1)}, bf16[32,2048]{1,0:T(8,128)(2,1)S(1)}, u32[]{:S(2)}, u32[]{:S(2)}) collective-permute-start(bf16[32,2048]{1,0:T(8,128)(2,1)S(1)} %get-tuple-element.88), channel_id=1, source_target_pairs={{0,1},{1,2},{2,3},{3,0},{4,5},{5,6},{6,7},{7,4},{8,9},{9,10},{10,1... | collective-permute-start | bytes 393224 | tf_op jit(solution)/shard_map/ppermute | solution.py:548
  97.1 2.0 %collective-permute-start.25 = (bf16[32,2048]{1,0:T(8,128)(2,1)S(1)}, bf16[32,2048]{1,0:T(8,128)(2,1)S(1)}, u32[]{:S(2)}, u32[]{:S(2)}) collective-permute-start(bf16[32,2048]{1,0:T(8,128)(2,1)S(1)} %get-tuple-element.89), channel_id=1, source_target_pairs={{0,2},{1,3},{2,0},{3,1},{4,6},{5,7},{6,4},{7,5},{8,10},{9,11},{10,... | collective-permute-start | bytes 393224 | tf_op jit(solution)/shard_map/ppermute | solution.py:548
  99.5 3.4 %collective-permute-done.24.refs_0_ = bf16[32,2048]{1,0:T(8,128)(2,1)S(1)} collective-permute-done((bf16[32,2048]{1,0:T(8,128)(2,1)S(1)}, bf16[32,2048]{1,0:T(8,128)(2,1)S(1)}, u32[]{:S(2)}, u32[]{:S(2)}) %collective-permute-start.24) | collective-permute-done | bytes 131104 | tf_op jit(solution)/shard_map/ppermute | solution.py:548
  103.0 5.4 %collective-permute-done.25.refs_1_ = bf16[32,2048]{1,0:T(8,128)(2,1)S(1)} collective-permute-done((bf16[32,2048]{1,0:T(8,128)(2,1)S(1)}, bf16[32,2048]{1,0:T(8,128)(2,1)S(1)}, u32[]{:S(2)}, u32[]{:S(2)}) %collective-permute-start.25) | collective-permute-done | bytes 131104 | tf_op jit(solution)/shard_map/ppermute | solution.py:548
  108.4 0.7 shard_map.202
  (74 shorter events, 3.7 us)
Async XLA Ops:
  1.2 0.7 copy-start.3
  1.8 9.0 %copy-start.4 = (bf16[32,2176]{1,0:T(8,128)(2,1)S(1)}, bf16[32,2176]{1,0:T(8,128)(2,1)}, u32[]{:S(2)}) copy-start(bf16[32,2176]{1,0:T(8,128)(2,1)} %copy-done.3) | copy-start | bytes 417796
  1.8 8.1 %collective-permute-start = (bf16[32,2176]{1,0:T(8,128)(2,1)S(1)}, bf16[32,2176]{1,0:T(8,128)(2,1)S(1)}, u32[]{:S(2)}, u32[]{:S(2)}) collective-permute-start(bf16[32,2176]{1,0:T(8,128)(2,1)S(1)} %get-tuple-element.49), channel_id=1, source_target_pairs={{0,8},{4,12},{8,0},{12,4},{1,9},{5,13},{9,1},{13,5},{2,10},{6,14},... | collective-permute-start | bytes 417800 | tf_op jit(solution)/shard_map/ppermute | solution.py:544
  4.8 5.2 %collective-permute-start.1 = (bf16[32,2176]{1,0:T(8,128)(2,1)S(1)}, bf16[32,2176]{1,0:T(8,128)(2,1)S(1)}, u32[]{:S(2)}, u32[]{:S(2)}) collective-permute-start(bf16[32,2176]{1,0:T(8,128)(2,1)S(1)} %get-tuple-element.50), channel_id=1, source_target_pairs={{0,4},{4,0},{8,12},{12,8},{1,5},{5,1},{9,13},{13,9},{2,6},{6,2},{1... | collective-permute-start | bytes 417800 | tf_op jit(solution)/shard_map/ppermute | solution.py:544
  4.8 6.0 %collective-permute-start.2 = (bf16[32,2176]{1,0:T(8,128)(2,1)S(1)}, bf16[32,2176]{1,0:T(8,128)(2,1)S(1)}, u32[]{:S(2)}, u32[]{:S(2)}) collective-permute-start(bf16[32,2176]{1,0:T(8,128)(2,1)S(1)} %get-tuple-element.51), channel_id=1, source_target_pairs={{0,12},{4,8},{8,4},{12,0},{1,13},{5,9},{9,5},{13,1},{2,14},{6,10},... | collective-permute-start | bytes 417800 | tf_op jit(solution)/shard_map/ppermute | solution.py:544
  4.9 8.9 %copy-start.7 = (s32[4]{0:T(128)S(1)}, s32[4]{0:T(128)}, u32[]{:S(2)}) copy-start(s32[4]{0:T(128)} %path_pages.1) | copy-start | bytes 52
  9.0 8.6 %copy-start.8 = (bf16[2048]{0:T(1024)(128)(2,1)S(1)}, bf16[2048]{0:T(1024)(128)(2,1)}, u32[]{:S(2)}) copy-start(bf16[2048]{0:T(1024)(128)(2,1)} %param.22) | copy-start | bytes 12292
  9.0 8.6 %copy-start.9 = (bf16[256]{0:T(256)(128)(2,1)S(1)}, bf16[256]{0:T(256)(128)(2,1)}, u32[]{:S(2)}) copy-start(bf16[256]{0:T(256)(128)(2,1)} %param.24) | copy-start | bytes 1540
  9.0 8.6 %copy-start.10 = (bf16[256]{0:T(256)(128)(2,1)S(1)}, bf16[256]{0:T(256)(128)(2,1)}, u32[]{:S(2)}) copy-start(bf16[256]{0:T(256)(128)(2,1)} %param.26) | copy-start | bytes 1540
  9.0 8.7 %copy-start.1 = (bf16[64,128,256]{2,1,0:T(8,128)(2,1)S(1)}, bf16[64,128,256]{2,1,0:T(8,128)(2,1)}, u32[]{:S(2)}) copy-start(bf16[64,128,256]{2,1,0:T(8,128)(2,1)} %refs_0_.7) | copy-start | bytes 12582916
  9.1 8.7 %copy-start.2 = (bf16[64,128,256]{2,1,0:T(8,128)(2,1)S(1)}, bf16[64,128,256]{2,1,0:T(8,128)(2,1)}, u32[]{:S(2)}) copy-start(bf16[64,128,256]{2,1,0:T(8,128)(2,1)} %refs_1_.3) | copy-start | bytes 12582916
  10.8 7.6 %copy-start.6 = (s32[4,32]{1,0:T(4,128)S(1)}, s32[4,32]{1,0:T(4,128)}, u32[]{:S(2)}) copy-start(s32[4,32]{1,0:T(4,128)} %page_table.1) | copy-start | bytes 1540
  10.8 11.6 %copy-start.5 = (f32[128,128]{1,0:T(8,128)S(1)}, f32[128,128]{1,0:T(8,128)}, u32[]{:S(2)}) copy-start(f32[128,128]{1,0:T(8,128)} %constant.24.clone.refs_6_) | copy-start | bytes 196612
  13.3 2.3 %collective-permute-start.3 = (f32[64,2688]{1,0:T(8,128)S(1)}, f32[64,2688]{1,0:T(8,128)S(1)}, u32[]{:S(2)}, u32[]{:S(2)}) collective-permute-start(f32[64,2688]{1,0:T(8,128)S(1)} %get-tuple-element.58), channel_id=1, source_target_pairs={{0,4},{4,0},{8,12},{12,8},{1,5},{5,1},{9,13},{13,9},{2,6},{6,2},{1... | collective-permute-start | bytes 2064392 | tf_op jit(solution)/shard_map/ppermute | solution.py:544
  15.6 19.3 %slice-start.4 = ((s8[8388608]{0:T(1024)(128)(4,1)}), s8[4194304]{0:T(1024)(128)(4,1)S(1)}, s32[]{:S(2)}) async-start(s8[8388608]{0:T(1024)(128)(4,1)} %bitcast.7), calls=%async_computation.4 | async-start | bytes 8388608
  15.7 6.7 %collective-permute-start.4 = (bf16[32,2688]{1,0:T(8,128)(2,1)S(1)}, bf16[32,2688]{1,0:T(8,128)(2,1)S(1)}, u32[]{:S(2)}, u32[]{:S(2)}) collective-permute-start(bf16[32,2688]{1,0:T(8,128)(2,1)S(1)} %get-tuple-element.59._.refs_2_), channel_id=1, source_target_pairs={{0,8},{4,12},{8,0},{12,4},{1,9},{5,13},{9,1},{13,5},{2,10},{6,14},... | collective-permute-start | bytes 516104 | tf_op jit(solution)/shard_map/ppermute | solution.py:544
  17.8 17.2 %slice-start.5 = ((s8[8388608]{0:T(1024)(128)(4,1)}), s8[4194304]{0:T(1024)(128)(4,1)S(1)}, s32[]{:S(2)}) async-start(s8[8388608]{0:T(1024)(128)(4,1)} %bitcast.7), calls=%async_computation.5 | async-start | bytes 8388608
  22.4 34.7 %slice-start = ((s8[15728640]{0:T(1024)(128)(4,1)}), s8[3145728]{0:T(1024)(128)(4,1)S(1)}, s32[]{:S(2)}) async-start(s8[15728640]{0:T(1024)(128)(4,1)} %bitcast.5), calls=%async_computation | async-start | bytes 6291456
  22.4 34.7 %slice-start.1 = ((s8[15728640]{0:T(1024)(128)(4,1)}), s8[4194304]{0:T(1024)(128)(4,1)S(1)}, s32[]{:S(2)}) async-start(s8[15728640]{0:T(1024)(128)(4,1)} %bitcast.5), calls=%async_computation.1 | async-start | bytes 8388608
  29.9 27.2 %slice-start.2 = ((s8[15728640]{0:T(1024)(128)(4,1)}), s8[4194304]{0:T(1024)(128)(4,1)S(1)}, s32[]{:S(2)}) async-start(s8[15728640]{0:T(1024)(128)(4,1)} %bitcast.5), calls=%async_computation.2 | async-start | bytes 8388608
  29.9 5.0 %collective-permute-start.5 = (bf16[32,2048]{1,0:T(8,128)(2,1)S(1)}, bf16[32,2048]{1,0:T(8,128)(2,1)S(1)}, u32[]{:S(2)}, u32[]{:S(2)}) collective-permute-start(bf16[32,2048]{1,0:T(8,128)(2,1)S(1)} %shard_map.187.refs_1_.refs_0_), channel_id=1, source_target_pairs={{0,8},{4,12},{8,0},{12,4},{1,9},{5,13},{9,1},{13,5},{2,10},{6,14},... | collective-permute-start | bytes 393224 | tf_op jit(solution)/shard_map/ppermute | solution.py:544
  31.7 3.8 %collective-permute-start.6 = (bf16[32,2048]{1,0:T(8,128)(2,1)S(1)}, bf16[32,2048]{1,0:T(8,128)(2,1)S(1)}, u32[]{:S(2)}, u32[]{:S(2)}) collective-permute-start(bf16[32,2048]{1,0:T(8,128)(2,1)S(1)} %shard_map.187.refs_1_.refs_0_), channel_id=1, source_target_pairs={{0,4},{4,0},{8,12},{12,8},{1,5},{5,1},{9,13},{13,9},{2,6},{6,2},{1... | collective-permute-start | bytes 393224 | tf_op jit(solution)/shard_map/ppermute | solution.py:544
  35.0 1.3 %collective-permute-start.7 = (bf16[32,2048]{1,0:T(8,128)(2,1)S(1)}, bf16[32,2048]{1,0:T(8,128)(2,1)S(1)}, u32[]{:S(2)}, u32[]{:S(2)}) collective-permute-start(bf16[32,2048]{1,0:T(8,128)(2,1)S(1)} %collective-permute-done.5.refs_1_), channel_id=1, source_target_pairs={{0,4},{4,0},{8,12},{12,8},{1,5},{5,1},{9,13},{13,9},{2,6},{6,2},{1... | collective-permute-start | bytes 393224 | tf_op jit(solution)/shard_map/ppermute | solution.py:544
  36.3 20.8 %slice-start.3 = ((s8[15728640]{0:T(1024)(128)(4,1)}), s8[4194304]{0:T(1024)(128)(4,1)S(1)}, s32[]{:S(2)}) async-start(s8[15728640]{0:T(1024)(128)(4,1)} %bitcast.5), calls=%async_computation.3 | async-start | bytes 8388608
  37.7 8.3 %collective-permute-start.8 = (bf16[32,2048]{1,0:T(8,128)(2,1)S(1)}, bf16[32,2048]{1,0:T(8,128)(2,1)S(1)}, u32[]{:S(2)}, u32[]{:S(2)}) collective-permute-start(bf16[32,2048]{1,0:T(8,128)(2,1)S(1)} %get-tuple-element.69), channel_id=1, source_target_pairs={{0,1},{1,2},{2,3},{3,0},{4,5},{5,6},{6,7},{7,4},{8,9},{9,10},{10,1... | collective-permute-start | bytes 393224 | tf_op jit(solution)/shard_map/ppermute | solution.py:548
  39.6 11.5 %collective-permute-start.9 = (bf16[32,2048]{1,0:T(8,128)(2,1)S(1)}, bf16[32,2048]{1,0:T(8,128)(2,1)S(1)}, u32[]{:S(2)}, u32[]{:S(2)}) collective-permute-start(bf16[32,2048]{1,0:T(8,128)(2,1)S(1)} %get-tuple-element.70), channel_id=1, source_target_pairs={{0,2},{1,3},{2,0},{3,1},{4,6},{5,7},{6,4},{7,5},{8,10},{9,11},{10,... | collective-permute-start | bytes 393224 | tf_op jit(solution)/shard_map/ppermute | solution.py:548
  42.2 9.0 %collective-permute-start.10 = (bf16[32,2048]{1,0:T(8,128)(2,1)S(1)}, bf16[32,2048]{1,0:T(8,128)(2,1)S(1)}, u32[]{:S(2)}, u32[]{:S(2)}) collective-permute-start(bf16[32,2048]{1,0:T(8,128)(2,1)S(1)} %get-tuple-element.71), channel_id=1, source_target_pairs={{0,3},{1,0},{2,1},{3,2},{4,7},{5,4},{6,5},{7,6},{8,11},{9,8},{10,9... | collective-permute-start | bytes 393224 | tf_op jit(solution)/shard_map/ppermute | solution.py:548
  51.3 13.4 %collective-permute-start.11 = (bf16[32,2176]{1,0:T(8,128)(2,1)S(1)}, bf16[32,2176]{1,0:T(8,128)(2,1)S(1)}, u32[]{:S(2)}, u32[]{:S(2)}) collective-permute-start(bf16[32,2176]{1,0:T(8,128)(2,1)S(1)} %get-tuple-element.75.refs_1_), channel_id=1, source_target_pairs={{0,1},{1,2},{2,3},{3,0},{4,5},{5,6},{6,7},{7,4},{8,9},{9,10},{10,1... | collective-permute-start | bytes 417800 | tf_op jit(solution)/shard_map/ppermute | solution.py:548
  54.6 10.3 %collective-permute-start.12 = (bf16[32,2176]{1,0:T(8,128)(2,1)S(1)}, bf16[32,2176]{1,0:T(8,128)(2,1)S(1)}, u32[]{:S(2)}, u32[]{:S(2)}) collective-permute-start(bf16[32,2176]{1,0:T(8,128)(2,1)S(1)} %get-tuple-element.75.refs_1_), channel_id=1, source_target_pairs={{0,2},{1,3},{2,0},{3,1},{4,6},{5,7},{6,4},{7,5},{8,10},{9,11},{10,... | collective-permute-start | bytes 417800 | tf_op jit(solution)/shard_map/ppermute | solution.py:548
  56.3 8.7 %collective-permute-start.13 = (bf16[32,2176]{1,0:T(8,128)(2,1)S(1)}, bf16[32,2176]{1,0:T(8,128)(2,1)S(1)}, u32[]{:S(2)}, u32[]{:S(2)}) collective-permute-start(bf16[32,2176]{1,0:T(8,128)(2,1)S(1)} %get-tuple-element.75.refs_1_), channel_id=1, source_target_pairs={{0,3},{1,0},{2,1},{3,2},{4,7},{5,4},{6,5},{7,6},{8,11},{9,8},{10,9... | collective-permute-start | bytes 417800 | tf_op jit(solution)/shard_map/ppermute | solution.py:548
  58.2 5.5 %copy-start = (bf16[2048,3840]{1,0:T(8,128)(2,1)S(1)}, bf16[2048,3840]{1,0:T(8,128)(2,1)}, u32[]{:S(2)}) copy-start(bf16[2048,3840]{1,0:T(8,128)(2,1)} %refs_0_.10) | copy-start | bytes 47185924
  67.8 3.4 %collective-permute-start.14 = (bf16[64,3968]{1,0:T(8,128)(2,1)S(1)}, bf16[64,3968]{1,0:T(8,128)(2,1)S(1)}, u32[]{:S(2)}, u32[]{:S(2)}) collective-permute-start(bf16[64,3968]{1,0:T(8,128)(2,1)S(1)} %get-tuple-element.77), channel_id=1, source_target_pairs={{0,4},{4,0},{8,12},{12,8},{1,5},{5,1},{9,13},{13,9},{2,6},{6,2},{1... | collective-permute-start | bytes 1523720 | tf_op jit(solution)/shard_map/ppermute | solution.py:544
  70.6 2.3 %collective-permute-start.16 = (bf16[64,3840]{1,0:T(8,128)(2,1)S(1)}, bf16[64,3840]{1,0:T(8,128)(2,1)S(1)}, u32[]{:S(2)}, u32[]{:S(2)}) collective-permute-start(bf16[64,3840]{1,0:T(8,128)(2,1)S(1)} %get-tuple-element.82), channel_id=1, source_target_pairs={{0,4},{4,0},{8,12},{12,8},{1,5},{5,1},{9,13},{13,9},{2,6},{6,2},{1... | collective-permute-start | bytes 1474568 | tf_op jit(solution)/shard_map/ppermute | solution.py:544
  71.3 9.1 %collective-permute-start.15 = (bf16[32,3968]{1,0:T(8,128)(2,1)S(1)}, bf16[32,3968]{1,0:T(8,128)(2,1)S(1)}, u32[]{:S(2)}, u32[]{:S(2)}) collective-permute-start(bf16[32,3968]{1,0:T(8,128)(2,1)S(1)} %get-tuple-element.79), channel_id=1, source_target_pairs={{0,8},{4,12},{8,0},{12,4},{1,9},{5,13},{9,1},{13,5},{2,10},{6,14},... | collective-permute-start | bytes 761864 | tf_op jit(solution)/shard_map/ppermute | solution.py:544
  73.0 12.6 %collective-permute-start.17 = (bf16[32,3840]{1,0:T(8,128)(2,1)S(1)}, bf16[32,3840]{1,0:T(8,128)(2,1)S(1)}, u32[]{:S(2)}, u32[]{:S(2)}) collective-permute-start(bf16[32,3840]{1,0:T(8,128)(2,1)S(1)} %get-tuple-element.83.refs_1_), channel_id=1, source_target_pairs={{0,8},{4,12},{8,0},{12,4},{1,9},{5,13},{9,1},{13,5},{2,10},{6,14},... | collective-permute-start | bytes 737288 | tf_op jit(solution)/shard_map/ppermute | solution.py:544
  80.6 7.3 %collective-permute-start.21 = (bf16[32,1920]{1,0:T(8,128)(2,1)S(1)}, bf16[32,1920]{1,0:T(8,128)(2,1)S(1)}, u32[]{:S(2)}, u32[]{:S(2)}) collective-permute-start(bf16[32,1920]{1,0:T(8,128)(2,1)S(1)} %get-tuple-element.86.refs_1_), channel_id=1, source_target_pairs={{0,8},{4,12},{8,0},{12,4},{1,9},{5,13},{9,1},{13,5},{2,10},{6,14},... | collective-permute-start | bytes 368648 | tf_op jit(solution)/shard_map/ppermute | solution.py:544
  85.8 4.9 %collective-permute-start.18 = (bf16[32,1920]{1,0:T(8,128)(2,1)S(1)}, bf16[32,1920]{1,0:T(8,128)(2,1)S(1)}, u32[]{:S(2)}, u32[]{:S(2)}) collective-permute-start(bf16[32,1920]{1,0:T(8,128)(2,1)S(1)} %shard_map.199.refs_1_), channel_id=1, source_target_pairs={{0,8},{4,12},{8,0},{12,4},{1,9},{5,13},{9,1},{13,5},{2,10},{6,14},... | collective-permute-start | bytes 368648 | tf_op jit(solution)/shard_map/ppermute | solution.py:544
  87.4 3.4 %collective-permute-start.22 = (bf16[32,1920]{1,0:T(8,128)(2,1)S(1)}, bf16[32,1920]{1,0:T(8,128)(2,1)S(1)}, u32[]{:S(2)}, u32[]{:S(2)}) collective-permute-start(bf16[32,1920]{1,0:T(8,128)(2,1)S(1)} %get-tuple-element.86.refs_1_), channel_id=1, source_target_pairs={{0,4},{4,0},{8,12},{12,8},{1,5},{5,1},{9,13},{13,9},{2,6},{6,2},{1... | collective-permute-start | bytes 368648 | tf_op jit(solution)/shard_map/ppermute | solution.py:544
  87.9 2.8 %collective-permute-start.23 = (bf16[32,1920]{1,0:T(8,128)(2,1)S(1)}, bf16[32,1920]{1,0:T(8,128)(2,1)S(1)}, u32[]{:S(2)}, u32[]{:S(2)}) collective-permute-start(bf16[32,1920]{1,0:T(8,128)(2,1)S(1)} %collective-permute-done.21.refs_2_), channel_id=1, source_target_pairs={{0,4},{4,0},{8,12},{12,8},{1,5},{5,1},{9,13},{13,9},{2,6},{6,2},{1... | collective-permute-start | bytes 368648 | tf_op jit(solution)/shard_map/ppermute | solution.py:544
  87.9 4.2 %collective-permute-start.19 = (bf16[32,1920]{1,0:T(8,128)(2,1)S(1)}, bf16[32,1920]{1,0:T(8,128)(2,1)S(1)}, u32[]{:S(2)}, u32[]{:S(2)}) collective-permute-start(bf16[32,1920]{1,0:T(8,128)(2,1)S(1)} %shard_map.199.refs_1_), channel_id=1, source_target_pairs={{0,4},{4,0},{8,12},{12,8},{1,5},{5,1},{9,13},{13,9},{2,6},{6,2},{1... | collective-permute-start | bytes 368648 | tf_op jit(solution)/shard_map/ppermute | solution.py:544
  90.7 1.4 %collective-permute-start.20 = (bf16[32,1920]{1,0:T(8,128)(2,1)S(1)}, bf16[32,1920]{1,0:T(8,128)(2,1)S(1)}, u32[]{:S(2)}, u32[]{:S(2)}) collective-permute-start(bf16[32,1920]{1,0:T(8,128)(2,1)S(1)} %collective-permute-done.18.refs_2_), channel_id=1, source_target_pairs={{0,4},{4,0},{8,12},{12,8},{1,5},{5,1},{9,13},{13,9},{2,6},{6,2},{1... | collective-permute-start | bytes 368648 | tf_op jit(solution)/shard_map/ppermute | solution.py:544
  93.6 9.4 %collective-permute-start.24 = (bf16[32,2048]{1,0:T(8,128)(2,1)S(1)}, bf16[32,2048]{1,0:T(8,128)(2,1)S(1)}, u32[]{:S(2)}, u32[]{:S(2)}) collective-permute-start(bf16[32,2048]{1,0:T(8,128)(2,1)S(1)} %get-tuple-element.88), channel_id=1, source_target_pairs={{0,1},{1,2},{2,3},{3,0},{4,5},{5,6},{6,7},{7,4},{8,9},{9,10},{10,1... | collective-permute-start | bytes 393224 | tf_op jit(solution)/shard_map/ppermute | solution.py:548
  97.1 11.3 %collective-permute-start.25 = (bf16[32,2048]{1,0:T(8,128)(2,1)S(1)}, bf16[32,2048]{1,0:T(8,128)(2,1)S(1)}, u32[]{:S(2)}, u32[]{:S(2)}) collective-permute-start(bf16[32,2048]{1,0:T(8,128)(2,1)S(1)} %get-tuple-element.89), channel_id=1, source_target_pairs={{0,2},{1,3},{2,0},{3,1},{4,6},{5,7},{6,4},{7,5},{8,10},{9,11},{10,... | collective-permute-start | bytes 393224 | tf_op jit(solution)/shard_map/ppermute | solution.py:548
  99.1 9.3 %collective-permute-start.26 = (bf16[32,2048]{1,0:T(8,128)(2,1)S(1)}, bf16[32,2048]{1,0:T(8,128)(2,1)S(1)}, u32[]{:S(2)}, u32[]{:S(2)}) collective-permute-start(bf16[32,2048]{1,0:T(8,128)(2,1)S(1)} %get-tuple-element.90), channel_id=1, source_target_pairs={{0,3},{1,0},{2,1},{3,2},{4,7},{5,4},{6,5},{7,6},{8,11},{9,8},{10,9... | collective-permute-start | bytes 393224 | tf_op jit(solution)/shard_map/ppermute | solution.py:548

commit v4 on v3

--- a/solution.py
+++ b/solution.py
@@ -152,12 +152,21 @@
     ).astype(BF16)
 
 
+def split_terms(values, axis):
+    high = values.astype(BF16)
+    rest = values - high.astype(F32)
+    middle = rest.astype(BF16)
+    low = (rest - middle.astype(F32)).astype(BF16)
+    return jnp.concatenate([high, middle, low], axis)
+
+
 def dot32(left, right):
     return jnp.dot(left, right, preferred_element_type=F32)
 
 
 def send_kernel(chips, hidden, parents, *refs):
-    blocks, (listed, sems) = refs[:-2], refs[-2:]
+    blocks, (begun, listed, sems) = refs[:-3], refs[-3:]
+    begun[...] = jnp.zeros_like(begun)
     place = Place((lax.axis_index("branch"), 0), chips, 1)
     length, width = hidden.shape[0], blocks[0].shape[1] - EXT
     copies = [pltpu.make_async_copy(parents, listed, sems.at[0])]
@@ -304,8 +313,10 @@
 
     queries = rope(stacked(0, heads), heads)
     new_keys = rope(stacked(heads, kv_local), kv_local)
-    turned = jnp.dot(
-        queries, rotation, precision=lax.Precision.HIGHEST, preferred_element_type=F32
+    signs = jnp.where(rotation > 0.0, 1.0, -1.0).astype(BF16)
+    even = 1.0 / math.sqrt(HD)
+    turned = (
+        dot32(split_terms(queries, 1), jnp.concatenate([signs] * 3, 0)) * even
     ).astype(BF16)
     scale = 1.0 / math.sqrt(HD)
     rate = scale * math.log2(math.e)
@@ -358,8 +369,8 @@
         sums = lax.fori_loop(0, chunks, second_pass, jnp.zeros((8, rows), F32), unroll=unroll)
         own = jnp.exp2(own_row * rate - top_rate)
         whole = jnp.sum(sums, 0, keepdims=True) + own
-        unturned = jnp.dot(
-            rotation, mixed[...], precision=lax.Precision.HIGHEST, preferred_element_type=F32
+        unturned = (
+            dot32(jnp.concatenate([signs] * 3, 1), split_terms(mixed[...], 0)) * even
         )
         value_at = (heads + kv_local + kv_at) * HD
         value_now = jnp.concatenate([packed[:, value_at : value_at + HD]] * group_size, 0)
@@ -552,9 +563,9 @@
             None
         ]
 
-    outgoing = call(
+    *outgoing, begun = call(
         functools.partial(send_kernel, chips),
-        [((local_rows, model_cols + EXT), BF16)] * branch_count,
+        [((local_rows, model_cols + EXT), BF16)] * branch_count + [((8, EXT), F32)],
         ["hbm", "hbm"],
         [pltpu.VMEM((1, local_rows), jnp.int32), pltpu.SemaphoreType.DMA((branch_count + 1,))],
         hidden_in,
@@ -565,9 +576,9 @@
     hidden_blocks = [outgoing[0]]
     for block, (chip, core) in zip(outgoing[1:], steps[1:]):
         hidden_blocks.append(over_branch(block, chip, core))
-    wq, wk, wv = fetch([w_query, w_key, w_value], outgoing[0], 44 * MIB)
+    wq, wk, wv = fetch([w_query, w_key, w_value], begun, 44 * MIB)
     keep, send, share, codes = call(
-        functools.partial(qkv_kernel, slots, chips, head_count, 512),
+        functools.partial(qkv_kernel, slots, chips, head_count, 1024),
         [
             ((chips * slots, packed_cols + EXT), F32),
             ((chips * slots, packed_cols + EXT), F32),
@@ -656,7 +667,7 @@
 
     gathered = gather_branch(attention)
     (w_out_near,) = fetch([w_out], attention)
-    out_width = block_width(model_cols, 512)
+    out_width = block_width(model_cols, 2048)
     mixer, *others = call(
         functools.partial(mixer_kernel, branch_count, out_width),
         [((share_rows, model_cols), F32)] + [((share_rows, model_cols), BF16)] * (head_count - 1),
@@ -693,7 +704,7 @@
             first_gate_kernel,
             head_count,
             counts[0],
-            block_width(counts[0], 768),
+            block_width(counts[0], 1920),
         ),
         gate_outs(2 * counts[0] + EXT) + [((all_rows, model_cols + EXT), BF16)],
         ["vmem"] * (head_count + 3),
@@ -706,7 +717,7 @@
     )
     parts = [(keep, over_branch(send, 0, 1))]
     keep, send = call(
-        functools.partial(next_gate_kernel, cuts[1], counts[1], block_width(counts[1], 768)),
+        functools.partial(next_gate_kernel, cuts[1], counts[1], block_width(counts[1], 1920)),
         gate_outs(2 * counts[1]),
         ["vmem"] * 3,
         [],

time: 110 us -> 108 us (0.982)
    unnamed x34 -> x32, local copies, waits for them, and re-layouts: 6.18 us -> 5.54 us
where the time goes in v4:
time: 108 us
  Pallas kernels  35.5 us (33%)
  waiting for transfers between devices  32.4 us (30%)
  starting transfers between devices  32.1 us (30%)
  local copies, waits for them, and re-layouts  5.56 us (5%)
  other arithmetic  1.81 us (2%)
    pallas_call x16, Pallas kernels, call(): pl.pallas_call(kernel, out_shape=[pltpu.VMEM(shape, kind) if near else ja...  22.7 us
    ppermute x9, starting transfers between devices, over_head(): return lax.ppermute(array, 'head', pairs)  17.5 us
    ppermute x18, waiting for transfers between devices, over_branch(): return lax.ppermute(array, 'branch', pairs)  16.4 us
    ppermute x9, waiting for transfers between devices, over_head(): return lax.ppermute(array, 'head', pairs)  16 us
    ppermute x18, starting transfers between devices, over_branch(): return lax.ppermute(array, 'branch', pairs)  14.6 us
    pallas_call x6, Pallas kernels, fetch(): pl.pallas_call(functools.partial(fetch_kernel, len(arrays)), out_shape=[p...  12.8 us
    unnamed x32, local copies, waits for them, and re-layouts  5.54 us
  transfers between devices with their start and end apart: 27, of which 14 were waited for; matrix products, arithmetic and copies ran while one was open for 2% of the time, Pallas kernels for 17%

profile of v4, /device:TPU:0, one launch (start us, length us, event | category | flops | bytes accessed | tf_op | source)
XLA Modules:
  0.0 107.8 jit_solution(113765253056069020)
XLA Ops:
  0.0 1.2 %shard_map.181 = (bf16[32,2176]{1,0:T(8,128)(2,1)S(1)}, bf16[32,2176]{1,0:T(8,128)(2,1)S(1)}, bf16[32,2176]{1,0:T(8,128)(2,1)S(1)}, bf16[32,2176]{1,0:T(8,128)(2,1)S(1)}, f32[8,128]{1,0:T(8,128)S(1)}) custom-call(bf16[32,8192]{1,0:T(8,128)(2,1)} %hidden.1, s32[1,32]{1,0:T(1,128)} %bitcast.11), custom_call_target="tpu_custom_call" | custom-call | tf_op jit(solution)/shard_map/pallas_call | solution.py:48
  1.2 3.0 %collective-permute-start = (bf16[32,2176]{1,0:T(8,128)(2,1)S(1)}, bf16[32,2176]{1,0:T(8,128)(2,1)S(1)}, u32[]{:S(2)}, u32[]{:S(2)}) collective-permute-start(bf16[32,2176]{1,0:T(8,128)(2,1)S(1)} %get-tuple-element.50), channel_id=1, source_target_pairs={{0,8},{4,12},{8,0},{12,4},{1,9},{5,13},{9,1},{13,5},{2,10},{6,14},... | collective-permute-start | bytes 417800 | tf_op jit(solution)/shard_map/ppermute | solution.py:555
  4.5 4.1 %shard_map.182 = (bf16[2048,2048]{1,0:T(8,128)(2,1)S(1)}, bf16[2048,256]{1,0:T(8,128)(2,1)S(1)}, bf16[2048,256]{1,0:T(8,128)(2,1)S(1)}) custom-call(bf16[2048,2048]{1,0:T(8,128)(2,1)} %refs_0_.6, bf16[2048,256]{1,0:T(8,128)(2,1)} %refs_1_.2, bf16[2048,256]{1,0:T(8,128)(2,1)} %refs_2_.1, f32[8,128]{1,0:T(8,128)} %copy-done.4), custom_call_target="tpu_custom_call" | custom-call | bytes 20971520 | tf_op jit(solution)/shard_map/pallas_call | solution.py:76
  8.6 0.8 dynamic-slice_convert_fusion.1
  9.4 0.8 collective-permute-done.2.refs_4_
  10.2 2.5 %shard_map.183 = (f32[64,2688]{1,0:T(8,128)S(1)}, f32[64,2688]{1,0:T(8,128)S(1)}, bf16[32,2048]{1,0:T(8,128)(2,1)S(1)}, f32[128,128]{1,0:T(8,128)S(1)}) custom-call(s32[2]{0:T(128)S(1)} %pad_add_fusion.refs_0_.spot, bf16[32,2176]{1,0:T(8,128)(2,1)S(1)} %get-tuple-element.49.refs_1_, bf16[32,2176]{1,0:T(8,128)(2,1)S(1)} %collective-permute-done.refs_2_, ...), custom_call_target="tpu_custom_call" | custom-call | flops 1342177280 | tf_op jit(solution)/shard_map/pallas_call | solution.py:48
  13.3 1.7 %collective-permute-done.3.got = f32[64,2688]{1,0:T(8,128)S(1)} collective-permute-done((f32[64,2688]{1,0:T(8,128)S(1)}, f32[64,2688]{1,0:T(8,128)S(1)}, u32[]{:S(2)}, u32[]{:S(2)}) %collective-permute-start.3) | collective-permute-done | bytes 688160 | tf_op jit(solution)/shard_map/ppermute | solution.py:555
  15.1 1.8 %collective-permute-start.4 = (bf16[32,2688]{1,0:T(8,128)(2,1)S(1)}, bf16[32,2688]{1,0:T(8,128)(2,1)S(1)}, u32[]{:S(2)}, u32[]{:S(2)}) collective-permute-start(bf16[32,2688]{1,0:T(8,128)(2,1)S(1)} %get-tuple-element.61._.refs_2_), channel_id=1, source_target_pairs={{0,8},{4,12},{8,0},{12,4},{1,9},{5,13},{9,1},{13,5},{2,10},{6,14},... | collective-permute-start | bytes 516104 | tf_op jit(solution)/shard_map/ppermute | solution.py:555
  17.2 0.6 shard_map.186
  17.8 0.9 shard_map.185
  18.7 3.1 %collective-permute-done.4.refs_1_ = bf16[32,2688]{1,0:T(8,128)(2,1)S(1)} collective-permute-done((bf16[32,2688]{1,0:T(8,128)(2,1)S(1)}, bf16[32,2688]{1,0:T(8,128)(2,1)S(1)}, u32[]{:S(2)}, u32[]{:S(2)}) %collective-permute-start.4) | collective-permute-done | bytes 172064 | tf_op jit(solution)/shard_map/ppermute | solution.py:555
  21.8 7.3 %shard_map.187.refs_1_.refs_0_ = bf16[32,2048]{1,0:T(8,128)(2,1)S(1)} custom-call(f32[32,2688]{1,0:T(8,128)S(1)} %get-tuple-element.63.refs_0_, bf16[32,2688]{1,0:T(8,128)(2,1)S(1)} %collective-permute-done.4.refs_1_, f32[1,2560]{1,0:T(1,128)S(1)} %get-tuple-element.64.refs_2_, f32[32,256]{1,0:T(8,128)S(1)} %get-tuple-element.65.refs_3_, ...), custom_call_target="tpu_custom_call" | custom-call | flops 2147483648 | tf_op jit(solution)/shard_map/pallas_call | solution.py:48
  29.1 1.8 %collective-permute-start.5 = (bf16[32,2048]{1,0:T(8,128)(2,1)S(1)}, bf16[32,2048]{1,0:T(8,128)(2,1)S(1)}, u32[]{:S(2)}, u32[]{:S(2)}) collective-permute-start(bf16[32,2048]{1,0:T(8,128)(2,1)S(1)} %shard_map.187.refs_1_.refs_0_), channel_id=1, source_target_pairs={{0,8},{4,12},{8,0},{12,4},{1,9},{5,13},{9,1},{13,5},{2,10},{6,14},... | collective-permute-start | bytes 393224 | tf_op jit(solution)/shard_map/ppermute | solution.py:555
  30.9 3.2 %collective-permute-done.5.refs_1_ = bf16[32,2048]{1,0:T(8,128)(2,1)S(1)} collective-permute-done((bf16[32,2048]{1,0:T(8,128)(2,1)S(1)}, bf16[32,2048]{1,0:T(8,128)(2,1)S(1)}, u32[]{:S(2)}, u32[]{:S(2)}) %collective-permute-start.5) | collective-permute-done | bytes 131104 | tf_op jit(solution)/shard_map/ppermute | solution.py:555
  34.2 0.6 shard_map.188.refs_4_
  34.8 0.7 collective-permute-done.7.refs_3_
  35.5 1.4 %shard_map.189 = (f32[32,2048]{1,0:T(8,128)S(1)}, bf16[32,2048]{1,0:T(8,128)(2,1)S(1)}, bf16[32,2048]{1,0:T(8,128)(2,1)S(1)}, bf16[32,2048]{1,0:T(8,128)(2,1)S(1)}) custom-call(bf16[128,128]{1,0:T(8,128)(2,1)S(1)} %get-tuple-element.62.order, bf16[32,2048]{1,0:T(8,128)(2,1)S(1)} %shard_map.187.refs_1_.refs_0_, ...), custom_call_target="tpu_custom_call" | custom-call | flops 1073741824 | tf_op jit(solution)/shard_map/pallas_call | solution.py:48
  36.9 1.9 %collective-permute-start.8 = (bf16[32,2048]{1,0:T(8,128)(2,1)S(1)}, bf16[32,2048]{1,0:T(8,128)(2,1)S(1)}, u32[]{:S(2)}, u32[]{:S(2)}) collective-permute-start(bf16[32,2048]{1,0:T(8,128)(2,1)S(1)} %get-tuple-element.71), channel_id=1, source_target_pairs={{0,1},{1,2},{2,3},{3,0},{4,5},{5,6},{6,7},{7,4},{8,9},{9,10},{10,1... | collective-permute-start | bytes 393224 | tf_op jit(solution)/shard_map/ppermute | solution.py:559
  38.8 2.6 %collective-permute-start.9 = (bf16[32,2048]{1,0:T(8,128)(2,1)S(1)}, bf16[32,2048]{1,0:T(8,128)(2,1)S(1)}, u32[]{:S(2)}, u32[]{:S(2)}) collective-permute-start(bf16[32,2048]{1,0:T(8,128)(2,1)S(1)} %get-tuple-element.72), channel_id=1, source_target_pairs={{0,2},{1,3},{2,0},{3,1},{4,6},{5,7},{6,4},{7,5},{8,10},{9,11},{10,... | collective-permute-start | bytes 393224 | tf_op jit(solution)/shard_map/ppermute | solution.py:559
  41.4 1.3 %collective-permute-start.10 = (bf16[32,2048]{1,0:T(8,128)(2,1)S(1)}, bf16[32,2048]{1,0:T(8,128)(2,1)S(1)}, u32[]{:S(2)}, u32[]{:S(2)}) collective-permute-start(bf16[32,2048]{1,0:T(8,128)(2,1)S(1)} %get-tuple-element.73), channel_id=1, source_target_pairs={{0,3},{1,0},{2,1},{3,2},{4,7},{5,4},{6,5},{7,6},{8,11},{9,8},{10,9... | collective-permute-start | bytes 393224 | tf_op jit(solution)/shard_map/ppermute | solution.py:559
  42.7 0.7 dynamic-slice_convert_fusion
  43.4 1.8 %collective-permute-done.8.refs_0_ = bf16[32,2048]{1,0:T(8,128)(2,1)S(1)} collective-permute-done((bf16[32,2048]{1,0:T(8,128)(2,1)S(1)}, bf16[32,2048]{1,0:T(8,128)(2,1)S(1)}, u32[]{:S(2)}, u32[]{:S(2)}) %collective-permute-start.8) | collective-permute-done | bytes 131104 | tf_op jit(solution)/shard_map/ppermute | solution.py:559
  45.2 5.1 %collective-permute-done.9.refs_1_ = bf16[32,2048]{1,0:T(8,128)(2,1)S(1)} collective-permute-done((bf16[32,2048]{1,0:T(8,128)(2,1)S(1)}, bf16[32,2048]{1,0:T(8,128)(2,1)S(1)}, u32[]{:S(2)}, u32[]{:S(2)}) %collective-permute-start.9) | collective-permute-done | bytes 131104 | tf_op jit(solution)/shard_map/ppermute | solution.py:559
  50.5 3.3 %collective-permute-start.11 = (bf16[32,2176]{1,0:T(8,128)(2,1)S(1)}, bf16[32,2176]{1,0:T(8,128)(2,1)S(1)}, u32[]{:S(2)}, u32[]{:S(2)}) collective-permute-start(bf16[32,2176]{1,0:T(8,128)(2,1)S(1)} %get-tuple-element.77.refs_1_), channel_id=1, source_target_pairs={{0,1},{1,2},{2,3},{3,0},{4,5},{5,6},{6,7},{7,4},{8,9},{9,10},{10,1... | collective-permute-start | bytes 417800 | tf_op jit(solution)/shard_map/ppermute | solution.py:559
  53.9 1.6 %collective-permute-start.12 = (bf16[32,2176]{1,0:T(8,128)(2,1)S(1)}, bf16[32,2176]{1,0:T(8,128)(2,1)S(1)}, u32[]{:S(2)}, u32[]{:S(2)}) collective-permute-start(bf16[32,2176]{1,0:T(8,128)(2,1)S(1)} %get-tuple-element.77.refs_1_), channel_id=1, source_target_pairs={{0,2},{1,3},{2,0},{3,1},{4,6},{5,7},{6,4},{7,5},{8,10},{9,11},{10,... | collective-permute-start | bytes 417800 | tf_op jit(solution)/shard_map/ppermute | solution.py:559
  55.5 0.8 collective-permute-start.13
  56.3 1.1 shard_map.191.refs_5_.w_gate
  57.4 5.5 %copy-done = bf16[2048,3840]{1,0:T(8,128)(2,1)S(1)} copy-done((bf16[2048,3840]{1,0:T(8,128)(2,1)S(1)}, bf16[2048,3840]{1,0:T(8,128)(2,1)}, u32[]{:S(2)}) %copy-start) | copy-done | bytes 15728664
  62.9 1.1 shard_map.192.refs_6_.w_up
  64.1 2.6 %shard_map.193 = (f32[64,3968]{1,0:T(8,128)S(1)}, bf16[64,3968]{1,0:T(8,128)(2,1)S(1)}, bf16[128,2176]{1,0:T(8,128)(2,1)S(1)}) custom-call(bf16[128,128]{1,0:T(8,128)(2,1)S(1)} %get-tuple-element.76.refs_0_, bf16[32,2176]{1,0:T(8,128)(2,1)S(1)} %get-tuple-element.77.refs_1_, bf16[32,2176]{1,0:T(8,128)(2,1)S(1)} %collective-permute-done.11.refs_2_, ...), custom_call_target="tpu_custom_call" | custom-call | flops 2013265920 | tf_op jit(solution)/shard_map/pallas_call | solution.py:48
  66.8 2.5 %shard_map.195 = (f32[64,3840]{1,0:T(8,128)S(1)}, bf16[64,3840]{1,0:T(8,128)(2,1)S(1)}) custom-call(bf16[128,2176]{1,0:T(8,128)(2,1)S(1)} %get-tuple-element.82.ordered, bf16[2048,3840]{1,0:T(8,128)(2,1)S(1)} %shard_map.191.refs_5_.w_gate, bf16[2048,3840]{1,0:T(8,128)(2,1)S(1)} %shard_map.192.refs_6_.w_up), custom_call_target="tpu_custom_call" | custom-call | flops 2013265920 | tf_op jit(solution)/shard_map/pallas_call | solution.py:48
  69.3 0.6 collective-permute-start.16
  70.0 1.6 %collective-permute-start.15 = (bf16[32,3968]{1,0:T(8,128)(2,1)S(1)}, bf16[32,3968]{1,0:T(8,128)(2,1)S(1)}, u32[]{:S(2)}, u32[]{:S(2)}) collective-permute-start(bf16[32,3968]{1,0:T(8,128)(2,1)S(1)} %get-tuple-element.81), channel_id=1, source_target_pairs={{0,8},{4,12},{8,0},{12,4},{1,9},{5,13},{9,1},{13,5},{2,10},{6,14},... | collective-permute-start | bytes 761864 | tf_op jit(solution)/shard_map/ppermute | solution.py:555
  71.7 1.3 %collective-permute-start.17 = (bf16[32,3840]{1,0:T(8,128)(2,1)S(1)}, bf16[32,3840]{1,0:T(8,128)(2,1)S(1)}, u32[]{:S(2)}, u32[]{:S(2)}) collective-permute-start(bf16[32,3840]{1,0:T(8,128)(2,1)S(1)} %get-tuple-element.85.refs_1_), channel_id=1, source_target_pairs={{0,8},{4,12},{8,0},{12,4},{1,9},{5,13},{9,1},{13,5},{2,10},{6,14},... | collective-permute-start | bytes 737288 | tf_op jit(solution)/shard_map/ppermute | solution.py:555
  73.0 5.5 %shard_map.197.refs_1_.refs_5_ = bf16[3840,2048]{1,0:T(8,128)(2,1)S(1)} custom-call(bf16[3840,2048]{1,0:T(8,128)(2,1)} %refs_0_.11, bf16[32,3840]{1,0:T(8,128)(2,1)S(1)} %get-tuple-element.85.refs_1_), custom_call_target="tpu_custom_call" | custom-call | bytes 31457280 | tf_op jit(solution)/shard_map/pallas_call | solution.py:76
  78.5 0.5 collective-permute-done.15.refs_0_
  79.2 1.6 %collective-permute-start.21 = (bf16[32,1920]{1,0:T(8,128)(2,1)S(1)}, bf16[32,1920]{1,0:T(8,128)(2,1)S(1)}, u32[]{:S(2)}, u32[]{:S(2)}) collective-permute-start(bf16[32,1920]{1,0:T(8,128)(2,1)S(1)} %get-tuple-element.88.refs_1_), channel_id=1, source_target_pairs={{0,8},{4,12},{8,0},{12,4},{1,9},{5,13},{9,1},{13,5},{2,10},{6,14},... | collective-permute-start | bytes 368648 | tf_op jit(solution)/shard_map/ppermute | solution.py:555
  80.8 3.5 %collective-permute-done.17.refs_0_ = bf16[32,3840]{1,0:T(8,128)(2,1)S(1)} collective-permute-done((bf16[32,3840]{1,0:T(8,128)(2,1)S(1)}, bf16[32,3840]{1,0:T(8,128)(2,1)S(1)}, u32[]{:S(2)}, u32[]{:S(2)}) %collective-permute-start.17) | collective-permute-done | bytes 245792 | tf_op jit(solution)/shard_map/ppermute | solution.py:555
  84.4 1.6 %collective-permute-start.18 = (bf16[32,1920]{1,0:T(8,128)(2,1)S(1)}, bf16[32,1920]{1,0:T(8,128)(2,1)S(1)}, u32[]{:S(2)}, u32[]{:S(2)}) collective-permute-start(bf16[32,1920]{1,0:T(8,128)(2,1)S(1)} %shard_map.199.refs_1_), channel_id=1, source_target_pairs={{0,8},{4,12},{8,0},{12,4},{1,9},{5,13},{9,1},{13,5},{2,10},{6,14},... | collective-permute-start | bytes 368648 | tf_op jit(solution)/shard_map/ppermute | solution.py:555
  86.0 0.5 collective-permute-done.21.refs_2_
  87.1 2.3 %collective-permute-done.18.refs_2_ = bf16[32,1920]{1,0:T(8,128)(2,1)S(1)} collective-permute-done((bf16[32,1920]{1,0:T(8,128)(2,1)S(1)}, bf16[32,1920]{1,0:T(8,128)(2,1)S(1)}, u32[]{:S(2)}, u32[]{:S(2)}) %collective-permute-start.18) | collective-permute-done | bytes 122912 | tf_op jit(solution)/shard_map/ppermute | solution.py:555
  89.4 1.4 %shard_map.200.refs_6_ = f32[128,2048]{1,0:T(8,128)S(1)} custom-call(bf16[128,128]{1,0:T(8,128)(2,1)S(1)} %get-tuple-element.75.refs_0_, bf16[32,1920]{1,0:T(8,128)(2,1)S(1)} %get-tuple-element.88.refs_1_, bf16[32,1920]{1,0:T(8,128)(2,1)S(1)} %collective-permute-done.21.refs_2_, bf16[32,1920]{1,0:T(8,128)(2,1)S(1)} %collective-permute-done.22.refs_3_, ...), custom_call_target="tpu_custom_call" | custom-call | flops 1006632960 | tf_op jit(solution)/shard_map/pallas_call | solution.py:48
  90.8 1.4 %shard_map.201 = (f32[32,2048]{1,0:T(8,128)S(1)}, bf16[32,2048]{1,0:T(8,128)(2,1)S(1)}, bf16[32,2048]{1,0:T(8,128)(2,1)S(1)}, bf16[32,2048]{1,0:T(8,128)(2,1)S(1)}) custom-call(bf16[128,128]{1,0:T(8,128)(2,1)S(1)} %get-tuple-element.75.refs_0_, bf16[32,1920]{1,0:T(8,128)(2,1)S(1)} %shard_map.199.refs_1_, ...), custom_call_target="tpu_custom_call" | custom-call | flops 1006632960 | tf_op jit(solution)/shard_map/pallas_call | solution.py:48
  92.2 3.5 %collective-permute-start.24 = (bf16[32,2048]{1,0:T(8,128)(2,1)S(1)}, bf16[32,2048]{1,0:T(8,128)(2,1)S(1)}, u32[]{:S(2)}, u32[]{:S(2)}) collective-permute-start(bf16[32,2048]{1,0:T(8,128)(2,1)S(1)} %get-tuple-element.90), channel_id=1, source_target_pairs={{0,1},{1,2},{2,3},{3,0},{4,5},{5,6},{6,7},{7,4},{8,9},{9,10},{10,1... | collective-permute-start | bytes 393224 | tf_op jit(solution)/shard_map/ppermute | solution.py:559
  95.7 2.0 %collective-permute-start.25 = (bf16[32,2048]{1,0:T(8,128)(2,1)S(1)}, bf16[32,2048]{1,0:T(8,128)(2,1)S(1)}, u32[]{:S(2)}, u32[]{:S(2)}) collective-permute-start(bf16[32,2048]{1,0:T(8,128)(2,1)S(1)} %get-tuple-element.91), channel_id=1, source_target_pairs={{0,2},{1,3},{2,0},{3,1},{4,6},{5,7},{6,4},{7,5},{8,10},{9,11},{10,... | collective-permute-start | bytes 393224 | tf_op jit(solution)/shard_map/ppermute | solution.py:559
  98.2 3.5 %collective-permute-done.24.refs_0_ = bf16[32,2048]{1,0:T(8,128)(2,1)S(1)} collective-permute-done((bf16[32,2048]{1,0:T(8,128)(2,1)S(1)}, bf16[32,2048]{1,0:T(8,128)(2,1)S(1)}, u32[]{:S(2)}, u32[]{:S(2)}) %collective-permute-start.24) | collective-permute-done | bytes 131104 | tf_op jit(solution)/shard_map/ppermute | solution.py:559
  101.6 5.4 %collective-permute-done.25.refs_1_ = bf16[32,2048]{1,0:T(8,128)(2,1)S(1)} collective-permute-done((bf16[32,2048]{1,0:T(8,128)(2,1)S(1)}, bf16[32,2048]{1,0:T(8,128)(2,1)S(1)}, u32[]{:S(2)}, u32[]{:S(2)}) %collective-permute-start.25) | collective-permute-done | bytes 131104 | tf_op jit(solution)/shard_map/ppermute | solution.py:559
  107.0 0.7 shard_map.202
  (72 shorter events, 3.2 us)
Async XLA Ops:
  1.2 3.3 %copy-start.4 = (f32[8,128]{1,0:T(8,128)}, f32[8,128]{1,0:T(8,128)S(1)}, u32[]{:S(2)}) copy-start(f32[8,128]{1,0:T(8,128)S(1)} %get-tuple-element.53.refs_3_) | copy-start | bytes 12292
  1.2 8.3 %collective-permute-start = (bf16[32,2176]{1,0:T(8,128)(2,1)S(1)}, bf16[32,2176]{1,0:T(8,128)(2,1)S(1)}, u32[]{:S(2)}, u32[]{:S(2)}) collective-permute-start(bf16[32,2176]{1,0:T(8,128)(2,1)S(1)} %get-tuple-element.50), channel_id=1, source_target_pairs={{0,8},{4,12},{8,0},{12,4},{1,9},{5,13},{9,1},{13,5},{2,10},{6,14},... | collective-permute-start | bytes 417800 | tf_op jit(solution)/shard_map/ppermute | solution.py:555
  4.2 5.3 %collective-permute-start.1 = (bf16[32,2176]{1,0:T(8,128)(2,1)S(1)}, bf16[32,2176]{1,0:T(8,128)(2,1)S(1)}, u32[]{:S(2)}, u32[]{:S(2)}) collective-permute-start(bf16[32,2176]{1,0:T(8,128)(2,1)S(1)} %get-tuple-element.51), channel_id=1, source_target_pairs={{0,4},{4,0},{8,12},{12,8},{1,5},{5,1},{9,13},{13,9},{2,6},{6,2},{1... | collective-permute-start | bytes 417800 | tf_op jit(solution)/shard_map/ppermute | solution.py:555
  4.2 6.0 %collective-permute-start.2 = (bf16[32,2176]{1,0:T(8,128)(2,1)S(1)}, bf16[32,2176]{1,0:T(8,128)(2,1)S(1)}, u32[]{:S(2)}, u32[]{:S(2)}) collective-permute-start(bf16[32,2176]{1,0:T(8,128)(2,1)S(1)} %get-tuple-element.52), channel_id=1, source_target_pairs={{0,12},{4,8},{8,4},{12,0},{1,13},{5,9},{9,5},{13,1},{2,14},{6,10},... | collective-permute-start | bytes 417800 | tf_op jit(solution)/shard_map/ppermute | solution.py:555
  4.5 8.8 %copy-start.6 = (s32[4]{0:T(128)S(1)}, s32[4]{0:T(128)}, u32[]{:S(2)}) copy-start(s32[4]{0:T(128)} %path_pages.1) | copy-start | bytes 52
  8.5 8.5 %copy-start.7 = (bf16[2048]{0:T(1024)(128)(2,1)S(1)}, bf16[2048]{0:T(1024)(128)(2,1)}, u32[]{:S(2)}) copy-start(bf16[2048]{0:T(1024)(128)(2,1)} %param.22) | copy-start | bytes 12292
  8.5 8.5 %copy-start.8 = (bf16[256]{0:T(256)(128)(2,1)S(1)}, bf16[256]{0:T(256)(128)(2,1)}, u32[]{:S(2)}) copy-start(bf16[256]{0:T(256)(128)(2,1)} %param.24) | copy-start | bytes 1540
  8.6 8.5 %copy-start.9 = (bf16[256]{0:T(256)(128)(2,1)S(1)}, bf16[256]{0:T(256)(128)(2,1)}, u32[]{:S(2)}) copy-start(bf16[256]{0:T(256)(128)(2,1)} %param.26) | copy-start | bytes 1540
  8.6 8.6 %copy-start.1 = (bf16[64,128,256]{2,1,0:T(8,128)(2,1)S(1)}, bf16[64,128,256]{2,1,0:T(8,128)(2,1)}, u32[]{:S(2)}) copy-start(bf16[64,128,256]{2,1,0:T(8,128)(2,1)} %refs_0_.7) | copy-start | bytes 12582916
  8.6 8.6 %copy-start.2 = (bf16[64,128,256]{2,1,0:T(8,128)(2,1)S(1)}, bf16[64,128,256]{2,1,0:T(8,128)(2,1)}, u32[]{:S(2)}) copy-start(bf16[64,128,256]{2,1,0:T(8,128)(2,1)} %refs_1_.3) | copy-start | bytes 12582916
  10.2 7.6 %copy-start.5 = (s32[4,32]{1,0:T(4,128)S(1)}, s32[4,32]{1,0:T(4,128)}, u32[]{:S(2)}) copy-start(s32[4,32]{1,0:T(4,128)} %page_table.1) | copy-start | bytes 1540
  10.2 11.6 %copy-start.3 = (f32[128,128]{1,0:T(8,128)S(1)}, f32[128,128]{1,0:T(8,128)}, u32[]{:S(2)}) copy-start(f32[128,128]{1,0:T(8,128)} %constant.24.clone.refs_6_) | copy-start | bytes 196612
  12.8 2.3 %collective-permute-start.3 = (f32[64,2688]{1,0:T(8,128)S(1)}, f32[64,2688]{1,0:T(8,128)S(1)}, u32[]{:S(2)}, u32[]{:S(2)}) collective-permute-start(f32[64,2688]{1,0:T(8,128)S(1)} %get-tuple-element.60), channel_id=1, source_target_pairs={{0,4},{4,0},{8,12},{12,8},{1,5},{5,1},{9,13},{13,9},{2,6},{6,2},{1... | collective-permute-start | bytes 2064392 | tf_op jit(solution)/shard_map/ppermute | solution.py:555
  15.0 19.1 %slice-start.4 = ((s8[8388608]{0:T(1024)(128)(4,1)}), s8[4194304]{0:T(1024)(128)(4,1)S(1)}, s32[]{:S(2)}) async-start(s8[8388608]{0:T(1024)(128)(4,1)} %bitcast.7), calls=%async_computation.4 | async-start | bytes 8388608
  15.1 6.7 %collective-permute-start.4 = (bf16[32,2688]{1,0:T(8,128)(2,1)S(1)}, bf16[32,2688]{1,0:T(8,128)(2,1)S(1)}, u32[]{:S(2)}, u32[]{:S(2)}) collective-permute-start(bf16[32,2688]{1,0:T(8,128)(2,1)S(1)} %get-tuple-element.61._.refs_2_), channel_id=1, source_target_pairs={{0,8},{4,12},{8,0},{12,4},{1,9},{5,13},{9,1},{13,5},{2,10},{6,14},... | collective-permute-start | bytes 516104 | tf_op jit(solution)/shard_map/ppermute | solution.py:555
  17.2 17.0 %slice-start.5 = ((s8[8388608]{0:T(1024)(128)(4,1)}), s8[4194304]{0:T(1024)(128)(4,1)S(1)}, s32[]{:S(2)}) async-start(s8[8388608]{0:T(1024)(128)(4,1)} %bitcast.7), calls=%async_computation.5 | async-start | bytes 8388608
  21.8 34.5 %slice-start = ((s8[15728640]{0:T(1024)(128)(4,1)}), s8[3145728]{0:T(1024)(128)(4,1)S(1)}, s32[]{:S(2)}) async-start(s8[15728640]{0:T(1024)(128)(4,1)} %bitcast.5), calls=%async_computation | async-start | bytes 6291456
  21.8 34.5 %slice-start.1 = ((s8[15728640]{0:T(1024)(128)(4,1)}), s8[4194304]{0:T(1024)(128)(4,1)S(1)}, s32[]{:S(2)}) async-start(s8[15728640]{0:T(1024)(128)(4,1)} %bitcast.5), calls=%async_computation.1 | async-start | bytes 8388608
  29.1 27.2 %slice-start.2 = ((s8[15728640]{0:T(1024)(128)(4,1)}), s8[4194304]{0:T(1024)(128)(4,1)S(1)}, s32[]{:S(2)}) async-start(s8[15728640]{0:T(1024)(128)(4,1)} %bitcast.5), calls=%async_computation.2 | async-start | bytes 8388608
  29.1 5.0 %collective-permute-start.5 = (bf16[32,2048]{1,0:T(8,128)(2,1)S(1)}, bf16[32,2048]{1,0:T(8,128)(2,1)S(1)}, u32[]{:S(2)}, u32[]{:S(2)}) collective-permute-start(bf16[32,2048]{1,0:T(8,128)(2,1)S(1)} %shard_map.187.refs_1_.refs_0_), channel_id=1, source_target_pairs={{0,8},{4,12},{8,0},{12,4},{1,9},{5,13},{9,1},{13,5},{2,10},{6,14},... | collective-permute-start | bytes 393224 | tf_op jit(solution)/shard_map/ppermute | solution.py:555
  30.9 3.8 %collective-permute-start.6 = (bf16[32,2048]{1,0:T(8,128)(2,1)S(1)}, bf16[32,2048]{1,0:T(8,128)(2,1)S(1)}, u32[]{:S(2)}, u32[]{:S(2)}) collective-permute-start(bf16[32,2048]{1,0:T(8,128)(2,1)S(1)} %shard_map.187.refs_1_.refs_0_), channel_id=1, source_target_pairs={{0,4},{4,0},{8,12},{12,8},{1,5},{5,1},{9,13},{13,9},{2,6},{6,2},{1... | collective-permute-start | bytes 393224 | tf_op jit(solution)/shard_map/ppermute | solution.py:555
  34.1 1.3 %collective-permute-start.7 = (bf16[32,2048]{1,0:T(8,128)(2,1)S(1)}, bf16[32,2048]{1,0:T(8,128)(2,1)S(1)}, u32[]{:S(2)}, u32[]{:S(2)}) collective-permute-start(bf16[32,2048]{1,0:T(8,128)(2,1)S(1)} %collective-permute-done.5.refs_1_), channel_id=1, source_target_pairs={{0,4},{4,0},{8,12},{12,8},{1,5},{5,1},{9,13},{13,9},{2,6},{6,2},{1... | collective-permute-start | bytes 393224 | tf_op jit(solution)/shard_map/ppermute | solution.py:555
  35.5 20.8 %slice-start.3 = ((s8[15728640]{0:T(1024)(128)(4,1)}), s8[4194304]{0:T(1024)(128)(4,1)S(1)}, s32[]{:S(2)}) async-start(s8[15728640]{0:T(1024)(128)(4,1)} %bitcast.5), calls=%async_computation.3 | async-start | bytes 8388608
  36.9 8.3 %collective-permute-start.8 = (bf16[32,2048]{1,0:T(8,128)(2,1)S(1)}, bf16[32,2048]{1,0:T(8,128)(2,1)S(1)}, u32[]{:S(2)}, u32[]{:S(2)}) collective-permute-start(bf16[32,2048]{1,0:T(8,128)(2,1)S(1)} %get-tuple-element.71), channel_id=1, source_target_pairs={{0,1},{1,2},{2,3},{3,0},{4,5},{5,6},{6,7},{7,4},{8,9},{9,10},{10,1... | collective-permute-start | bytes 393224 | tf_op jit(solution)/shard_map/ppermute | solution.py:559
  38.8 11.6 %collective-permute-start.9 = (bf16[32,2048]{1,0:T(8,128)(2,1)S(1)}, bf16[32,2048]{1,0:T(8,128)(2,1)S(1)}, u32[]{:S(2)}, u32[]{:S(2)}) collective-permute-start(bf16[32,2048]{1,0:T(8,128)(2,1)S(1)} %get-tuple-element.72), channel_id=1, source_target_pairs={{0,2},{1,3},{2,0},{3,1},{4,6},{5,7},{6,4},{7,5},{8,10},{9,11},{10,... | collective-permute-start | bytes 393224 | tf_op jit(solution)/shard_map/ppermute | solution.py:559
  41.4 9.0 %collective-permute-start.10 = (bf16[32,2048]{1,0:T(8,128)(2,1)S(1)}, bf16[32,2048]{1,0:T(8,128)(2,1)S(1)}, u32[]{:S(2)}, u32[]{:S(2)}) collective-permute-start(bf16[32,2048]{1,0:T(8,128)(2,1)S(1)} %get-tuple-element.73), channel_id=1, source_target_pairs={{0,3},{1,0},{2,1},{3,2},{4,7},{5,4},{6,5},{7,6},{8,11},{9,8},{10,9... | collective-permute-start | bytes 393224 | tf_op jit(solution)/shard_map/ppermute | solution.py:559
  50.5 13.4 %collective-permute-start.11 = (bf16[32,2176]{1,0:T(8,128)(2,1)S(1)}, bf16[32,2176]{1,0:T(8,128)(2,1)S(1)}, u32[]{:S(2)}, u32[]{:S(2)}) collective-permute-start(bf16[32,2176]{1,0:T(8,128)(2,1)S(1)} %get-tuple-element.77.refs_1_), channel_id=1, source_target_pairs={{0,1},{1,2},{2,3},{3,0},{4,5},{5,6},{6,7},{7,4},{8,9},{9,10},{10,1... | collective-permute-start | bytes 417800 | tf_op jit(solution)/shard_map/ppermute | solution.py:559
  53.9 10.3 %collective-permute-start.12 = (bf16[32,2176]{1,0:T(8,128)(2,1)S(1)}, bf16[32,2176]{1,0:T(8,128)(2,1)S(1)}, u32[]{:S(2)}, u32[]{:S(2)}) collective-permute-start(bf16[32,2176]{1,0:T(8,128)(2,1)S(1)} %get-tuple-element.77.refs_1_), channel_id=1, source_target_pairs={{0,2},{1,3},{2,0},{3,1},{4,6},{5,7},{6,4},{7,5},{8,10},{9,11},{10,... | collective-permute-start | bytes 417800 | tf_op jit(solution)/shard_map/ppermute | solution.py:559
  55.5 8.7 %collective-permute-start.13 = (bf16[32,2176]{1,0:T(8,128)(2,1)S(1)}, bf16[32,2176]{1,0:T(8,128)(2,1)S(1)}, u32[]{:S(2)}, u32[]{:S(2)}) collective-permute-start(bf16[32,2176]{1,0:T(8,128)(2,1)S(1)} %get-tuple-element.77.refs_1_), channel_id=1, source_target_pairs={{0,3},{1,0},{2,1},{3,2},{4,7},{5,4},{6,5},{7,6},{8,11},{9,8},{10,9... | collective-permute-start | bytes 417800 | tf_op jit(solution)/shard_map/ppermute | solution.py:559
  57.4 5.5 %copy-start = (bf16[2048,3840]{1,0:T(8,128)(2,1)S(1)}, bf16[2048,3840]{1,0:T(8,128)(2,1)}, u32[]{:S(2)}) copy-start(bf16[2048,3840]{1,0:T(8,128)(2,1)} %refs_0_.10) | copy-start | bytes 47185924
  66.7 3.1 %collective-permute-start.14 = (bf16[64,3968]{1,0:T(8,128)(2,1)S(1)}, bf16[64,3968]{1,0:T(8,128)(2,1)S(1)}, u32[]{:S(2)}, u32[]{:S(2)}) collective-permute-start(bf16[64,3968]{1,0:T(8,128)(2,1)S(1)} %get-tuple-element.79), channel_id=1, source_target_pairs={{0,4},{4,0},{8,12},{12,8},{1,5},{5,1},{9,13},{13,9},{2,6},{6,2},{1... | collective-permute-start | bytes 1523720 | tf_op jit(solution)/shard_map/ppermute | solution.py:555
  69.3 2.3 %collective-permute-start.16 = (bf16[64,3840]{1,0:T(8,128)(2,1)S(1)}, bf16[64,3840]{1,0:T(8,128)(2,1)S(1)}, u32[]{:S(2)}, u32[]{:S(2)}) collective-permute-start(bf16[64,3840]{1,0:T(8,128)(2,1)S(1)} %get-tuple-element.84), channel_id=1, source_target_pairs={{0,4},{4,0},{8,12},{12,8},{1,5},{5,1},{9,13},{13,9},{2,6},{6,2},{1... | collective-permute-start | bytes 1474568 | tf_op jit(solution)/shard_map/ppermute | solution.py:555
  70.0 9.1 %collective-permute-start.15 = (bf16[32,3968]{1,0:T(8,128)(2,1)S(1)}, bf16[32,3968]{1,0:T(8,128)(2,1)S(1)}, u32[]{:S(2)}, u32[]{:S(2)}) collective-permute-start(bf16[32,3968]{1,0:T(8,128)(2,1)S(1)} %get-tuple-element.81), channel_id=1, source_target_pairs={{0,8},{4,12},{8,0},{12,4},{1,9},{5,13},{9,1},{13,5},{2,10},{6,14},... | collective-permute-start | bytes 761864 | tf_op jit(solution)/shard_map/ppermute | solution.py:555
  71.7 12.6 %collective-permute-start.17 = (bf16[32,3840]{1,0:T(8,128)(2,1)S(1)}, bf16[32,3840]{1,0:T(8,128)(2,1)S(1)}, u32[]{:S(2)}, u32[]{:S(2)}) collective-permute-start(bf16[32,3840]{1,0:T(8,128)(2,1)S(1)} %get-tuple-element.85.refs_1_), channel_id=1, source_target_pairs={{0,8},{4,12},{8,0},{12,4},{1,9},{5,13},{9,1},{13,5},{2,10},{6,14},... | collective-permute-start | bytes 737288 | tf_op jit(solution)/shard_map/ppermute | solution.py:555
  79.2 7.3 %collective-permute-start.21 = (bf16[32,1920]{1,0:T(8,128)(2,1)S(1)}, bf16[32,1920]{1,0:T(8,128)(2,1)S(1)}, u32[]{:S(2)}, u32[]{:S(2)}) collective-permute-start(bf16[32,1920]{1,0:T(8,128)(2,1)S(1)} %get-tuple-element.88.refs_1_), channel_id=1, source_target_pairs={{0,8},{4,12},{8,0},{12,4},{1,9},{5,13},{9,1},{13,5},{2,10},{6,14},... | collective-permute-start | bytes 368648 | tf_op jit(solution)/shard_map/ppermute | solution.py:555
  84.4 4.9 %collective-permute-start.18 = (bf16[32,1920]{1,0:T(8,128)(2,1)S(1)}, bf16[32,1920]{1,0:T(8,128)(2,1)S(1)}, u32[]{:S(2)}, u32[]{:S(2)}) collective-permute-start(bf16[32,1920]{1,0:T(8,128)(2,1)S(1)} %shard_map.199.refs_1_), channel_id=1, source_target_pairs={{0,8},{4,12},{8,0},{12,4},{1,9},{5,13},{9,1},{13,5},{2,10},{6,14},... | collective-permute-start | bytes 368648 | tf_op jit(solution)/shard_map/ppermute | solution.py:555
  86.0 3.4 %collective-permute-start.22 = (bf16[32,1920]{1,0:T(8,128)(2,1)S(1)}, bf16[32,1920]{1,0:T(8,128)(2,1)S(1)}, u32[]{:S(2)}, u32[]{:S(2)}) collective-permute-start(bf16[32,1920]{1,0:T(8,128)(2,1)S(1)} %get-tuple-element.88.refs_1_), channel_id=1, source_target_pairs={{0,4},{4,0},{8,12},{12,8},{1,5},{5,1},{9,13},{13,9},{2,6},{6,2},{1... | collective-permute-start | bytes 368648 | tf_op jit(solution)/shard_map/ppermute | solution.py:555
  86.6 2.8 %collective-permute-start.23 = (bf16[32,1920]{1,0:T(8,128)(2,1)S(1)}, bf16[32,1920]{1,0:T(8,128)(2,1)S(1)}, u32[]{:S(2)}, u32[]{:S(2)}) collective-permute-start(bf16[32,1920]{1,0:T(8,128)(2,1)S(1)} %collective-permute-done.21.refs_2_), channel_id=1, source_target_pairs={{0,4},{4,0},{8,12},{12,8},{1,5},{5,1},{9,13},{13,9},{2,6},{6,2},{1... | collective-permute-start | bytes 368648 | tf_op jit(solution)/shard_map/ppermute | solution.py:555
  86.6 4.2 %collective-permute-start.19 = (bf16[32,1920]{1,0:T(8,128)(2,1)S(1)}, bf16[32,1920]{1,0:T(8,128)(2,1)S(1)}, u32[]{:S(2)}, u32[]{:S(2)}) collective-permute-start(bf16[32,1920]{1,0:T(8,128)(2,1)S(1)} %shard_map.199.refs_1_), channel_id=1, source_target_pairs={{0,4},{4,0},{8,12},{12,8},{1,5},{5,1},{9,13},{13,9},{2,6},{6,2},{1... | collective-permute-start | bytes 368648 | tf_op jit(solution)/shard_map/ppermute | solution.py:555
  89.4 1.4 %collective-permute-start.20 = (bf16[32,1920]{1,0:T(8,128)(2,1)S(1)}, bf16[32,1920]{1,0:T(8,128)(2,1)S(1)}, u32[]{:S(2)}, u32[]{:S(2)}) collective-permute-start(bf16[32,1920]{1,0:T(8,128)(2,1)S(1)} %collective-permute-done.18.refs_2_), channel_id=1, source_target_pairs={{0,4},{4,0},{8,12},{12,8},{1,5},{5,1},{9,13},{13,9},{2,6},{6,2},{1... | collective-permute-start | bytes 368648 | tf_op jit(solution)/shard_map/ppermute | solution.py:555
  92.2 9.4 %collective-permute-start.24 = (bf16[32,2048]{1,0:T(8,128)(2,1)S(1)}, bf16[32,2048]{1,0:T(8,128)(2,1)S(1)}, u32[]{:S(2)}, u32[]{:S(2)}) collective-permute-start(bf16[32,2048]{1,0:T(8,128)(2,1)S(1)} %get-tuple-element.90), channel_id=1, source_target_pairs={{0,1},{1,2},{2,3},{3,0},{4,5},{5,6},{6,7},{7,4},{8,9},{9,10},{10,1... | collective-permute-start | bytes 393224 | tf_op jit(solution)/shard_map/ppermute | solution.py:559
  95.7 11.3 %collective-permute-start.25 = (bf16[32,2048]{1,0:T(8,128)(2,1)S(1)}, bf16[32,2048]{1,0:T(8,128)(2,1)S(1)}, u32[]{:S(2)}, u32[]{:S(2)}) collective-permute-start(bf16[32,2048]{1,0:T(8,128)(2,1)S(1)} %get-tuple-element.91), channel_id=1, source_target_pairs={{0,2},{1,3},{2,0},{3,1},{4,6},{5,7},{6,4},{7,5},{8,10},{9,11},{10,... | collective-permute-start | bytes 393224 | tf_op jit(solution)/shard_map/ppermute | solution.py:559
  97.7 9.3 %collective-permute-start.26 = (bf16[32,2048]{1,0:T(8,128)(2,1)S(1)}, bf16[32,2048]{1,0:T(8,128)(2,1)S(1)}, u32[]{:S(2)}, u32[]{:S(2)}) collective-permute-start(bf16[32,2048]{1,0:T(8,128)(2,1)S(1)} %get-tuple-element.92), channel_id=1, source_target_pairs={{0,3},{1,0},{2,1},{3,2},{4,7},{5,4},{6,5},{7,6},{8,11},{9,8},{10,9... | collective-permute-start | bytes 393224 | tf_op jit(solution)/shard_map/ppermute | solution.py:559
